TPU v7x, 32 devices: a whole 2x2x4 slice. The times are simulated.
32 devices in a mesh: wide: 8 (over z, x), narrow: 4 (over y, core).
Axes of the slice: x: 2, y: 2, z: 4, core: 2. Of those that a mesh axis runs over, the one named last changes fastest.
Arguments:
- frames: bfloat16 [32768, 1024], P(('wide', 'narrow')), may hold values from -6 to 6
- skip: bfloat16 [32768, 1024], P(('wide', 'narrow')), may hold values from -6 to 6
- lengths: int32 [32, 8], P(('wide', 'narrow')), may hold values from 0 to 1024, as said below
- key_mask: int32 [32768], P(('wide', 'narrow')), may hold values 0 or 1
- cotangent: bfloat16 [32768, 1024], P(('wide', 'narrow')), may hold values from -6 to 6
- w_skip: bfloat16 [2048, 1024], P(('wide', 'narrow')), may hold values from -0.125 to 0.125
- b_skip: bfloat16 [1024], P(('wide', 'narrow')), may hold values from -2 to 2
- pre_attn_gain: bfloat16 [1024], P(('wide', 'narrow')), may hold values from 0.5 to 1.5
- pre_attn_bias: bfloat16 [1024], P(('wide', 'narrow')), may hold values from -1.5 to 1.5
- w_qkv: bfloat16 [1024, 3072], P(('wide', 'narrow')), may hold values from -0.1875 to 0.1875
- b_query: bfloat16 [1024], P(('wide', 'narrow')), may hold values from -2 to 2
- b_value: bfloat16 [1024], P(('wide', 'narrow')), may hold values from -2 to 2
- w_out: bfloat16 [1024, 1024], P(('wide', 'narrow')), may hold values from -0.75 to 0.75
- b_out: bfloat16 [1024], P(('wide', 'narrow')), may hold values from -2 to 2
- pre_ffn_gain: bfloat16 [1024], P(('wide', 'narrow')), may hold values from 0.5 to 1.5
- pre_ffn_bias: bfloat16 [1024], P(('wide', 'narrow')), may hold values from -1.5 to 1.5
- w_up: bfloat16 [1024, 4096], P(('wide', 'narrow')), may hold values from -0.1875 to 0.1875
- b_up: bfloat16 [4096], P(('wide', 'narrow')), may hold values from -2 to 2
- w_down: bfloat16 [4096, 1024], P(('wide', 'narrow')), may hold values from -0.09375 to 0.09375
- b_down: bfloat16 [1024], P(('wide', 'narrow')), may hold values from -2 to 2
Outputs:
- layer_out: bfloat16 [32768, 1024], P(('wide', 'narrow'))
- grad_frames: bfloat16 [32768, 1024], P(('wide', 'narrow'))
- grad_skip: bfloat16 [32768, 1024], P(('wide', 'narrow'))
- grad_w_skip: float32 [2048, 1024], P(('wide', 'narrow'))
- grad_b_skip: float32 [1024], P(('wide', 'narrow'))
- grad_pre_attn_gain: float32 [1024], P(('wide', 'narrow'))
- grad_pre_attn_bias: float32 [1024], P(('wide', 'narrow'))
- grad_w_qkv: float32 [1024, 3072], P(('wide', 'narrow'))
- grad_b_query: float32 [1024], P(('wide', 'narrow'))
- grad_b_value: float32 [1024], P(('wide', 'narrow'))
- grad_w_out: float32 [1024, 1024], P(('wide', 'narrow'))
- grad_b_out: float32 [1024], P(('wide', 'narrow'))
- grad_pre_ffn_gain: float32 [1024], P(('wide', 'narrow'))
- grad_pre_ffn_bias: float32 [1024], P(('wide', 'narrow'))
- grad_w_up: float32 [1024, 4096], P(('wide', 'narrow'))
- grad_b_up: float32 [4096], P(('wide', 'narrow'))
- grad_w_down: float32 [4096, 1024], P(('wide', 'narrow'))
- grad_b_down: float32 [1024], P(('wide', 'narrow'))
Inputs may be any that keep to these rules, and one draw needn't show every extreme that they name: `lengths`: each row sums to at most 1024; zeros stand only after the last utterance of a row; every row holds at least one utterance, and in every draw some row holds one utterance of exactly 1024 frames.
All inputs are finite; a program needn't handle non-finite values. No bound on the sum of `key_mask` on one device may be relied on, other than what follows from the above.
Results may differ from a plain program's by a relative error of at most 0.014.
Values may be sent and summed in bfloat16 or wider, within the bound.
No kernel may reach another device: no remote copies, remote signals or barrier semaphores. Data moves between devices by JAX's collectives and lax.ppermute only.
A program may use at most 320 MiB of HBM per device.

v0:
```python
import jax
import jax.numpy as jnp
from jax import lax
from jax.sharding import PartitionSpec as P

HEADS = 16


EPSILON = 1e-05
MASKED = -1e30


def norm_apply(hidden, gain_vec, shift_vec):
    center = hidden - jnp.mean(hidden, axis=1, keepdims=True)
    spread = jnp.mean(center * center, axis=1, keepdims=True)
    return center * lax.rsqrt(spread + EPSILON) * gain_vec + shift_vec


def gelu_tanh(v):
    return 0.5 * v * (1.0 + jnp.tanh(0.7978845608 * (v + 0.044715 * v * v * v)))


def outer_product(left_op, right_op):
    return lax.dot_general(
        left_op, right_op, (((0,), (0,)), ((), ())), preferred_element_type=jnp.float32
    )


def back_product(grad_in, weight):
    return lax.dot_general(
        grad_in, weight, (((1,), (1,)), ((), ())), preferred_element_type=jnp.float32
    )


def column_sums(grad_in):
    return jnp.sum(grad_in.astype(jnp.float32), axis=0)


def segment_layout(length_row, mask_row, tok_rows):
    utter_ends = jnp.cumsum(length_row)
    slot_ids = jnp.arange(tok_rows, dtype=jnp.int32)
    segment = jnp.sum((slot_ids[:, None] >= utter_ends[None, :]).astype(jnp.int32), axis=1)
    in_use = slot_ids < utter_ends[-1]
    key_live = in_use & (mask_row == 1)
    return (segment, in_use, key_live)


def block_scores(query_block, keys_all, offset, segment, in_use, key_live, slopes, scale):
    block_rows = query_block.shape[0]
    row_ids = offset + jnp.arange(block_rows, dtype=jnp.int32)
    col_ids = jnp.arange(keys_all.shape[0], dtype=jnp.int32)
    raw = (
        jnp.einsum("qhd,khd->hqk", query_block, keys_all, preferred_element_type=jnp.float32)
        * scale
    )
    distance = jnp.abs(row_ids[:, None] - col_ids[None, :]).astype(jnp.float32)
    scores = raw - slopes[:, None, None] * distance[None]
    row_segment = lax.dynamic_slice_in_dim(segment, offset, block_rows)
    row_use = lax.dynamic_slice_in_dim(in_use, offset, block_rows)
    allowed = (row_segment[:, None] == segment[None, :]) & row_use[:, None] & key_live[None, :] | (
        row_ids[:, None] == col_ids[None, :]
    )
    return jnp.where(allowed[None], scores, MASKED)


def fetch_weights(p):
    return (
        lax.all_gather(p[0], ("wide", "narrow"), axis=0, tiled=True),
        lax.all_gather(p[1], ("wide", "narrow"), axis=0, tiled=True),
        lax.all_gather(p[2], ("wide", "narrow"), axis=0, tiled=True),
        lax.all_gather(p[3], ("wide", "narrow"), axis=0, tiled=True),
        lax.all_gather(p[4], ("wide", "narrow"), axis=0, tiled=True),
        lax.all_gather(p[5], ("wide", "narrow"), axis=0, tiled=True),
        lax.all_gather(p[6], ("wide", "narrow"), axis=0, tiled=True),
        lax.all_gather(p[7], ("wide", "narrow"), axis=0, tiled=True),
        lax.all_gather(p[8], ("wide", "narrow"), axis=0, tiled=True),
        lax.all_gather(p[9], ("wide", "narrow"), axis=0, tiled=True),
        lax.all_gather(p[10], ("wide", "narrow"), axis=0, tiled=True),
        lax.all_gather(p[11], ("wide", "narrow"), axis=0, tiled=True),
        lax.all_gather(p[12], ("wide", "narrow"), axis=0, tiled=True),
        lax.all_gather(p[13], ("wide", "narrow"), axis=0, tiled=True),
        lax.all_gather(p[14], ("wide", "narrow"), axis=0, tiled=True),
    )


def reduce_grads(g):
    return (
        lax.psum_scatter(g[0], ("wide", "narrow"), scatter_dimension=0, tiled=True),
        lax.psum_scatter(g[1], ("wide", "narrow"), scatter_dimension=0, tiled=True),
        lax.psum_scatter(g[2], ("wide", "narrow"), scatter_dimension=0, tiled=True),
        lax.psum_scatter(g[3], ("wide", "narrow"), scatter_dimension=0, tiled=True),
        lax.psum_scatter(g[4], ("wide", "narrow"), scatter_dimension=0, tiled=True),
        lax.psum_scatter(g[5], ("wide", "narrow"), scatter_dimension=0, tiled=True),
        lax.psum_scatter(g[6], ("wide", "narrow"), scatter_dimension=0, tiled=True),
        lax.psum_scatter(g[7], ("wide", "narrow"), scatter_dimension=0, tiled=True),
        lax.psum_scatter(g[8], ("wide", "narrow"), scatter_dimension=0, tiled=True),
        lax.psum_scatter(g[9], ("wide", "narrow"), scatter_dimension=0, tiled=True),
        lax.psum_scatter(g[10], ("wide", "narrow"), scatter_dimension=0, tiled=True),
        lax.psum_scatter(g[11], ("wide", "narrow"), scatter_dimension=0, tiled=True),
        lax.psum_scatter(g[12], ("wide", "narrow"), scatter_dimension=0, tiled=True),
        lax.psum_scatter(g[13], ("wide", "narrow"), scatter_dimension=0, tiled=True),
        lax.psum_scatter(g[14], ("wide", "narrow"), scatter_dimension=0, tiled=True),
    )


def body(
    frames,
    skip,
    lengths,
    key_mask,
    cotangent,
    w_skip,
    b_skip,
    pre_attn_gain,
    pre_attn_bias,
    w_qkv,
    b_query,
    b_value,
    w_out,
    b_out,
    pre_ffn_gain,
    pre_ffn_bias,
    w_up,
    b_up,
    w_down,
    b_down,
):
    params = (
        w_skip,
        b_skip,
        pre_attn_gain,
        pre_attn_bias,
        w_qkv,
        b_query,
        b_value,
        w_out,
        b_out,
        pre_ffn_gain,
        pre_ffn_bias,
        w_up,
        b_up,
        w_down,
        b_down,
    )
    tok_rows = frames.shape[0]
    width = frames.shape[1]
    heads = HEADS
    head_size = width // heads
    scale = head_size ** (-0.5)
    block_rows = min(512, tok_rows)
    block_count = tok_rows // block_rows
    segment, in_use, key_live = segment_layout(lengths[0], key_mask, tok_rows)
    slopes = jnp.exp2(-8.0 * (jnp.arange(heads, dtype=jnp.float32) + 1.0) / heads)
    offsets = jnp.arange(block_count, dtype=jnp.int32) * block_rows
    (
        skip_mat,
        skip_vec,
        gain_one,
        shift_one,
        qkv_mat,
        query_vec,
        value_vec,
        out_mat,
        out_vec,
        gain_two,
        shift_two,
        up_mat,
        up_vec,
        down_mat,
        down_vec,
    ) = fetch_weights(params)
    gain_one = gain_one.astype(jnp.float32)
    shift_one = shift_one.astype(jnp.float32)
    gain_two = gain_two.astype(jnp.float32)
    shift_two = shift_two.astype(jnp.float32)
    joined = jnp.concatenate([frames, skip], axis=1)
    first_proj = jnp.dot(joined, skip_mat, preferred_element_type=jnp.float32) + skip_vec.astype(
        jnp.float32
    )
    normed_low = norm_apply(first_proj, gain_one, shift_one).astype(jnp.bfloat16)
    qkv_bias = jnp.concatenate([query_vec, jnp.zeros_like(query_vec), value_vec]).astype(
        jnp.float32
    )
    qkv_low = (jnp.dot(normed_low, qkv_mat, preferred_element_type=jnp.float32) + qkv_bias).astype(
        jnp.bfloat16
    )
    queries = qkv_low[:, :width].reshape(tok_rows, heads, head_size)
    keys_all = qkv_low[:, width : 2 * width].reshape(tok_rows, heads, head_size)
    values = qkv_low[:, 2 * width :].reshape(tok_rows, heads, head_size)
    query_blocks = queries.reshape(block_count, block_rows, heads, head_size)

    def attend(inputs):
        query_block, offset = inputs
        scores = block_scores(
            query_block, keys_all, offset, segment, in_use, key_live, slopes, scale
        )
        top_val = jnp.max(scores, axis=2, keepdims=True)
        expo = jnp.exp(scores - top_val)
        denom = jnp.sum(expo, axis=2, keepdims=True)
        probs_low = (expo / denom).astype(jnp.bfloat16)
        out_block = jnp.einsum(
            "hqk,khd->qhd", probs_low, values, preferred_element_type=jnp.float32
        )
        return (out_block, top_val[:, :, 0] + jnp.log(denom[:, :, 0]))

    attn_blocks, log_norm = lax.map(attend, (query_blocks, offsets))
    mixed_low = attn_blocks.reshape(tok_rows, width).astype(jnp.bfloat16)
    second = (
        first_proj
        + jnp.dot(mixed_low, out_mat, preferred_element_type=jnp.float32)
        + out_vec.astype(jnp.float32)
    )
    normed_two_low = norm_apply(second, gain_two, shift_two).astype(jnp.bfloat16)
    hidden = jnp.dot(normed_two_low, up_mat, preferred_element_type=jnp.float32) + up_vec.astype(
        jnp.float32
    )
    activated_low = gelu_tanh(hidden).astype(jnp.bfloat16)
    result = (
        second
        + jnp.dot(activated_low, down_mat, preferred_element_type=jnp.float32)
        + down_vec.astype(jnp.float32)
    )
    layer_out = result.astype(jnp.bfloat16)
    (
        skip_mat,
        skip_vec,
        gain_back,
        shift_back,
        qkv_mat,
        query_vec,
        value_vec,
        out_mat,
        out_vec,
        gain_back_two,
        shift_back_two,
        up_mat,
        up_vec,
        down_mat,
        down_vec,
    ) = fetch_weights(params)
    gain_back = gain_back.astype(jnp.float32)
    shift_back = shift_back.astype(jnp.float32)
    gain_back_two = gain_back_two.astype(jnp.float32)
    shift_back_two = shift_back_two.astype(jnp.float32)
    grad_w_down = outer_product(activated_low, cotangent)
    grad_b_down = column_sums(cotangent)
    grad_act = back_product(cotangent, down_mat)
    gelu_pull = jax.vjp(gelu_tanh, hidden)[1]
    grad_hidden_low = gelu_pull(grad_act)[0].astype(jnp.bfloat16)
    grad_w_up = outer_product(normed_two_low, grad_hidden_low)
    grad_b_up = column_sums(grad_hidden_low)
    grad_normed_two = back_product(grad_hidden_low, up_mat)
    norm_pull_two = jax.vjp(norm_apply, second, gain_back_two, shift_back_two)[1]
    grad_second, grad_gain_two, grad_shift_two = norm_pull_two(grad_normed_two)
    grad_second = grad_second + cotangent.astype(jnp.float32)
    grad_attn_low = grad_second.astype(jnp.bfloat16)
    grad_w_out = outer_product(mixed_low, grad_attn_low)
    grad_b_out = column_sums(grad_attn_low)
    grad_mixed_low = back_product(grad_attn_low, out_mat).astype(jnp.bfloat16)
    grad_mixed_blocks = grad_mixed_low.reshape(block_count, block_rows, heads, head_size)

    def back_step(state_in, inputs):
        grad_keys, grad_values = state_in
        query_block, grad_block, norm_block, offset = inputs
        scores = block_scores(
            query_block, keys_all, offset, segment, in_use, key_live, slopes, scale
        )
        probs = jnp.exp(scores - norm_block[:, :, None])
        grad_probs = jnp.einsum(
            "qhd,khd->hqk", grad_block, values, preferred_element_type=jnp.float32
        )
        grad_values = grad_values + jnp.einsum(
            "hqk,qhd->khd",
            probs.astype(jnp.bfloat16),
            grad_block,
            preferred_element_type=jnp.float32,
        )
        centered = grad_probs - jnp.sum(probs * grad_probs, axis=2, keepdims=True)
        grad_scores_low = (probs * centered).astype(jnp.bfloat16)
        grad_query_block = (
            jnp.einsum(
                "hqk,khd->qhd", grad_scores_low, keys_all, preferred_element_type=jnp.float32
            )
            * scale
        )
        grad_keys = (
            grad_keys
            + jnp.einsum(
                "hqk,qhd->khd", grad_scores_low, query_block, preferred_element_type=jnp.float32
            )
            * scale
        )
        return ((grad_keys, grad_values), grad_query_block)

    zero_heads = jnp.zeros((tok_rows, heads, head_size), jnp.float32)
    (grad_keys, grad_values), grad_query_blocks = lax.scan(
        back_step, (zero_heads, zero_heads), (query_blocks, grad_mixed_blocks, log_norm, offsets)
    )
    grad_qkv_low = jnp.concatenate(
        [
            grad_query_blocks.reshape(tok_rows, width),
            grad_keys.reshape(tok_rows, width),
            grad_values.reshape(tok_rows, width),
        ],
        axis=1,
    ).astype(jnp.bfloat16)
    grad_w_qkv = outer_product(normed_low, grad_qkv_low)
    grad_qkv_sums = column_sums(grad_qkv_low)
    grad_b_query = grad_qkv_sums[:width]
    grad_b_value = grad_qkv_sums[2 * width :]
    grad_normed = back_product(grad_qkv_low, qkv_mat)
    norm_pull_one = jax.vjp(norm_apply, first_proj, gain_back, shift_back)[1]
    grad_first, grad_gain_one, grad_shift_one = norm_pull_one(grad_normed)
    grad_first_low = (grad_first + grad_second).astype(jnp.bfloat16)
    grad_w_skip = outer_product(joined, grad_first_low)
    grad_b_skip = column_sums(grad_first_low)
    grad_joined = back_product(grad_first_low, skip_mat).astype(jnp.bfloat16)
    grad_frames = grad_joined[:, :width]
    grad_skip = grad_joined[:, width:]
    shards = reduce_grads(
        (
            grad_w_skip,
            grad_b_skip,
            grad_gain_one,
            grad_shift_one,
            grad_w_qkv,
            grad_b_query,
            grad_b_value,
            grad_w_out,
            grad_b_out,
            grad_gain_two,
            grad_shift_two,
            grad_w_up,
            grad_b_up,
            grad_w_down,
            grad_b_down,
        )
    )
    return (
        layer_out,
        grad_frames,
        grad_skip,
        shards[0],
        shards[1],
        shards[2],
        shards[3],
        shards[4],
        shards[5],
        shards[6],
        shards[7],
        shards[8],
        shards[9],
        shards[10],
        shards[11],
        shards[12],
        shards[13],
        shards[14],
    )


def solution(mesh):
    placed = (
        P(("wide", "narrow"), None),
        P(("wide", "narrow"), None),
        P(("wide", "narrow"), None),
        P(("wide", "narrow")),
        P(("wide", "narrow"), None),
        P(("wide", "narrow"), None),
        P(("wide", "narrow")),
        P(("wide", "narrow")),
        P(("wide", "narrow")),
        P(("wide", "narrow"), None),
        P(("wide", "narrow")),
        P(("wide", "narrow")),
        P(("wide", "narrow"), None),
        P(("wide", "narrow")),
        P(("wide", "narrow")),
        P(("wide", "narrow")),
        P(("wide", "narrow"), None),
        P(("wide", "narrow")),
        P(("wide", "narrow"), None),
        P(("wide", "narrow")),
    )
    return jax.shard_map(
        body,
        mesh=mesh,
        in_specs=placed,
        out_specs=(
            P(("wide", "narrow"), None),
            P(("wide", "narrow"), None),
            P(("wide", "narrow"), None),
            P(("wide", "narrow"), None),
            P(("wide", "narrow")),
            P(("wide", "narrow")),
            P(("wide", "narrow")),
            P(("wide", "narrow"), None),
            P(("wide", "narrow")),
            P(("wide", "narrow")),
            P(("wide", "narrow"), None),
            P(("wide", "narrow")),
            P(("wide", "narrow")),
            P(("wide", "narrow")),
            P(("wide", "narrow"), None),
            P(("wide", "narrow")),
            P(("wide", "narrow"), None),
            P(("wide", "narrow")),
        ),
        check_vma=False,
    )
```

profile of v0, /device:TPU:0, one launch (start us, length us, event | category | flops | bytes accessed | tf_op | source)
XLA Modules:
  0.0 1374.6 jit_solution(16584838109708940868)
XLA Ops:
  19.6 42.6 %all-reduce.20 = (bf16[1024]{0:T(1024)(128)(2,1)S(1)}, bf16[1024]{0:T(1024)(128)(2,1)S(1)}, bf16[1024]{0:T(1024)(128)(2,1)S(1)}, bf16[1024]{0:T(1024)(128)(2,1)S...) all-reduce(bf16[1024]{0:T(1024)(128)(2,1)S(1)} %dynamic-update-slic, ...), channel_id=1, replica_groups=mesh['wide'=8,'narrow'=4] {'wide','narrow'}, use_global_device_ids=true, to_apply=%add.5 | all-reduce | flops 9216 | bytes 36864
  64.2 41.4 %all-gather = bf16[32,1,128]{2,1,0:T(2,128)(2,1)S(1)} all-gather(bf16[1,1,128]{2,1,0:T(2,128)(2,1)} %bitcast.139), channel_id=1, replica_groups=mesh['wide'=8,'narrow'=4] {'wide','narrow'}, dimensions={0}, use_global_device_ids=true | all-gather | bytes 8448 | tf_op jit(solution)/shard_map/all_gather | solution.py:80
  114.1 7.7 add_reduce_fusion
  124.7 22.4 %all-gather.9.cloned.1.call-done = bf16[1024,3072]{1,0:T(8,128)(2,1)} async-done(((bf16[32,3072]{1,0:T(8,128)(2,1)}), bf16[1024,3072]{1,0:T(8,128)(2,1)}) %all-gather.9.cloned.1.call-update) | async-done | bytes 6291472 | tf_op jit(solution)/shard_map/all_gather | solution.py:72
  147.1 11.1 add_convert_fusion
  173.1 5.4 copy.87
  178.8 111.1 %while.28 = (s32[]{:T(128)}, bf16[2,512,16,64]{1,3,2,0:T(8,128)(2,1)S(1)}, f32[2,16,512]{2,1,0:T(8,128)S(1)}, s32[2]{0:T(128)S(1)}, s32[1024]{0:T(1024)S(1)}, /*...) while((s32[]{:T(128)}, ...), condition=%wide.region_7.8_spmd.clone, body=%wide.region_4.7_spmd.clone.sunk | while | flops 2302665216 | bytes 118771072 | solution.py:206
  183.4 17.2 %fusion.106 = (f32[16,512]{1,0:T(8,128)S(1)}, f32[16,512,1024]{2,1,0:T(8,128)}) fusion(f32[512,1024]{1,0:T(8,128)S(1)} %abs_convert_fusion.4, f32[16]{0:T(128)S(1)} %multiply_exponential_fusion.4, pred[512,1024]{1,0:T(8,128)(4,1)S(1)} %fusion.105, bf16[1024,16,64]{0,2,1:T(8,128)(2,1)} %get-tuple-element.666, ...), kind=kOutput, calls=%fused_computation.6.clone.1 | convolution fusion | flops 1115676672 | bytes 39354436 | tf_op jit(solution)/shard_map/while/body/eval_jaxpr/qhd,khd->hqk/dot_general | solution.py:53
  200.7 16.4 %fusion.107 = f32[16,512]{1,0:T(8,128)S(1)} fusion(f32[16,512,1024]{2,1,0:T(8,128)} %get-tuple-element.615, f32[16,512]{1,0:T(8,128)S(1)} %get-tuple-element.616, f32[512,1024]{1,0:T(8,128)S(1)} %abs_convert_fusion.4, f32[16]{0:T(128)S(1)} %multiply_exponential_fusion.4, pred[512,1024]{1,0:T(8,128)(4,1)S(1)} %fusion.105), kind=kLoop, calls=%fused_computation.5.clone.1 | loop fusion | flops 50323456 | bytes 36241472 | tf_op jit(solution)/shard_map/while/body/eval_jaxpr/reduce_sum | solution.py:199
  217.1 16.7 %bitcast_dynamic-update-slice_fusion.6 = bf16[2,512,16,64]{1,3,2,0:T(8,128)(2,1)S(1)} fusion(bf16[2,512,16,64]{1,3,2,0:T(8,128)(2,1)S(1)} %get-tuple-element.646, s32[]{:T(128)S(6)} %copy.123, bf16[1024,16,64]{0,2,1:T(8,128)(2,1)} %get-tuple-element.667, f32[16,512,1024]{2,1,0:T(8,128)} %get-tuple-element.615, f32[16,512]{1,0:T(8,128)S(1)} %fusion.107, ...), kind=kOutput, calls=%fused_computation.8.clone.1 | convolution fusion | flops 1132462080 | bytes 40436228 | tf_op jit(solution)/shard_map/while/body/eval_jaxpr/hqk,khd->qhd/dot_general | solution.py:201
  238.3 18.1 %fusion.106 = (f32[16,512]{1,0:T(8,128)S(1)}, f32[16,512,1024]{2,1,0:T(8,128)}) fusion(f32[512,1024]{1,0:T(8,128)S(1)} %abs_convert_fusion.4, f32[16]{0:T(128)S(1)} %multiply_exponential_fusion.4, pred[512,1024]{1,0:T(8,128)(4,1)S(1)} %fusion.105, bf16[1024,16,64]{0,2,1:T(8,128)(2,1)} %get-tuple-element.666, ...), kind=kOutput, calls=%fused_computation.6.clone.1 | convolution fusion | flops 1115676672 | bytes 39354436 | tf_op jit(solution)/shard_map/while/body/eval_jaxpr/qhd,khd->hqk/dot_general | solution.py:53
  256.4 16.3 %fusion.107 = f32[16,512]{1,0:T(8,128)S(1)} fusion(f32[16,512,1024]{2,1,0:T(8,128)} %get-tuple-element.615, f32[16,512]{1,0:T(8,128)S(1)} %get-tuple-element.616, f32[512,1024]{1,0:T(8,128)S(1)} %abs_convert_fusion.4, f32[16]{0:T(128)S(1)} %multiply_exponential_fusion.4, pred[512,1024]{1,0:T(8,128)(4,1)S(1)} %fusion.105), kind=kLoop, calls=%fused_computation.5.clone.1 | loop fusion | flops 50323456 | bytes 36241472 | tf_op jit(solution)/shard_map/while/body/eval_jaxpr/reduce_sum | solution.py:199
  272.7 16.9 %bitcast_dynamic-update-slice_fusion.6 = bf16[2,512,16,64]{1,3,2,0:T(8,128)(2,1)S(1)} fusion(bf16[2,512,16,64]{1,3,2,0:T(8,128)(2,1)S(1)} %get-tuple-element.646, s32[]{:T(128)S(6)} %copy.123, bf16[1024,16,64]{0,2,1:T(8,128)(2,1)} %get-tuple-element.667, f32[16,512,1024]{2,1,0:T(8,128)} %get-tuple-element.615, f32[16,512]{1,0:T(8,128)S(1)} %fusion.107, ...), kind=kOutput, calls=%fused_computation.8.clone.1 | convolution fusion | flops 1132462080 | bytes 40436228 | tf_op jit(solution)/shard_map/while/body/eval_jaxpr/hqk,khd->qhd/dot_general | solution.py:201
  292.6 6.3 fusion.53
  301.7 17.0 %fusion.45 = f32[1024,4096]{1,0:T(8,128)} fusion(bf16[1024,4096]{1,0:T(8,128)(2,1)} %all-gather.13.cloned.1.call-done, f32[1024,1024]{0,1:T(8,128)} %copy-done.9, f32[1024]{0:T(1024)S(1)} %copy-done.47, f32[1024]{0:T(1024)S(1)} %copy-done.34, f32[1024]{0:T(1024)S(1)} %fusion.40, f32[1024]{0:T(1024)S(1)} %broadcast_multiply_fusion), kind=kOutput, calls=%fused_computation.107 | convolution fusion | flops 8595177472 | bytes 29376512 | tf_op jit(solution)/shard_map/dot_general | solution.py:214
  318.7 44.3 %all-gather.15.cloned.1.call-done = bf16[4096,1024]{1,0:T(8,128)(2,1)} async-done(((bf16[128,1024]{1,0:T(8,128)(2,1)}), bf16[4096,1024]{1,0:T(8,128)(2,1)}) %all-gather.15.cloned.1.call-update) | async-done | bytes 8388624 | tf_op jit(solution)/shard_map/all_gather | solution.py:81
  363.0 27.9 %convert_reduce_fusion = (f32[4096]{0:T(1024)}, bf16[1024,4096]{1,0:T(8,128)(2,1)}) fusion(f32[1024,4096]{1,0:T(8,128)} %fusion.45, f32[4096]{0:T(1024)S(1)} %bitcast.136, bf16[1024,1024]{1,0:T(8,128)(2,1)S(1)} %copy-done.18, bf16[4096,1024]{1,0:T(8,128)(2,1)} %all-gather.15.cloned.1.call-done), kind=kOutput, calls=%fused_computation.58 | convolution fusion | flops 8703176704 | bytes 35684352 | tf_op jit(solution)/shard_map/dot_general | solution.py:30
  390.9 13.3 fusion.55
  404.2 5.5 copy.90
  409.7 5.4 multiply_reduce_fusion.1
  424.2 5.3 convolution_convert_fusion.1
  429.5 6.4 reshape.406
  435.9 5.5 copy.94
  442.9 226.4 %while.29 = (s32[]{:T(128)}, f32[1024,16,64]{0,2,1:T(8,128)}, f32[1024,16,64]{0,2,1:T(8,128)}, bf16[2,512,16,64]{1,3,2,0:T(8,128)(2,1)}, bf16[2,512,16,64]{1,3,2...) while((s32[]{:T(128)}, f32[1024,16,64]{0,2,1:T(8,128)}, ...), condition=%wide.region_14.15_spmd.clone, body=%wide.region_12.14_spmd.clone.sunk | while | flops 5470937600 | bytes 353553280 | solution.py:296
  447.6 17.7 %fusion.117 = f32[16,512,1024]{2,1,0:T(8,128)} fusion(bf16[1024,16,64]{0,2,1:T(8,128)(2,1)} %get-tuple-element.715, bf16[2,512,16,64]{1,3,2,0:T(8,128)(2,1)} %get-tuple-element.714, s32[]{:T(128)S(6)} %copy.133), kind=kOutput, calls=%fused_computation.33.clone.1 | convolution fusion | flops 1073741824 | bytes 36700164 | tf_op jit(solution)/shard_map/while/body/eval_jaxpr/qhd,khd->hqk/dot_general | solution.py:269
  465.3 28.0 %multiply_reduce_fusion.8 = (f32[16,512]{1,0:T(8,128)S(1)}, f32[16,512,1024]{2,1,0:T(8,128)}) fusion(f32[16,512,1024]{2,1,0:T(8,128)} %fusion.117, f32[16,512]{1,0:T(8,128)S(1)} %dynamic-slice_bitcast_fusion.2, f32[512,1024]{1,0:T(8,128)S(1)} %abs_convert_fusion.5, f32[16]{0:T(128)S(1)} %multiply_exponential_fusion.5, ...), kind=kOutput, calls=%fused_computation.22.clone.1 | convolution fusion | flops 1132453888 | bytes 72941632 | tf_op jit(solution)/shard_map/while/body/eval_jaxpr/qhd,khd->hqk/dot_general | solution.py:53
  493.3 27.7 %multiply_convert_fusion.5 = bf16[16,512,1024]{2,1,0:T(8,128)(2,1)} fusion(f32[16,512,1024]{2,1,0:T(8,128)} %get-tuple-element.630, f32[16,512,1024]{2,1,0:T(8,128)} %fusion.117, f32[16,512]{1,0:T(8,128)S(1)} %get-tuple-element.631), kind=kLoop, calls=%fused_computation.21.clone.1 | loop fusion | flops 25165824 | bytes 83918848 | tf_op jit(solution)/shard_map/while/body/eval_jaxpr/convert_element_type | solution.py:279
  520.9 16.1 %bitcast_add_fusion.5 = f32[1024,16,64]{0,2,1:T(8,128)} fusion(f32[1024,16,64]{0,2,1:T(8,128)} %get-tuple-element.689, f32[16,512,1024]{2,1,0:T(8,128)} %get-tuple-element.630, pred[]{:T(512)S(6)} %compare.3, bf16[2,512,16,64]{1,3,2,0:T(8,128)(2,1)} %get-tuple-element.714, s32[]{:T(128)S(6)} %copy.133), kind=kOutput, calls=%fused_computation.26.clone.1 | convolution fusion | flops 1084227584 | bytes 42991620 | tf_op jit(solution)/shard_map/while/body/eval_jaxpr/hqk,qhd->khd/dot_general | solution.py:272
  537.0 10.4 bitcast_dynamic-update-slice_fusion.8
  548.7 6.4 bitcast_add_fusion.4
  559.6 17.5 %fusion.117 = f32[16,512,1024]{2,1,0:T(8,128)} fusion(bf16[1024,16,64]{0,2,1:T(8,128)(2,1)} %get-tuple-element.715, bf16[2,512,16,64]{1,3,2,0:T(8,128)(2,1)} %get-tuple-element.714, s32[]{:T(128)S(6)} %copy.133), kind=kOutput, calls=%fused_computation.33.clone.1 | convolution fusion | flops 1073741824 | bytes 36700164 | tf_op jit(solution)/shard_map/while/body/eval_jaxpr/qhd,khd->hqk/dot_general | solution.py:269
  577.1 28.0 %multiply_reduce_fusion.8 = (f32[16,512]{1,0:T(8,128)S(1)}, f32[16,512,1024]{2,1,0:T(8,128)}) fusion(f32[16,512,1024]{2,1,0:T(8,128)} %fusion.117, f32[16,512]{1,0:T(8,128)S(1)} %dynamic-slice_bitcast_fusion.2, f32[512,1024]{1,0:T(8,128)S(1)} %abs_convert_fusion.5, f32[16]{0:T(128)S(1)} %multiply_exponential_fusion.5, ...), kind=kOutput, calls=%fused_computation.22.clone.1 | convolution fusion | flops 1132453888 | bytes 72941632 | tf_op jit(solution)/shard_map/while/body/eval_jaxpr/qhd,khd->hqk/dot_general | solution.py:53
  605.1 27.4 %multiply_convert_fusion.5 = bf16[16,512,1024]{2,1,0:T(8,128)(2,1)} fusion(f32[16,512,1024]{2,1,0:T(8,128)} %get-tuple-element.630, f32[16,512,1024]{2,1,0:T(8,128)} %fusion.117, f32[16,512]{1,0:T(8,128)S(1)} %get-tuple-element.631), kind=kLoop, calls=%fused_computation.21.clone.1 | loop fusion | flops 25165824 | bytes 83918848 | tf_op jit(solution)/shard_map/while/body/eval_jaxpr/convert_element_type | solution.py:279
  632.5 17.1 %bitcast_add_fusion.5 = f32[1024,16,64]{0,2,1:T(8,128)} fusion(f32[1024,16,64]{0,2,1:T(8,128)} %get-tuple-element.689, f32[16,512,1024]{2,1,0:T(8,128)} %get-tuple-element.630, pred[]{:T(512)S(6)} %compare.3, bf16[2,512,16,64]{1,3,2,0:T(8,128)(2,1)} %get-tuple-element.714, s32[]{:T(128)S(6)} %copy.133), kind=kOutput, calls=%fused_computation.26.clone.1 | convolution fusion | flops 1084227584 | bytes 42991620 | tf_op jit(solution)/shard_map/while/body/eval_jaxpr/hqk,qhd->khd/dot_general | solution.py:272
  649.7 10.3 bitcast_dynamic-update-slice_fusion.8
  661.2 7.7 bitcast_add_fusion.4
  679.0 13.1 fusion.41
  692.1 12.0 fusion.54
  704.1 5.6 copy.96
  724.3 7.0 fusion.56
  732.1 20.8 %fusion.46 = f32[4096,1024]{1,0:T(8,128)} fusion(bf16[1024,1024]{1,0:T(8,128)(2,1)} %param.28, f32[1024,4096]{1,0:T(8,128)} %fusion.45, f32[4096]{0:T(1024)S(1)} %bitcast.137), kind=kOutput, calls=%fused_computation.108 | convolution fusion | flops 8631877632 | bytes 35667968 | tf_op jit(solution)/shard_map/dot_general | solution.py:24
  753.5 17.0 %fusion.44 = f32[1024,4096]{1,0:T(8,128)} fusion(bf16[1024,4096]{1,0:T(8,128)(2,1)} %get-tuple-element.455, f32[1024,1024]{0,1:T(8,128)} %copy-done.9, f32[1024]{0:T(1024)S(1)} %copy-done.48, f32[1024]{0:T(1024)S(1)} %copy-done.35, f32[1024]{0:T(1024)S(1)} %copy-done.39, f32[1024]{0:T(1024)S(1)} %copy-done.31), kind=kOutput, calls=%fused_computation.106 | convolution fusion | flops 8595177472 | bytes 29376512 | tf_op jit(solution)/shard_map/dot_general | solution.py:24
  771.2 17.2 %add_convert_fusion.2 = bf16[1024,1024]{0,1:T(8,128)(2,1)} fusion(f32[1024,1024]{0,1:T(8,128)} %copy-done.9, f32[1024]{0:T(1024)S(1)} %convert_element_type.127, bf16[4096,1024]{1,0:T(8,128)(2,1)} %all-gather.15.cloned.1.call-done, f32[1024,4096]{1,0:T(8,128)} %fusion.45, f32[4096]{0:T(1024)S(1)} %bitcast.138), kind=kOutput, calls=%fused_computation.74 | convolution fusion | flops 8635023360 | bytes 31477760 | tf_op jit(solution)/shard_map/dot_general | solution.py:220
  796.4 41.9 %all-reduce.19 = (f32[1024]{0:T(1024)S(1)}, f32[1024]{0:T(1024)S(1)}, f32[1024]{0:T(1024)S(1)}, f32[1024]{0:T(1024)S(1)}, f32[1024]{0:T(1024)S(1)}, /*index=5*/f...) all-reduce(f32[1024]{0:T(1024)S(1)} %get-tuple-element.458, ...), channel_id=3, replica_groups=mesh['wide'=8,'narrow'=4] {'wide','narrow'}, use_global_device_ids=true, to_apply=%region_19.20.clone | all-reduce | flops 13312 | bytes 106496
  844.1 7.4 convolution_convert_fusion
  854.0 144.1 %reduce-scatter.6.cloned.1.call-done = f32[64,1024]{1,0:T(8,128)} async-done(((f32[2048,1024]{1,0:T(8,128)}), f32[64,1024]{1,0:T(8,128)}) %reduce-scatter.6.cloned.1.call-update) | async-done | bytes 262160 | tf_op jit(solution)/shard_map/reduce_scatter | solution.py:88
  998.1 181.9 %reduce-scatter.14.cloned.1.call-done = f32[128,1024]{1,0:T(8,128)} async-done(((f32[4096,1024]{1,0:T(8,128)}), f32[128,1024]{1,0:T(8,128)}) %reduce-scatter.14.cloned.1.call-update) | async-done | bytes 524304 | tf_op jit(solution)/shard_map/reduce_scatter | solution.py:101
  1180.0 187.4 %reduce-scatter.12.cloned.1.call-done = f32[32,4096]{1,0:T(8,128)} async-done(((f32[1024,4096]{1,0:T(8,128)}), f32[32,4096]{1,0:T(8,128)}) %reduce-scatter.12.cloned.1.call-update) | async-done | bytes 524304 | tf_op jit(solution)/shard_map/reduce_scatter | solution.py:99
  (252 shorter events, 111.8 us)
Async XLA Ops:
  7.2 103.1 %copy-start.16 = (bf16[1024,1024]{1,0:T(8,128)(2,1)S(1)}, bf16[1024,1024]{1,0:T(8,128)(2,1)}, u32[]{:S(2)}) copy-start(bf16[1024,1024]{1,0:T(8,128)(2,1)} %param.24) | copy-start | bytes 6291460
  7.2 106.9 %all-gather.7.cloned.1.call-start = ((), (), s32[]{:S(2)}) async-start(), calls=%async_computation.5 | async-start | bytes 4325376 | tf_op jit(solution)/shard_map/all_gather | solution.py:68
  7.9 139.2 %all-gather.9.cloned.1.call-start = ((), (), s32[]{:S(2)}) async-start(), calls=%async_computation.6 | async-start | bytes 6488064 | tf_op jit(solution)/shard_map/all_gather | solution.py:72
  8.7 283.9 %all-gather.11.cloned.1.call-start = ((), (), s32[]{:S(2)}) async-start(), calls=%async_computation.7 | async-start | bytes 2162688 | tf_op jit(solution)/shard_map/all_gather | solution.py:75
  9.4 292.2 %all-gather.13.cloned.1.call-start = ((), (), s32[]{:S(2)}) async-start(), calls=%async_computation.8 | async-start | bytes 8650752 | tf_op jit(solution)/shard_map/all_gather | solution.py:79
  10.0 353.0 %all-gather.15.cloned.1.call-start = ((), (), s32[]{:S(2)}) async-start(), calls=%async_computation.9 | async-start | bytes 8650752 | tf_op jit(solution)/shard_map/all_gather | solution.py:81
  10.6 843.4 %reduce-scatter.10.cloned.1.call-start = ((), (), s32[]{:S(2)}) async-start(), calls=%async_computation.12 | async-start | bytes 4325376 | tf_op jit(solution)/shard_map/reduce_scatter | solution.py:95
  63.0 84.1 %copy-start.23 = (f32[1024]{0:T(1024)}, f32[1024]{0:T(1024)S(1)}, u32[]{:S(2)}) copy-start(f32[1024]{0:T(1024)S(1)} %convert_element_type.112) | copy-start | bytes 12292
  63.0 84.1 %copy-start.28 = (f32[1024]{0:T(1024)}, f32[1024]{0:T(1024)S(1)}, u32[]{:S(2)}) copy-start(f32[1024]{0:T(1024)S(1)} %convert_element_type.114) | copy-start | bytes 12292
  63.6 83.5 %copy-start.49 = (f32[1024]{0:T(1024)}, f32[1024]{0:T(1024)S(1)}, u32[]{:S(2)}) copy-start(f32[1024]{0:T(1024)S(1)} %convert_element_type.115) | copy-start | bytes 12292
  106.3 4.2 copy-start.52
  121.8 36.4 %copy-start.26 = (f32[1024]{0:T(1024)}, f32[1024]{0:T(1024)S(1)}, u32[]{:S(2)}) copy-start(f32[1024]{0:T(1024)S(1)} %broadcast_multiply_fusion.1) | copy-start | bytes 12292
  124.7 33.5 %copy-start.40 = (f32[1024]{0:T(1024)}, f32[1024]{0:T(1024)S(1)}, u32[]{:S(2)}) copy-start(f32[1024]{0:T(1024)S(1)} %multiply_reduce_fusion.6) | copy-start | bytes 12292
  124.7 33.5 %copy-start.36 = (f32[1024]{0:T(1024)}, f32[1024]{0:T(1024)S(1)}, u32[]{:S(2)}) copy-start(f32[1024]{0:T(1024)S(1)} %fusion.39) | copy-start | bytes 12292
  289.8 2.8 copy-start.24
  289.8 2.8 copy-start.51
  292.6 6.4 copy-start.19
  299.0 2.6 copy-start.34
  299.1 116.1 %copy-start.30 = (f32[1024]{0:T(1024)}, f32[1024]{0:T(1024)S(1)}, u32[]{:S(2)}) copy-start(f32[1024]{0:T(1024)S(1)} %broadcast_multiply_fusion) | copy-start | bytes 12292
  301.6 113.5 %copy-start.38 = (f32[1024]{0:T(1024)}, f32[1024]{0:T(1024)S(1)}, u32[]{:S(2)}) copy-start(f32[1024]{0:T(1024)S(1)} %fusion.40) | copy-start | bytes 12292
  301.6 61.4 %copy-start.18 = (bf16[1024,1024]{1,0:T(8,128)(2,1)S(1)}, bf16[1024,1024]{1,0:T(8,128)(2,1)}, u32[]{:S(2)}) copy-start(bf16[1024,1024]{1,0:T(8,128)(2,1)} %param.28) | copy-start | bytes 6291460
  301.6 61.3 %copy-start.44 = (f32[32,1,128]{2,1,0:T(1,128)S(1)}, f32[32,1,128]{2,1,0:T(1,128)}, u32[]{:S(2)}) copy-start(f32[32,1,128]{2,1,0:T(1,128)} %convert_element_type.139) | copy-start | bytes 49156
  363.0 27.9 %copy-start.55 = (bf16[1024,4096]{1,0:T(8,128)(2,1)S(1)}, bf16[1024,4096]{1,0:T(8,128)(2,1)}, u32[]{:S(2)}) copy-start(bf16[1024,4096]{1,0:T(8,128)(2,1)} %all-gather.13.cloned.1.call-done) | copy-start | bytes 25165828
  409.7 5.4 copy-start.10
  409.7 5.9 copy-start.11
  424.2 429.8 %reduce-scatter.8.cloned.1.call-start = ((), (), s32[]{:S(2)}) async-start(), calls=%async_computation.11 | async-start | bytes 12976128 | tf_op jit(solution)/shard_map/reduce_scatter | solution.py:92
  537.0 11.7 copy-start
  649.7 11.5 copy-start
  669.3 5.9 copy-start.1
  675.5 3.5 copy-start.4
  675.5 3.5 copy-start.25
  675.5 3.5 copy-start.27
  675.5 3.5 copy-start.29
  675.5 3.5 copy-start.37
  675.5 3.5 copy-start.50
  692.1 306.0 %reduce-scatter.6.cloned.1.call-start = ((), (), s32[]{:S(2)}) async-start(), calls=%async_computation.10 | async-start | bytes 8650752 | tf_op jit(solution)/shard_map/reduce_scatter | solution.py:88
  709.7 4.9 copy-start.41
  709.7 5.4 copy-start.5
  709.7 6.8 copy-start.6
  716.5 3.2 copy-start.13
  716.5 3.2 copy-start.33
  719.7 4.6 copy-start.22
  731.4 448.6 %reduce-scatter.14.cloned.1.call-start = ((), (), s32[]{:S(2)}) async-start(), calls=%async_computation.14 | async-start | bytes 17301504 | tf_op jit(solution)/shard_map/reduce_scatter | solution.py:101
  752.9 614.5 %reduce-scatter.12.cloned.1.call-start = ((), (), s32[]{:S(2)}) async-start(), calls=%async_computation.13 | async-start | bytes 17301504 | tf_op jit(solution)/shard_map/reduce_scatter | solution.py:99
  792.3 4.1 copy-start.42
  792.3 4.1 copy-start.43
  792.3 4.1 copy-start.46
  792.3 4.1 copy-start.53
  (19 other events, 30.3 us)
Sparse Core Ops, SparseCore 0:
  10.9 65.0 all-gather.6
  78.9 68.1 all-gather.8
  150.0 54.8 all-gather.10
  207.6 76.3 all-gather.12
  286.8 76.1 all-gather.14
  424.3 140.0 reduce-scatter.9
  692.2 155.5 reduce-scatter.7
  850.8 147.3 reduce-scatter.5
  1001.1 178.8 reduce-scatter.13
  1182.8 184.5 reduce-scatter.11
where the time goes:
time: 1380 us; the launch traced here: 1370 us
  waiting for transfers between devices  583 us (42%)
  matrix products  415 us (30%)
  blocking collectives  126 us (9%)
  other arithmetic  123 us (9%)
  local copies, waits for them, and re-layouts  102 us (7%)
  between operations  15.3 us (1%)
    reduce_scatter x1, waiting for transfers between devices, reduce_grads(): lax.psum_scatter(g[11], ('wide', 'narrow'), scatter_dimension=0, tiled=True)  187 us
    reduce_scatter x1, waiting for transfers between devices, reduce_grads(): lax.psum_scatter(g[13], ('wide', 'narrow'), scatter_dimension=0, tiled=True)  182 us
    reduce_scatter x1, waiting for transfers between devices, reduce_grads(): lax.psum_scatter(g[0], ('wide', 'narrow'), scatter_dimension=0, tiled=True)  144 us
    dot_general x4, matrix products, block_scores(): jnp.einsum('qhd,khd->hqk', query_block, keys_all, preferred_element_type=...  91.3 us
    unnamed x2, blocking collectives  84.5 us
    dot_general x5, matrix products, back_product(): lax.dot_general(grad_in, weight, (((1,), (1,)), ((), ())), preferred_elem...  65.9 us
    dot_general x5, matrix products, outer_product(): lax.dot_general(left_op, right_op, (((0,), (0,)), ((), ())), preferred_el...  62.2 us
    convert_element_type x2, other arithmetic, back_step(): grad_scores_low = (probs * centered).astype(jnp.bfloat16)  55.1 us
  transfers between devices with their start and end apart: 10, of which 5 were waited for; matrix products, arithmetic and copies ran while one was open for 41% of the time, Pallas kernels for 0%

commit v1 on v0

v1 whole, which is shorter than its diff:
```python
import functools
import math

import jax
import jax.numpy as jnp
from jax import lax
from jax.experimental import pallas as pl
from jax.experimental.pallas import tpu as pltpu
from jax.sharding import PartitionSpec as P

HEADS = 16
EPSILON = 1e-05
FAR = 1e32
AXES = ("wide", "narrow")
BF = jnp.bfloat16
F32 = jnp.float32
VMEM_LIMIT = 56 * 1024 * 1024

ANY = pl.BlockSpec(memory_space=pl.ANY)
SMEM = pl.BlockSpec(memory_space=pltpu.SMEM)


def params():
    return pltpu.CompilerParams(vmem_limit_bytes=VMEM_LIMIT)


def cost(flops, nbytes, trans=0):
    return pl.CostEstimate(flops=int(flops), bytes_accessed=int(nbytes), transcendentals=int(trans))


class Net:
    def __init__(self, size, rows_min):
        self.size = size
        self.bits = size.bit_length() - 1
        self.high = self.bits - 3
        self.groups = 1 << self.high
        self.fast = size == 1 << self.bits and self.bits >= 3 and rows_min % 16 == 0
        self.shards = size if self.fast else 1

    def pp(self, x, mask):
        pairs = [(d, d ^ mask(d & 1)) for d in range(self.size)]
        return lax.ppermute(x, AXES, pairs)


def first_bit(core):
    return 2 + 2 * core


def second_bit(core):
    return 4 - 2 * core


def gather(net, shard):
    if not net.fast:
        return [lax.all_gather(shard, AXES, axis=0, tiled=True)[None]]
    block = shard[None]
    for bit in range(3, net.bits):
        block = jnp.concatenate([block, net.pp(block, lambda c: 1 << bit)], axis=0)
    one = net.pp(block, first_bit)
    own = [block, one, net.pp(block, second_bit), net.pp(one, second_bit)]
    return own + [net.pp(piece, lambda c: 1) for piece in own]


def piece_masks(core):
    a, b = first_bit(core), second_bit(core)
    return [0, a, b, 6, 1, 1 ^ b, 1 ^ a, 7]


def gather_vector(net, row):
    if not net.fast:
        return lax.all_gather(row, AXES, axis=0, tiled=True)
    me = lax.axis_index(AXES)
    for bit in range(net.bits):
        other = net.pp(row, lambda c: 1 << bit)
        row = jnp.where(
            (me >> bit) & 1 == 1,
            jnp.concatenate([other, row], axis=0),
            jnp.concatenate([row, other], axis=0),
        )
    return row


def scatter_vector(net, rows):
    if not net.fast:
        return lax.psum_scatter(rows, AXES, scatter_dimension=0, tiled=True)[0]
    me = lax.axis_index(AXES)
    for bit in reversed(range(net.bits)):
        half = 1 << bit
        up = (me >> bit) & 1 == 1
        keep = jnp.where(up, rows[half:], rows[:half])
        send = jnp.where(up, rows[:half], rows[half:])
        rows = keep + net.pp(send, lambda c: 1 << bit)
    return rows[0]


def scatter(net, parts):
    if not net.fast:
        return lax.psum_scatter(parts[0][0].astype(F32), AXES, scatter_dimension=0, tiled=True)
    keep, send = parts
    got = [net.pp(send, lambda c: 1)]
    masks = [second_bit, first_bit] + [
        (lambda c, bit=bit: 1 << bit) for bit in reversed(range(3, net.bits))
    ]
    half = keep.shape[0] // 2

    def summed(lo, hi):
        total = keep[lo:hi].astype(F32)
        for arr in got:
            total = total + arr[lo:hi].astype(F32)
        return total

    for mask in masks:
        got.append(net.pp(summed(half, 2 * half).astype(BF), mask))
        half //= 2
    return summed(0, 1)[0]


def load_start(net, me, pieces, dst, sems):
    copies = []
    if len(pieces) == 1:
        copies.append(pltpu.make_async_copy(pieces[0].at[0], dst, sems.at[0]))
    else:
        masks = piece_masks(me & 1)
        rows = dst.shape[0] // net.size
        for i, piece in enumerate(pieces):
            for j in range(net.groups):
                source = me ^ (masks[i] ^ (j << 3))
                at = pl.multiple_of(source * rows, rows)
                copies.append(
                    pltpu.make_async_copy(
                        piece.at[j], dst.at[pl.ds(at, rows), :], sems.at[len(copies)]
                    )
                )
    for copy in copies:
        copy.start()
    return copies


def relative(net, rel, core):
    bit_one, bit_two, group = (rel >> 1) & 1, (rel >> 2) & 1, rel >> 3
    top = jnp.where(core == 0, bit_two, bit_one)
    low = jnp.where(core == 0, bit_one, bit_two)
    return (top << (net.high + 1)) | (low << net.high) | group


def grad_out_shapes(net, rows, cols):
    if not net.fast:
        return [jax.ShapeDtypeStruct((1, rows, cols), BF)]
    shape = jax.ShapeDtypeStruct((net.size // 2, rows // net.size, cols), BF)
    return [shape, shape]


def store_start(net, me, src, base, rows, total_rows, outs, sems, first_sem):
    copies = []
    if not net.fast:
        copies.append(
            pltpu.make_async_copy(
                src.at[pl.ds(base, rows), :],
                outs[0].at[0, pl.ds(base, rows), :],
                sems.at[first_sem],
            )
        )
    else:
        shard = total_rows // net.size
        core = me & 1
        for i in range(0, rows // shard, 2):
            even = base // shard + i
            for k, out in enumerate(outs):
                owner_core = core if k == 0 else 1 - core
                target = even | owner_core
                rel = (me if k == 0 else me ^ 1) ^ target
                at = pl.multiple_of(target * shard, shard)
                copies.append(
                    pltpu.make_async_copy(
                        src.at[pl.ds(at, shard), :],
                        out.at[relative(net, rel, owner_core)],
                        sems.at[first_sem + i + k],
                    )
                )
    for copy in copies:
        copy.start()
    return copies


def dot(a, b):
    return jnp.dot(a, b, preferred_element_type=F32)


def dot_t(a, b):
    return lax.dot_general(a, b, (((1,), (1,)), ((), ())), preferred_element_type=F32)


def norm_parts(x):
    center = x - jnp.mean(x, axis=1, keepdims=True)
    spread = jnp.mean(center * center, axis=1, keepdims=True)
    rstd = lax.rsqrt(spread + EPSILON)
    return center * rstd, rstd


def sums(x):
    return jnp.sum(x, axis=0, keepdims=True)


def add_to(ref, value, step):
    @pl.when(step == 0)
    def _():
        ref[...] = value

    @pl.when(step > 0)
    def _():
        ref[...] += value


def row_block(tok):
    return min(512, tok)


def weight_scratch(net, *shapes):
    out = []
    for shape in shapes:
        out += [pltpu.VMEM(shape, BF), pltpu.SemaphoreType.DMA((net.shards,))]
    return out


def n_pieces(net):
    return 8 if net.fast else 1


def skip_kernel(net, me_ref, frames, skip, bias, gain, shift, *rest):
    np_ = n_pieces(net)
    pieces, (first_ref, normed_ref, w, sems) = rest[:np_], rest[np_:]

    @pl.when(pl.program_id(0) == 0)
    def _():
        for copy in load_start(net, me_ref[0], pieces, w, sems):
            copy.wait()

    width = frames.shape[1]
    first = dot(frames[...], w[:width, :]) + dot(skip[...], w[width:, :]) + bias[...]
    first_ref[...] = first
    xhat, _ = norm_parts(first)
    normed_ref[...] = (xhat * gain[...] + shift[...]).astype(BF)


def skip_forward(net, me, frames, skip, pieces, bias, gain, shift):
    tok, width = frames.shape
    blk = row_block(tok)
    rows = pl.BlockSpec((blk, width), lambda i: (i, 0))
    vec = pl.BlockSpec((1, width), lambda i: (0, 0))
    return pl.pallas_call(
        functools.partial(skip_kernel, net),
        grid=(tok // blk,),
        in_specs=[SMEM, rows, rows, vec, vec, vec] + [ANY] * len(pieces),
        out_specs=[rows, rows],
        out_shape=[jax.ShapeDtypeStruct((tok, width), F32), jax.ShapeDtypeStruct((tok, width), BF)],
        scratch_shapes=weight_scratch(net, (2 * width, width)),
        compiler_params=params(),
        cost_estimate=cost(4 * tok * width * width, tok * width * 10 + 4 * width * width),
        name="skip_forward",
    )(me, frames, skip, bias, gain, shift, *pieces)


def qkv_kernel(net, me_ref, normed, bias, *rest):
    np_ = n_pieces(net)
    pieces, (out_ref, w, sems) = rest[:np_], rest[np_:]

    @pl.when(pl.program_id(0) == 0)
    def _():
        for copy in load_start(net, me_ref[0], pieces, w, sems):
            copy.wait()

    chunk = 1024
    for at in range(0, w.shape[1], chunk):
        part = slice(at, at + chunk)
        out_ref[:, part] = (dot(normed[...], w[:, part]) + bias[:, part]).astype(BF)


def qkv_forward(net, me, normed, pieces, bias):
    tok, width = normed.shape
    cols = bias.shape[1]
    blk = row_block(tok)
    return pl.pallas_call(
        functools.partial(qkv_kernel, net),
        grid=(tok // blk,),
        in_specs=[
            SMEM,
            pl.BlockSpec((blk, width), lambda i: (i, 0)),
            pl.BlockSpec((1, cols), lambda i: (0, 0)),
        ]
        + [ANY] * len(pieces),
        out_specs=pl.BlockSpec((blk, cols), lambda i: (i, 0)),
        out_shape=jax.ShapeDtypeStruct((tok, cols), BF),
        scratch_shapes=weight_scratch(net, (width, cols)),
        compiler_params=params(),
        cost_estimate=cost(2 * tok * width * cols, tok * width * 8 + 6 * width * width),
        name="qkv_forward",
    )(me, normed, bias, *pieces)


def gelu_both(v):
    square = v * v
    th = jnp.tanh(0.7978845608 * v * (1.0 + 0.044715 * square))
    half = 0.5 * (1.0 + th)
    slope = half + 0.5 * v * (1.0 - th * th) * (0.7978845608 + 3 * 0.7978845608 * 0.044715 * square)
    return v * half, slope


def up_kernel(net, me_ref, first, mixed, b_out, gain, shift, b_up, *rest):
    np_ = n_pieces(net)
    out_pieces, up_pieces, rest = rest[:np_], rest[np_ : 2 * np_], rest[2 * np_ :]
    second_ref, normed_ref, act_ref, pull_ref, w_out, sems_out, w_up, sems_up = rest

    @pl.when(pl.program_id(0) == 0)
    def _():
        copies = load_start(net, me_ref[0], out_pieces, w_out, sems_out)
        copies += load_start(net, me_ref[0], up_pieces, w_up, sems_up)
        for copy in copies:
            copy.wait()

    second = first[...] + dot(mixed[...], w_out[...]) + b_out[...]
    second_ref[...] = second
    xhat, _ = norm_parts(second)
    normed = (xhat * gain[...] + shift[...]).astype(BF)
    normed_ref[...] = normed
    chunk = 1024
    for at in range(0, w_up.shape[1], chunk):
        part = slice(at, at + chunk)
        hidden = dot(normed, w_up[:, part]) + b_up[:, part]
        act, pull = gelu_both(hidden)
        act_ref[:, part] = act.astype(BF)
        pull_ref[:, part] = pull.astype(BF)


def up_forward(net, me, first, mixed, out_pieces, up_pieces, b_out, gain, shift, b_up):
    tok, width = first.shape
    ff = b_up.shape[1]
    blk = min(256, tok)
    rows = pl.BlockSpec((blk, width), lambda i: (i, 0))
    wide = pl.BlockSpec((blk, ff), lambda i: (i, 0))
    vec = pl.BlockSpec((1, width), lambda i: (0, 0))
    vec_ff = pl.BlockSpec((1, ff), lambda i: (0, 0))
    return pl.pallas_call(
        functools.partial(up_kernel, net),
        grid=(tok // blk,),
        in_specs=[SMEM, rows, rows, vec, vec, vec, vec_ff] + [ANY] * (2 * len(out_pieces)),
        out_specs=[rows, rows, wide, wide],
        out_shape=[
            jax.ShapeDtypeStruct((tok, width), F32),
            jax.ShapeDtypeStruct((tok, width), BF),
            jax.ShapeDtypeStruct((tok, ff), BF),
            jax.ShapeDtypeStruct((tok, ff), BF),
        ],
        scratch_shapes=weight_scratch(net, (width, width), (width, ff)),
        compiler_params=params(),
        cost_estimate=cost(
            2 * tok * width * (width + ff), tok * (width * 12 + ff * 4) + 2 * width * (width + ff)
        ),
        name="up_forward",
    )(me, first, mixed, b_out, gain, shift, b_up, *out_pieces, *up_pieces)


def down_kernel(net, me_ref, second, act, pull, cot, b_down, *rest):
    np_ = n_pieces(net)
    pieces, (out_ref, gh_ref, bsum_ref, csum_ref, w, sems) = rest[:np_], rest[np_:]
    step = pl.program_id(0)

    @pl.when(step == 0)
    def _():
        for copy in load_start(net, me_ref[0], pieces, w, sems):
            copy.wait()

    out_ref[...] = (second[...] + dot(act[...], w[...]) + b_down[...]).astype(BF)
    chunk = 1024
    for at in range(0, w.shape[0], chunk):
        part = slice(at, at + chunk)
        gh = (dot_t(cot[...], w[part, :]) * pull[:, part].astype(F32)).astype(BF)
        gh_ref[:, part] = gh
        add_to(bsum_ref.at[:, part], sums(gh.astype(F32)), step)
    add_to(csum_ref, sums(cot[...].astype(F32)), step)


def down_both(net, me, second, act, pull, cot, pieces, b_down):
    tok, width = second.shape
    ff = act.shape[1]
    blk = min(256, tok)
    rows = pl.BlockSpec((blk, width), lambda i: (i, 0))
    wide = pl.BlockSpec((blk, ff), lambda i: (i, 0))
    vec = pl.BlockSpec((1, width), lambda i: (0, 0))
    vec_ff = pl.BlockSpec((1, ff), lambda i: (0, 0))
    return pl.pallas_call(
        functools.partial(down_kernel, net),
        grid=(tok // blk,),
        in_specs=[SMEM, rows, wide, wide, rows, vec] + [ANY] * len(pieces),
        out_specs=[rows, wide, vec_ff, vec],
        out_shape=[
            jax.ShapeDtypeStruct((tok, width), BF),
            jax.ShapeDtypeStruct((tok, ff), BF),
            jax.ShapeDtypeStruct((1, ff), F32),
            jax.ShapeDtypeStruct((1, width), F32),
        ],
        scratch_shapes=weight_scratch(net, (ff, width)),
        compiler_params=params(),
        cost_estimate=cost(4 * tok * width * ff, tok * (width * 8 + ff * 6) + 2 * width * ff),
        name="down_both",
    )(me, second, act, pull, cot, b_down, *pieces)


def grad_kernel(net, lefts, blk, me_ref, *rest):
    left_refs, right, rest = rest[:lefts], rest[lefts], rest[lefts + 1 :]
    outs, (acc, sems) = rest[:-2], rest[-2:]
    step = pl.program_id(0)
    total = acc.shape[0]
    per_left = total // lefts // blk
    cols = acc.shape[1]
    chunk = 1024
    for k in range(lefts):

        @pl.when((step >= k * per_left) & (step < (k + 1) * per_left))
        def _():
            left = left_refs[k][...].T
            for at in range(0, cols, chunk):
                part = slice(at, at + chunk)
                acc[pl.ds(pl.multiple_of(step * blk, blk), blk), part] = dot(
                    left, right[:, part]
                ).astype(BF)

    steps = total // blk
    per_step = sems.shape[0] // steps
    for s in range(steps):

        @pl.when(step == s)
        def _():
            store_start(net, me_ref[0], acc, s * blk, blk, total, outs, sems, s * per_step)

    @pl.when(step == steps - 1)
    def _():
        for s in range(steps):
            for copy in store_list(
                net, me_ref[0], acc, s * blk, blk, total, outs, sems, s * per_step
            ):
                copy.wait()


def store_list(net, me, src, base, rows, total_rows, outs, sems, first_sem):
    copies = []
    if not net.fast:
        return [
            pltpu.make_async_copy(
                src.at[pl.ds(base, rows), :],
                outs[0].at[0, pl.ds(base, rows), :],
                sems.at[first_sem],
            )
        ]
    shard = total_rows // net.size
    core = me & 1
    for i in range(0, rows // shard, 2):
        even = base // shard + i
        for k, out in enumerate(outs):
            owner_core = core if k == 0 else 1 - core
            target = even | owner_core
            rel = (me if k == 0 else me ^ 1) ^ target
            at = pl.multiple_of(target * shard, shard)
            copies.append(
                pltpu.make_async_copy(
                    src.at[pl.ds(at, shard), :],
                    out.at[relative(net, rel, owner_core)],
                    sems.at[first_sem + i + k],
                )
            )
    return copies


def weight_grad(net, me, lefts, right, name):
    tok, cols = right.shape
    each = lefts[0].shape[1]
    total = each * len(lefts)
    blk = min(512, each)
    per_left = each // blk
    steps = total // blk
    per_step = blk // (total // net.size) if net.fast else 1

    def index(k):
        return lambda i: (0, jnp.clip(i - k * per_left, 0, per_left - 1))

    shapes = grad_out_shapes(net, total, cols)
    return pl.pallas_call(
        functools.partial(grad_kernel, net, len(lefts), blk),
        grid=(steps,),
        in_specs=[SMEM]
        + [pl.BlockSpec((tok, blk), index(k)) for k in range(len(lefts))]
        + [pl.BlockSpec((tok, cols), lambda i: (0, 0), pipeline_mode=pl.Buffered(1))],
        out_specs=[ANY] * len(shapes),
        out_shape=shapes,
        scratch_shapes=[
            pltpu.VMEM((total, cols), BF),
            pltpu.SemaphoreType.DMA((steps * per_step,)),
        ],
        compiler_params=params(),
        cost_estimate=cost(
            2 * tok * total * cols, 2 * tok * (total + cols) + 2 * total * cols
        ),
        name=name,
    )(me, *lefts, right)


def norm_back(dn, x, gain):
    xhat, rstd = norm_parts(x)
    scaled = dn * gain
    mean_one = jnp.mean(scaled, axis=1, keepdims=True)
    mean_two = jnp.mean(scaled * xhat, axis=1, keepdims=True)
    return (scaled - mean_one - xhat * mean_two) * rstd, dn * xhat


def second_kernel(net, me_ref, gh, second, cot, gain, *rest):
    np_ = n_pieces(net)
    up_pieces, out_pieces, rest = rest[:np_], rest[np_ : 2 * np_], rest[2 * np_ :]
    gsec_ref, gattn_ref, gmix_ref, ggain_ref, gshift_ref, gbout_ref = rest[:6]
    w_up, sems_up, w_out, sems_out = rest[6:]
    step = pl.program_id(0)

    @pl.when(step == 0)
    def _():
        copies = load_start(net, me_ref[0], up_pieces, w_up, sems_up)
        copies += load_start(net, me_ref[0], out_pieces, w_out, sems_out)
        for copy in copies:
            copy.wait()

    dn = dot_t(gh[...], w_up[...])
    pulled, dx = norm_back(dn, second[...], gain[...])
    gsec = cot[...].astype(F32) + pulled
    gsec_ref[...] = gsec
    gattn = gsec.astype(BF)
    gattn_ref[...] = gattn
    gmix_ref[...] = dot_t(gattn, w_out[...]).astype(BF)
    add_to(ggain_ref, sums(dx), step)
    add_to(gshift_ref, sums(dn), step)
    add_to(gbout_ref, sums(gattn.astype(F32)), step)


def second_back(net, me, gh, second, cot, up_pieces, out_pieces, gain):
    tok, width = second.shape
    ff = gh.shape[1]
    blk = min(256, tok)
    rows = pl.BlockSpec((blk, width), lambda i: (i, 0))
    wide = pl.BlockSpec((blk, ff), lambda i: (i, 0))
    vec = pl.BlockSpec((1, width), lambda i: (0, 0))
    vec_shape = jax.ShapeDtypeStruct((1, width), F32)
    return pl.pallas_call(
        functools.partial(second_kernel, net),
        grid=(tok // blk,),
        in_specs=[SMEM, wide, rows, rows, vec] + [ANY] * (2 * len(up_pieces)),
        out_specs=[rows, rows, rows, vec, vec, vec],
        out_shape=[
            jax.ShapeDtypeStruct((tok, width), F32),
            jax.ShapeDtypeStruct((tok, width), BF),
            jax.ShapeDtypeStruct((tok, width), BF),
            vec_shape,
            vec_shape,
            vec_shape,
        ],
        scratch_shapes=weight_scratch(net, (width, ff), (width, width)),
        compiler_params=params(),
        cost_estimate=cost(
            2 * tok * width * (width + ff), tok * (width * 14 + ff * 2) + 2 * width * (width + ff)
        ),
        name="second_back",
    )(me, gh, second, cot, gain, *up_pieces, *out_pieces)


def first_kernel(net, me_ref, gqkv, first, gsec, gain, *rest):
    np_ = n_pieces(net)
    pieces, rest = rest[:np_], rest[np_:]
    gfirst_ref, ggain_ref, gshift_ref, gbskip_ref, gbqkv_ref, w, sems = rest
    step = pl.program_id(0)

    @pl.when(step == 0)
    def _():
        for copy in load_start(net, me_ref[0], pieces, w, sems):
            copy.wait()

    dn = dot_t(gqkv[...], w[...])
    pulled, dx = norm_back(dn, first[...], gain[...])
    gfirst = (gsec[...] + pulled).astype(BF)
    gfirst_ref[...] = gfirst
    add_to(ggain_ref, sums(dx), step)
    add_to(gshift_ref, sums(dn), step)
    add_to(gbskip_ref, sums(gfirst.astype(F32)), step)
    add_to(gbqkv_ref, sums(gqkv[...].astype(F32)), step)


def first_back(net, me, gqkv, first, gsec, pieces, gain):
    tok, width = first.shape
    cols = gqkv.shape[1]
    blk = min(256, tok)
    rows = pl.BlockSpec((blk, width), lambda i: (i, 0))
    wide = pl.BlockSpec((blk, cols), lambda i: (i, 0))
    vec = pl.BlockSpec((1, width), lambda i: (0, 0))
    vec_wide = pl.BlockSpec((1, cols), lambda i: (0, 0))
    vec_shape = jax.ShapeDtypeStruct((1, width), F32)
    return pl.pallas_call(
        functools.partial(first_kernel, net),
        grid=(tok // blk,),
        in_specs=[SMEM, wide, rows, rows, vec] + [ANY] * len(pieces),
        out_specs=[rows, vec, vec, vec, vec_wide],
        out_shape=[
            jax.ShapeDtypeStruct((tok, width), BF),
            vec_shape,
            vec_shape,
            vec_shape,
            jax.ShapeDtypeStruct((1, cols), F32),
        ],
        scratch_shapes=weight_scratch(net, (width, cols)),
        compiler_params=params(),
        cost_estimate=cost(2 * tok * width * cols, tok * (width * 10 + cols * 2) + 2 * width * cols),
        name="first_back",
    )(me, gqkv, first, gsec, gain, *pieces)


def joined_kernel(net, me_ref, gfirst, *rest):
    np_ = n_pieces(net)
    pieces, (gframes_ref, gskip_ref, w, sems) = rest[:np_], rest[np_:]

    @pl.when(pl.program_id(0) == 0)
    def _():
        for copy in load_start(net, me_ref[0], pieces, w, sems):
            copy.wait()

    width = gframes_ref.shape[1]
    gframes_ref[...] = dot_t(gfirst[...], w[:width, :]).astype(BF)
    gskip_ref[...] = dot_t(gfirst[...], w[width:, :]).astype(BF)


def joined_back(net, me, gfirst, pieces):
    tok, width = gfirst.shape
    blk = row_block(tok)
    rows = pl.BlockSpec((blk, width), lambda i: (i, 0))
    out = jax.ShapeDtypeStruct((tok, width), BF)
    return pl.pallas_call(
        functools.partial(joined_kernel, net),
        grid=(tok // blk,),
        in_specs=[SMEM, rows] + [ANY] * len(pieces),
        out_specs=[rows, rows],
        out_shape=[out, out],
        scratch_shapes=weight_scratch(net, (2 * width, width)),
        compiler_params=params(),
        cost_estimate=cost(4 * tok * width * width, tok * width * 6 + 4 * width * width),
        name="joined_back",
    )(me, gfirst, *pieces)


def far_apart(row_tag, col_tag, row_at):
    shape = (row_tag.shape[0], col_tag.shape[1])
    i = row_at + lax.broadcasted_iota(jnp.int32, shape, 0)
    j = lax.broadcasted_iota(jnp.int32, shape, 1)
    ok = (row_tag == col_tag) | (i == j)
    return jnp.where(ok, jnp.abs(i - j).astype(F32), FAR)


def head_slope(head):
    return jnp.exp2((jnp.full((1, 1), head, jnp.int32).astype(F32) + 1.0) * (-8.0 / HEADS))


def attend_kernel(size, blk, q, k, v, tag_q, tag_k, out_ref, lse_ref, far):
    pair = pl.program_id(0)
    tok = q.shape[0]
    steps = tok // blk

    @pl.when(pair == 0)
    def _():
        lse_ref[...] = jnp.zeros_like(lse_ref)
        for i in range(steps):
            at = slice(i * blk, (i + 1) * blk)
            far[at, :] = far_apart(tag_q[at, :], tag_k[...], i * blk)

    lane = lax.broadcasted_iota(jnp.int32, (1, 2 * size), 1)
    lse_lane = lax.broadcasted_iota(jnp.int32, (1, lse_ref.shape[1]), 1)
    scale = size**-0.5
    for i in range(steps):
        at = slice(i * blk, (i + 1) * blk)
        q_blk = q[at, :] * scale
        outs, lse = [], lse_ref[at, :]
        for h in range(2):
            mine = (lane >= h * size) & (lane < (h + 1) * size)
            scores = dot_t(jnp.where(mine, q_blk, 0), k[...]) - head_slope(2 * pair + h) * far[at, :]
            top = jnp.max(scores, axis=1, keepdims=True)
            expo = jnp.exp(scores - top)
            denom = jnp.sum(expo, axis=1, keepdims=True)
            outs.append(dot(expo.astype(BF), v[...]) / denom)
            lse = jnp.where(lse_lane == 2 * pair + h, top + jnp.log(denom), lse)
        out_ref[at, :] = jnp.where(lane < size, outs[0], outs[1]).astype(BF)
        lse_ref[at, :] = lse


def attend(qkv, tag_q, tag_k, heads):
    tok = qkv.shape[0]
    width = qkv.shape[1] // 3
    size = width // heads
    pairs = heads // 2
    blk = min(256, tok)

    def cols(k):
        return pl.BlockSpec((tok, 2 * size), lambda p: (0, k * pairs + p))

    return pl.pallas_call(
        functools.partial(attend_kernel, size, blk),
        grid=(pairs,),
        in_specs=[
            cols(0),
            cols(1),
            cols(2),
            pl.BlockSpec((tok, 1), lambda p: (0, 0)),
            pl.BlockSpec((1, tok), lambda p: (0, 0)),
        ],
        out_specs=[
            pl.BlockSpec((tok, 2 * size), lambda p: (0, p)),
            pl.BlockSpec((tok, 128), lambda p: (0, 0)),
        ],
        out_shape=[
            jax.ShapeDtypeStruct((tok, width), BF),
            jax.ShapeDtypeStruct((tok, 128), F32),
        ],
        scratch_shapes=[pltpu.VMEM((tok, tok), F32)],
        compiler_params=params(),
        cost_estimate=cost(16 * heads * tok * tok * size, tok * width * 8, heads * tok * tok),
        name="attend",
    )(qkv, qkv, qkv, tag_q.reshape(tok, 1), tag_k.reshape(1, tok))


def attend_back_kernel(size, blk, q, k, v, g, o, lse, tag_k, tag_q, gq_ref, gk_ref, gv_ref, far, lse_t):
    pair = pl.program_id(0)
    tok = q.shape[0]
    steps = tok // blk

    @pl.when(pair == 0)
    def _():
        lse_t[...] = lse[...].T
        for i in range(steps):
            at = slice(i * blk, (i + 1) * blk)
            far[at, :] = far_apart(tag_k[at, :], tag_q[...], i * blk)

    lane = lax.broadcasted_iota(jnp.int32, (1, 2 * size), 1)
    scale = size**-0.5
    q_all = q[...] * scale
    g_all = g[...]
    products = (g_all.astype(F32) * o[...].astype(F32)).T
    k_t = (k[...] * scale).astype(F32).T.astype(BF)
    grads_q, kept = [], []
    for h in range(2):
        mine = (lane >= h * size) & (lane < (h + 1) * size)
        q_h = jnp.where(mine, q_all, 0)
        g_h = jnp.where(mine, g_all, 0)
        delta = jnp.sum(products[h * size : (h + 1) * size, :], axis=0, keepdims=True)
        norm = lse_t[pl.ds(2 * pair + h, 1), :]
        slope = head_slope(2 * pair + h)
        grad_q = jnp.zeros((size, tok), F32)
        for i in range(steps):
            at = slice(i * blk, (i + 1) * blk)
            scores = dot_t(k[at, :], q_h) - slope * far[at, :]
            probs = jnp.exp(scores - norm)
            pulled = dot_t(v[at, :], g_h)
            ds = (probs * (pulled - delta)).astype(BF)
            gv = dot(probs.astype(BF), g_all)
            gk = dot(ds, q_all)
            grad_q = grad_q + dot(k_t[h * size : (h + 1) * size, at], ds)
            if h == 0:
                gv_ref[at, :] = gv.astype(BF)
                gk_ref[at, :] = gk.astype(BF)
            else:
                gv_ref[at, :] = jnp.where(mine, gv.astype(BF), gv_ref[at, :])
                gk_ref[at, :] = jnp.where(mine, gk.astype(BF), gk_ref[at, :])
        grads_q.append(grad_q)
    gq_ref[...] = jnp.concatenate(grads_q, axis=0).T.astype(BF)


def attend_back(qkv, grad_mixed, mixed, lse, tag_q, tag_k, heads):
    tok = qkv.shape[0]
    width = qkv.shape[1] // 3
    size = width // heads
    pairs = heads // 2
    blk = min(256, tok)

    def cols(k):
        return pl.BlockSpec((tok, 2 * size), lambda p: (0, k * pairs + p))

    out = jax.ShapeDtypeStruct((tok, width), BF)
    return pl.pallas_call(
        functools.partial(attend_back_kernel, size, blk),
        grid=(pairs,),
        in_specs=[
            cols(0),
            cols(1),
            cols(2),
            cols(0),
            cols(0),
            pl.BlockSpec((tok, 128), lambda p: (0, 0)),
            pl.BlockSpec((tok, 1), lambda p: (0, 0)),
            pl.BlockSpec((1, tok), lambda p: (0, 0)),
        ],
        out_specs=[cols(0)] * 3,
        out_shape=[out] * 3,
        scratch_shapes=[pltpu.VMEM((tok, tok), F32), pltpu.VMEM((128, tok), F32)],
        compiler_params=params(),
        cost_estimate=cost(40 * heads * tok * tok * size, tok * width * 16, heads * tok * tok),
        name="attend_back",
    )(qkv, qkv, qkv, grad_mixed, mixed, lse, tag_k.reshape(tok, 1), tag_q.reshape(1, tok))


def tags(length_row, mask_row, tok):
    order = jnp.arange(length_row.shape[0])
    ends = jnp.sum(jnp.where(order[:, None] <= order[None, :], length_row[:, None], 0), axis=0)
    slots = jnp.arange(tok, dtype=jnp.int32)
    segment = jnp.sum((slots[:, None] >= ends[None, :]).astype(jnp.int32), axis=1)
    used = slots < jnp.sum(length_row)
    return jnp.where(used, segment, -1), jnp.where(used & (mask_row == 1), segment, -2)


def body(size, frames, skip, lengths, key_mask, cotangent, *weights):
    (
        w_skip, b_skip, pre_attn_gain, pre_attn_bias, w_qkv, b_query, b_value, w_out, b_out,
        pre_ffn_gain, pre_ffn_bias, w_up, b_up, w_down, b_down,
    ) = weights
    tok, width = frames.shape
    net = Net(size, min(w.shape[0] for w in (w_skip, w_qkv, w_out, w_up, w_down)))
    me = lax.axis_index(AXES).astype(jnp.int32).reshape(1)

    small = (
        b_skip, pre_attn_gain, pre_attn_bias, b_query, b_value, b_out, pre_ffn_gain, pre_ffn_bias, b_up, b_down,
    )
    vectors = gather_vector(net, jnp.concatenate(small).reshape(1, -1)).astype(F32)
    whole, at = [], 0
    for vec in small:
        whole.append(vectors[:, at : at + vec.shape[0]].reshape(1, -1))
        at += vec.shape[0]
    bskip, gain1, shift1, bquery, bvalue, bout, gain2, shift2, bup, bdown = whole

    skip_w = gather(net, w_skip)
    qkv_w = gather(net, w_qkv)
    out_w = gather(net, w_out)
    up_w = gather(net, w_up)
    down_w = gather(net, w_down)

    tag_q, tag_k = tags(lengths[0], key_mask, tok)

    first, normed = skip_forward(net, me, frames, skip, skip_w, bskip, gain1, shift1)
    qkv_bias = jnp.concatenate([bquery, jnp.zeros_like(bquery), bvalue], axis=1)
    qkv = qkv_forward(net, me, normed, qkv_w, qkv_bias)
    mixed, lse = attend(qkv, tag_q, tag_k, HEADS)
    second, normed2, act, pull = up_forward(
        net, me, first, mixed, out_w, up_w, bout, gain2, shift2, bup
    )
    down_parts = weight_grad(net, me, [act], cotangent, "grad_down")
    layer_out, gh, gbup, gbdown = down_both(net, me, second, act, pull, cotangent, down_w, bdown)
    up_parts = weight_grad(net, me, [normed2], gh, "grad_up")
    gsec, gattn, gmixed, ggain2, gshift2, gbout = second_back(
        net, me, gh, second, cotangent, up_w, out_w, gain2
    )
    out_parts = weight_grad(net, me, [mixed], gattn, "grad_out")
    gq, gk, gv = attend_back(qkv, gmixed, mixed, lse, tag_q, tag_k, HEADS)
    gqkv = jnp.concatenate([gq, gk, gv], axis=1)
    qkv_parts = weight_grad(net, me, [normed], gqkv, "grad_qkv")
    gfirst, ggain1, gshift1, gbskip, gbqkv = first_back(net, me, gqkv, first, gsec, qkv_w, gain1)
    skip_parts = weight_grad(net, me, [frames, skip], gfirst, "grad_skip")
    gframes, gskip = joined_back(net, me, gfirst, skip_w)

    grads_small = (
        gbskip, ggain1, gshift1, gbqkv[:, :width], gbqkv[:, 2 * width :], gbout, ggain2, gshift2, gbup, gbdown,
    )
    rows = jnp.concatenate([g.reshape(size, -1) for g in grads_small], axis=1)
    row = scatter_vector(net, rows)
    vec_out, at = [], 0
    for vec in small:
        vec_out.append(row[at : at + vec.shape[0]])
        at += vec.shape[0]
    obskip, ogain1, oshift1, obq, obv, obout, ogain2, oshift2, obup, obdown = vec_out
    return (
        layer_out,
        gframes,
        gskip,
        scatter(net, skip_parts),
        obskip,
        ogain1,
        oshift1,
        scatter(net, qkv_parts),
        obq,
        obv,
        scatter(net, out_parts),
        obout,
        ogain2,
        oshift2,
        scatter(net, up_parts),
        obup,
        scatter(net, down_parts),
        obdown,
    )


def solution(mesh):
    mat, vec = P(AXES, None), P(AXES)
    size = math.prod(mesh.shape.values())
    return jax.shard_map(
        functools.partial(body, size),
        mesh=mesh,
        in_specs=(
            mat, mat, mat, vec, mat,
            mat, vec, vec, vec, mat, vec, vec, mat, vec, vec, vec, mat, vec, mat, vec,
        ),
        out_specs=(
            mat, mat, mat,
            mat, vec, vec, vec, mat, vec, vec, mat, vec, vec, vec, mat, vec, mat, vec,
        ),
        check_vma=False,
    )
```

time: 1380 us -> 664 us (0.48)
  matrix products: 415 us -> 0 us
  waiting for transfers between devices: 583 us -> 231 us
  Pallas kernels: 0 us -> 285 us
  blocking collectives: 126 us -> 0 us
  other arithmetic: 123 us -> 39 us
  local copies, waits for them, and re-layouts: 102 us -> 27.8 us
  starting transfers between devices: 0.39 us -> 74 us
    reduce_scatter x5 -> x0, waiting for transfers between devices: 513 us -> none  [the longest x1 187 us: reduce_grads(): lax.psum_scatter(g[11], ('wide', 'narrow'), scatter_dimension=0, tiled=True)]
    dot_general x29 -> x0, matrix products: 415 us -> none  [the longest x4 91.3 us: block_scores(): jnp.einsum('qhd,khd->hqk', query_block, keys_all, preferred_element_type=...]
    pallas_call x0 -> x14, Pallas kernels: none -> 285 us  [the longest x5 58.1 us: weight_grad(): pl.pallas_call(functools.partial(grad_kernel, net, len(lefts), blk), grid...]
    ppermute x0 -> x80, waiting for transfers between devices: none -> 231 us  [pp(): return lax.ppermute(x, AXES, pairs)]
    unnamed x2 -> x0, blocking collectives: 84.5 us -> none
    ppermute x0 -> x80, starting transfers between devices: none -> 74 us  [pp(): return lax.ppermute(x, AXES, pairs)]
    all_gather x5 -> x0, waiting for transfers between devices: 66.7 us -> none  [the longest x1 44.3 us: fetch_weights(): lax.all_gather(p[13], ('wide', 'narrow'), axis=0, tiled=True)]
    reduce_sum x12 -> x3, other arithmetic: 56 us -> 0.8 us  [the longest x1 0.63 us: tags(): used = slots < jnp.sum(length_row)]
  transfers between devices with their start and end apart: 10 -> 80, of which waited for: 5 -> 28; matrix products, arithmetic and copies ran while one was open for 41% -> 6% of each run, Pallas kernels for 0% -> 23%
where the time goes in v1:
time: 664 us; the launch traced here: 659 us
  Pallas kernels  285 us (43%)
  waiting for transfers between devices  231 us (35%)
  starting transfers between devices  74 us (11%)
  other arithmetic  39 us (6%)
  local copies, waits for them, and re-layouts  27.8 us (4%)
    ppermute x80, waiting for transfers between devices, pp(): return lax.ppermute(x, AXES, pairs)  231 us
    ppermute x80, starting transfers between devices, pp(): return lax.ppermute(x, AXES, pairs)  74 us
    pallas_call x5, Pallas kernels, weight_grad(): pl.pallas_call(functools.partial(grad_kernel, net, len(lefts), blk), grid...  58.1 us
    pallas_call x1, Pallas kernels, attend_back(): pl.pallas_call(functools.partial(attend_back_kernel, size, blk), grid=(pa...  53.1 us
    pallas_call x1, Pallas kernels, attend(): pl.pallas_call(functools.partial(attend_kernel, size, blk), grid=(pairs,)...  38.8 us
    pallas_call x1, Pallas kernels, down_both(): pl.pallas_call(functools.partial(down_kernel, net), grid=(tok // blk,), i...  30.8 us
    pallas_call x1, Pallas kernels, up_forward(): pl.pallas_call(functools.partial(up_kernel, net), grid=(tok // blk,), in_...  30.8 us
    pallas_call x1, Pallas kernels, second_back(): pl.pallas_call(functools.partial(second_kernel, net), grid=(tok // blk,),...  22.4 us
  transfers between devices with their start and end apart: 80, of which 28 were waited for; matrix products, arithmetic and copies ran while one was open for 6% of the time, Pallas kernels for 23%

profile of v1, /device:TPU:0, one launch (start us, length us, event | category | flops | bytes accessed | tf_op | source)
XLA Modules:
  0.0 659.3 jit_solution(5534295072115211666)
XLA Ops:
  0.7 6.8 %concatenate.77 = bf16[416]{0:T(512)(128)(2,1)S(1)} concatenate(bf16[32]{0:T(256)(128)(2,1)} %param.26, bf16[32]{0:T(256)(128)(2,1)} %param.27, bf16[32]{0:T(256)(128)(2,1)} %param.28, bf16[32]{0:T(256)(128)(2,1)} %param.30, bf16[32]{0:T(256)(128)(2,1)} %param.31, bf16[32]{0:T(256)(128)(2,1)} %param.33, bf16[32]{0:T(256)(128)(2,1)} %param.34, bf16[32]{0:T(256)(128)(2,1)} %param.35, ...), dimensions={0} | concatenate | bytes 1664 | tf_op jit(solution)/shard_map/concatenate | solution.py:829
  8.8 2.9 collective-permute-start.1
  13.3 2.1 collective-permute-start.2
  21.1 6.6 collective-permute-done.23
  30.1 6.7 %collective-permute-done.3 = bf16[8,416]{1,0:T(8,128)(2,1)S(1)} collective-permute-done((bf16[8,416]{1,0:T(8,128)(2,1)S(1)}, bf16[8,416]{1,0:T(8,128)(2,1)S(1)}, u32[]{:S(2)}, u32[]{:S(2)}) %collective-permute-start.3) | collective-permute-done | bytes 6688 | tf_op jit(solution)/shard_map/ppermute | solution.py:42
  36.8 2.6 collective-permute-start.24
  40.7 3.5 collective-permute-done.24
  49.4 1.9 collective-permute-start.15
  53.0 2.9 collective-permute-start.42
  57.0 16.5 %collective-permute-done.15 = bf16[2,32,3072]{2,1,0:T(8,128)(2,1)S(1)} collective-permute-done((bf16[2,32,3072]{2,1,0:T(8,128)(2,1)S(1)}, bf16[2,32,3072]{2,1,0:T(8,128)(2,1)S(1)}, u32[]{:S(2)}, u32[]{:S(2)}) %collective-permute-start.15) | collective-permute-done | bytes 393248 | tf_op jit(solution)/shard_map/ppermute | solution.py:42
  76.0 12.7 %collective-permute-start.8 = (bf16[4,64,1024]{2,1,0:T(8,128)(2,1)S(1)}, bf16[4,64,1024]{2,1,0:T(8,128)(2,1)}, u32[]{:S(2)}, u32[]{:S(2)}) collective-permute-start(bf16[4,64,1024]{2,1,0:T(8,128)(2,1)S(1)} %pad_maximum_fusion.3.rest_0_), channel_id=1, source_target_pairs={{0,4},{1,3},{2,6},{3,1},{4,0},{5,7},{6,2},{7,5},{8,12},{9,11},{10,... | collective-permute-start | bytes 1572872 | tf_op jit(solution)/shard_map/ppermute | solution.py:42
  88.7 29.3 %collective-permute-done.42 = bf16[2,128,1024]{2,1,0:T(8,128)(2,1)S(1)} collective-permute-done((bf16[2,128,1024]{2,1,0:T(8,128)(2,1)S(1)}, bf16[2,128,1024]{2,1,0:T(8,128)(2,1)S(1)}, u32[]{:S(2)}, u32[]{:S(2)}) %collective-permute-start.42) | collective-permute-done | bytes 524320 | tf_op jit(solution)/shard_map/ppermute | solution.py:42
  124.4 6.6 collective-permute-done.17.rest_2_
  134.5 6.2 collective-permute-done.9.rest_3_
  146.4 8.5 %collective-permute-done.34.rest_9_.rest_1_ = bf16[4,32,4096]{2,1,0:T(8,128)(2,1)} collective-permute-done((bf16[4,32,4096]{2,1,0:T(8,128)(2,1)S(1)}, bf16[4,32,4096]{2,1,0:T(8,128)(2,1)}, u32[]{:S(2)}, u32[]{:S(2)}) %collective-permute-start.34) | collective-permute-done | bytes 1048608 | tf_op jit(solution)/shard_map/ppermute | solution.py:42
  164.3 11.2 %skip_forward.1 = (f32[1024,1024]{1,0:T(8,128)}, bf16[1024,1024]{1,0:T(8,128)(2,1)}) custom-call(s32[1]{0:T(128)} %bitcast.me_ref, bf16[1024,1024]{1,0:T(8,128)(2,1)} %rest_0_.1, bf16[1024,1024]{1,0:T(8,128)(2,1)} %rest_1_.2, f32[1,1024]{1,0:T(1,128)} %reshape.152.bias, f32[1,1024]{1,0:T(1,128)} %reshape.153.gain, f32[1,1024]{1,0:T(1,128)} %reshape.154.shift, ...), custom_call_target="tpu_custom_call" | custom-call | flops 4294967296 | bytes 14680064 | tf_op jit(solution)/shard_map/skip_forward/pallas_call | solution.py:250
  176.2 12.8 %qkv_forward.1.q.k.v = bf16[1024,3072]{1,0:T(8,128)(2,1)} custom-call(s32[1]{0:T(128)} %bitcast.me_ref, bf16[1024,1024]{1,0:T(8,128)(2,1)} %get-tuple-element.57.normed.rest_0_, f32[1,3072]{1,0:T(1,128)} %pad_maximum_fusion.10.bias, bf16[4,32,3072]{2,1,0:T(8,128)(2,1)} %copy-done.11, bf16[4,32,3072]{2,1,0:T(8,128)(2,1)} %collective-permute-done.16.rest_1_, ...), custom_call_target="tpu_custom_call" | custom-call | flops 6442450944 | bytes 14680064 | tf_op jit(solution)/shard_map/qkv_forward/pallas_call | solution.py:282
  192.3 38.8 %attend.1 = (bf16[1024,1024]{1,0:T(8,128)(2,1)}, f32[1024,128]{1,0:T(8,128)}) custom-call(bf16[1024,3072]{1,0:T(8,128)(2,1)} %qkv_forward.1.q.k.v, bf16[1024,3072]{1,0:T(8,128)(2,1)} %qkv_forward.1.q.k.v, bf16[1024,3072]{1,0:T(8,128)(2,1)} %qkv_forward.1.q.k.v, s32[1024,1]{1,0:T(8,128)} %fusion.tag_q, s32[1,1024]{1,0:T(1,128)} %bitcast.63), custom_call_target="tpu_custom_call" | custom-call | flops 17179869184 | bytes 8388608 | tf_op jit(solution)/shard_map/attend/pallas_call | solution.py:704
  233.5 30.8 %up_forward.1 = (f32[1024,1024]{1,0:T(8,128)}, bf16[1024,1024]{1,0:T(8,128)(2,1)}, bf16[1024,4096]{1,0:T(8,128)(2,1)}, bf16[1024,4096]{1,0:T(8,128)(2,1)}) custom-call(s32[1]{0:T(128)} %bitcast.me_ref, f32[1024,1024]{1,0:T(8,128)} %get-tuple-element.56.first, bf16[1024,1024]{1,0:T(8,128)(2,1)} %get-tuple-element.58.mixed.o.rest_0_, ...), custom_call_target="tpu_custom_call" | custom-call | flops 10737418240 | bytes 39845888 | tf_op jit(solution)/shard_map/up_forward/pallas_call | solution.py:342
  264.3 15.4 %grad_down.1 = (bf16[16,128,1024]{2,1,0:T(8,128)(2,1)}, bf16[16,128,1024]{2,1,0:T(8,128)(2,1)}) custom-call(s32[1]{0:T(128)} %bitcast.me_ref, bf16[1024,4096]{1,0:T(8,128)(2,1)} %get-tuple-element.60.act.rest_0_, bf16[1024,1024]{1,0:T(8,128)(2,1)} %rest_1_.3), custom_call_target="tpu_custom_call" | custom-call | flops 8589934592 | bytes 18874368 | tf_op jit(solution)/shard_map/grad_down/pallas_call | solution.py:486
  280.7 30.8 %down_both.1 = (bf16[1024,1024]{1,0:T(8,128)(2,1)}, bf16[1024,4096]{1,0:T(8,128)(2,1)}, f32[1,4096]{1,0:T(1,128)}, f32[1,1024]{1,0:T(1,128)}) custom-call(s32[1]{0:T(128)} %bitcast.me_ref, f32[1024,1024]{1,0:T(8,128)} %get-tuple-element.59.second, bf16[1024,4096]{1,0:T(8,128)(2,1)} %get-tuple-element.60.act.rest_0_, ...), custom_call_target="tpu_custom_call" | custom-call | flops 17179869184 | bytes 41943040 | tf_op jit(solution)/shard_map/down_both/pallas_call | solution.py:390
  311.5 22.4 %second_back.1 = (f32[1024,1024]{1,0:T(8,128)}, bf16[1024,1024]{1,0:T(8,128)(2,1)}, bf16[1024,1024]{1,0:T(8,128)(2,1)}, f32[1,1024]{1,0:T(1,128)}, f32[1,1024]{1,0:T(1,128)}, /*index=5*/f32[1,1024]{1,0:T(1,128)}) custom-call(s32[1]{0:T(128)} %bitcast.me_ref, bf16[1024,4096]{1,0:T(8,128)(2,1)} %get-tuple-element.63.gh.rest_1_, ...), custom_call_target="tpu_custom_call" | custom-call | flops 10737418240 | bytes 33554432 | tf_op jit(solution)/shard_map/second_back/pallas_call | solution.py:548
  333.9 53.1 %attend_back.1 = (bf16[1024,1024]{1,0:T(8,128)(2,1)}, bf16[1024,1024]{1,0:T(8,128)(2,1)}, bf16[1024,1024]{1,0:T(8,128)(2,1)}) custom-call(bf16[1024,3072]{1,0:T(8,128)(2,1)} %qkv_forward.1.q.k.v, bf16[1024,3072]{1,0:T(8,128)(2,1)} %qkv_forward.1.q.k.v, bf16[1024,3072]{1,0:T(8,128)(2,1)} %qkv_forward.1.q.k.v, bf16[1024,1024]{1,0:T(8,128)(2,1)} %get-tuple-element.64.g, ...), custom_call_target="tpu_custom_call" | custom-call | flops 42949672960 | bytes 16777216 | tf_op jit(solution)/shard_map/attend_back/pallas_call | solution.py:786
  387.0 1.9 constant_dynamic-update-slice_fusion.2
  391.0 2.6 copy-done.13
  393.6 12.3 %grad_qkv.1 = (bf16[16,32,3072]{2,1,0:T(8,128)(2,1)}, bf16[16,32,3072]{2,1,0:T(8,128)(2,1)}) custom-call(s32[1]{0:T(128)} %bitcast.me_ref, bf16[1024,1024]{1,0:T(8,128)(2,1)} %get-tuple-element.57.normed.rest_0_, bf16[1024,3072]{1,0:T(8,128)(2,1)} %copy-done.13), custom_call_target="tpu_custom_call" | custom-call | flops 6442450944 | bytes 14680064 | tf_op jit(solution)/shard_map/grad_qkv/pallas_call | solution.py:486
  406.0 17.7 %first_back.1 = (bf16[1024,1024]{1,0:T(8,128)(2,1)}, f32[1,1024]{1,0:T(1,128)}, f32[1,1024]{1,0:T(1,128)}, f32[1,1024]{1,0:T(1,128)}, f32[1,3072]{1,0:T(1,128)}) custom-call(s32[1]{0:T(128)} %bitcast.me_ref, bf16[1024,3072]{1,0:T(8,128)(2,1)} %copy-done.13, f32[1024,1024]{1,0:T(8,128)} %get-tuple-element.56.first, f32[1024,1024]{1,0:T(8,128)} %get-tuple-element.69.gsec, ...), custom_call_target="tpu_custom_call" | custom-call | flops 6442450944 | bytes 23068672 | tf_op jit(solution)/shard_map/first_back/pallas_call | solution.py:600
  432.5 9.1 %grad_skip.1 = (bf16[16,64,1024]{2,1,0:T(8,128)(2,1)}, bf16[16,64,1024]{2,1,0:T(8,128)(2,1)}) custom-call(s32[1]{0:T(128)} %bitcast.me_ref, bf16[1024,1024]{1,0:T(8,128)(2,1)} %rest_0_.1, bf16[1024,1024]{1,0:T(8,128)(2,1)} %rest_1_.2, bf16[1024,1024]{1,0:T(8,128)(2,1)} %get-tuple-element.70.gfirst.rest_2_), custom_call_target="tpu_custom_call" | custom-call | flops 4294967296 | bytes 10485760 | tf_op jit(solution)/shard_map/grad_skip/pallas_call | solution.py:486
  442.2 4.8 collective-permute-start.56
  447.0 5.9 grad_out.1
  454.3 15.4 %grad_up.1 = (bf16[16,32,4096]{2,1,0:T(8,128)(2,1)}, bf16[16,32,4096]{2,1,0:T(8,128)(2,1)}) custom-call(s32[1]{0:T(128)} %bitcast.me_ref, bf16[1024,1024]{1,0:T(8,128)(2,1)} %get-tuple-element.89.rest_0_, bf16[1024,4096]{1,0:T(8,128)(2,1)} %get-tuple-element.63.gh.rest_1_), custom_call_target="tpu_custom_call" | custom-call | flops 8589934592 | bytes 18874368 | tf_op jit(solution)/shard_map/grad_up/pallas_call | solution.py:486
  470.8 9.4 %joined_back.1 = (bf16[1024,1024]{1,0:T(8,128)(2,1)}, bf16[1024,1024]{1,0:T(8,128)(2,1)}) custom-call(s32[1]{0:T(128)} %bitcast.me_ref, bf16[1024,1024]{1,0:T(8,128)(2,1)} %get-tuple-element.70.gfirst.rest_2_, bf16[4,64,1024]{2,1,0:T(8,128)(2,1)} %copy-done.14, bf16[4,64,1024]{2,1,0:T(8,128)(2,1)} %copy-done.32, ...), custom_call_target="tpu_custom_call" | custom-call | flops 4294967296 | bytes 10485760 | tf_op jit(solution)/shard_map/joined_back/pallas_call | solution.py:638
  482.8 2.1 add_convert_fusion.5
  486.2 5.0 collective-permute-done.66
  494.2 7.3 %collective-permute-done.67 = bf16[4,32,1024]{2,1,0:T(8,128)(2,1)S(1)} collective-permute-done((bf16[4,32,1024]{2,1,0:T(8,128)(2,1)S(1)}, bf16[4,32,1024]{2,1,0:T(8,128)(2,1)S(1)}, u32[]{:S(2)}, u32[]{:S(2)}) %collective-permute-start.67) | collective-permute-done | bytes 262176 | tf_op jit(solution)/shard_map/ppermute | solution.py:42
  502.8 2.4 collective-permute-done.51
  511.9 9.4 %collective-permute-done.52 = bf16[4,64,1024]{2,1,0:T(8,128)(2,1)S(1)} collective-permute-done((bf16[4,64,1024]{2,1,0:T(8,128)(2,1)S(1)}, bf16[4,64,1024]{2,1,0:T(8,128)(2,1)S(1)}, u32[]{:S(2)}, u32[]{:S(2)}) %collective-permute-start.52) | collective-permute-done | bytes 524320 | tf_op jit(solution)/shard_map/ppermute | solution.py:42
  524.5 6.7 %collective-permute-done.61 = bf16[8,32,3072]{2,1,0:T(8,128)(2,1)S(1)} collective-permute-done((bf16[8,32,3072]{2,1,0:T(8,128)(2,1)S(1)}, bf16[8,32,3072]{2,1,0:T(8,128)(2,1)S(1)}, u32[]{:S(2)}, u32[]{:S(2)}) %collective-permute-start.61) | collective-permute-done | bytes 1572896 | tf_op jit(solution)/shard_map/ppermute | solution.py:42
  537.5 14.6 %collective-permute-done.62 = bf16[4,32,3072]{2,1,0:T(8,128)(2,1)S(1)} collective-permute-done((bf16[4,32,3072]{2,1,0:T(8,128)(2,1)S(1)}, bf16[4,32,3072]{2,1,0:T(8,128)(2,1)S(1)}, u32[]{:S(2)}, u32[]{:S(2)}) %collective-permute-start.62) | collective-permute-done | bytes 786464 | tf_op jit(solution)/shard_map/ppermute | solution.py:42
  552.5 9.6 %collective-permute-done.71 = bf16[8,32,4096]{2,1,0:T(8,128)(2,1)S(1)} collective-permute-done((bf16[8,32,4096]{2,1,0:T(8,128)(2,1)S(1)}, bf16[8,32,4096]{2,1,0:T(8,128)(2,1)S(1)}, u32[]{:S(2)}, u32[]{:S(2)}) %collective-permute-start.71) | collective-permute-done | bytes 2097184 | tf_op jit(solution)/shard_map/ppermute | solution.py:42
  564.0 1.7 add_bitcast_fusion.3
  565.7 7.0 %collective-permute-done.63 = bf16[2,32,3072]{2,1,0:T(8,128)(2,1)S(1)} collective-permute-done((bf16[2,32,3072]{2,1,0:T(8,128)(2,1)S(1)}, bf16[2,32,3072]{2,1,0:T(8,128)(2,1)S(1)}, u32[]{:S(2)}, u32[]{:S(2)}) %collective-permute-start.63) | collective-permute-done | bytes 393248 | tf_op jit(solution)/shard_map/ppermute | solution.py:42
  572.9 22.9 %collective-permute-done.76 = bf16[8,128,1024]{2,1,0:T(8,128)(2,1)S(1)} collective-permute-done((bf16[8,128,1024]{2,1,0:T(8,128)(2,1)S(1)}, bf16[8,128,1024]{2,1,0:T(8,128)(2,1)S(1)}, u32[]{:S(2)}, u32[]{:S(2)}) %collective-permute-start.76) | collective-permute-done | bytes 2097184 | tf_op jit(solution)/shard_map/ppermute | solution.py:42
  599.2 12.1 %collective-permute-done.77 = bf16[4,128,1024]{2,1,0:T(8,128)(2,1)S(1)} collective-permute-done((bf16[4,128,1024]{2,1,0:T(8,128)(2,1)S(1)}, bf16[4,128,1024]{2,1,0:T(8,128)(2,1)S(1)}, u32[]{:S(2)}, u32[]{:S(2)}) %collective-permute-start.77) | collective-permute-done | bytes 1048608 | tf_op jit(solution)/shard_map/ppermute | solution.py:42
  611.9 23.5 %collective-permute-done.73 = bf16[2,32,4096]{2,1,0:T(8,128)(2,1)S(1)} collective-permute-done((bf16[2,32,4096]{2,1,0:T(8,128)(2,1)S(1)}, bf16[2,32,4096]{2,1,0:T(8,128)(2,1)S(1)}, u32[]{:S(2)}, u32[]{:S(2)}) %collective-permute-start.73) | collective-permute-done | bytes 524320 | tf_op jit(solution)/shard_map/ppermute | solution.py:42
  635.6 11.0 %collective-permute-done.78 = bf16[2,128,1024]{2,1,0:T(8,128)(2,1)S(1)} collective-permute-done((bf16[2,128,1024]{2,1,0:T(8,128)(2,1)S(1)}, bf16[2,128,1024]{2,1,0:T(8,128)(2,1)S(1)}, u32[]{:S(2)}, u32[]{:S(2)}) %collective-permute-start.78) | collective-permute-done | bytes 524320 | tf_op jit(solution)/shard_map/ppermute | solution.py:42
  647.0 5.3 collective-permute-done.74
  653.2 4.5 collective-permute-done.79
  (312 shorter events, 101.7 us)
Async XLA Ops:
  15.4 24.0 %collective-permute-start.5 = (bf16[1,64,1024]{2,1,0:T(8,128)(2,1)}, bf16[1,64,1024]{2,1,0:T(8,128)(2,1)S(1)}, u32[]{:S(2)}, u32[]{:S(2)}) collective-permute-start(bf16[1,64,1024]{2,1,0:T(8,128)(2,1)} %bitcast.53), channel_id=1, source_target_pairs={{0,8},{1,9},{2,10},{3,11},{4,12},{5,13},{6,14},{7,15},{8,0},{9,1},... | collective-permute-start | bytes 393224 | tf_op jit(solution)/shard_map/ppermute | solution.py:42
  17.0 29.2 %collective-permute-start.14 = (bf16[1,32,3072]{2,1,0:T(8,128)(2,1)}, bf16[1,32,3072]{2,1,0:T(8,128)(2,1)S(1)}, u32[]{:S(2)}, u32[]{:S(2)}) collective-permute-start(bf16[1,32,3072]{2,1,0:T(8,128)(2,1)} %bitcast.50), channel_id=1, source_target_pairs={{0,8},{1,9},{2,10},{3,11},{4,12},{5,13},{6,14},{7,15},{8,0},{9,1},... | collective-permute-start | bytes 589832 | tf_op jit(solution)/shard_map/ppermute | solution.py:42
  19.0 30.4 %collective-permute-start.32 = (bf16[1,32,4096]{2,1,0:T(8,128)(2,1)}, bf16[1,32,4096]{2,1,0:T(8,128)(2,1)S(1)}, u32[]{:S(2)}, u32[]{:S(2)}) collective-permute-start(bf16[1,32,4096]{2,1,0:T(8,128)(2,1)} %bitcast.44), channel_id=1, source_target_pairs={{0,8},{1,9},{2,10},{3,11},{4,12},{5,13},{6,14},{7,15},{8,0},{9,1},... | collective-permute-start | bytes 786440 | tf_op jit(solution)/shard_map/ppermute | solution.py:42
  19.5 30.0 %collective-permute-start.41 = (bf16[1,128,1024]{2,1,0:T(8,128)(2,1)}, bf16[1,128,1024]{2,1,0:T(8,128)(2,1)S(1)}, u32[]{:S(2)}, u32[]{:S(2)}) collective-permute-start(bf16[1,128,1024]{2,1,0:T(8,128)(2,1)} %bitcast.47), channel_id=1, source_target_pairs={{0,8},{1,9},{2,10},{3,11},{4,12},{5,13},{6,14},{7,15},{8,0},{9,1},... | collective-permute-start | bytes 786440 | tf_op jit(solution)/shard_map/ppermute | solution.py:42
  49.4 24.1 %collective-permute-start.15 = (bf16[2,32,3072]{2,1,0:T(8,128)(2,1)S(1)}, bf16[2,32,3072]{2,1,0:T(8,128)(2,1)S(1)}, u32[]{:S(2)}, u32[]{:S(2)}) collective-permute-start(bf16[2,32,3072]{2,1,0:T(8,128)(2,1)S(1)} %pad_maximum_fusion.6), channel_id=1, source_target_pairs={{0,16},{1,17},{2,18},{3,19},{4,20},{5,21},{6,22},{7,23},{8,24},{9,... | collective-permute-start | bytes 1179656 | tf_op jit(solution)/shard_map/ppermute | solution.py:42
  53.0 35.7 %collective-permute-start.33 = (bf16[2,32,4096]{2,1,0:T(8,128)(2,1)S(1)}, bf16[2,32,4096]{2,1,0:T(8,128)(2,1)S(1)}, u32[]{:S(2)}, u32[]{:S(2)}) collective-permute-start(bf16[2,32,4096]{2,1,0:T(8,128)(2,1)S(1)} %pad_maximum_fusion.4), channel_id=1, source_target_pairs={{0,16},{1,17},{2,18},{3,19},{4,20},{5,21},{6,22},{7,23},{8,24},{9,... | collective-permute-start | bytes 1572872 | tf_op jit(solution)/shard_map/ppermute | solution.py:42
  53.0 65.0 %collective-permute-start.42 = (bf16[2,128,1024]{2,1,0:T(8,128)(2,1)S(1)}, bf16[2,128,1024]{2,1,0:T(8,128)(2,1)S(1)}, u32[]{:S(2)}, u32[]{:S(2)}) collective-permute-start(bf16[2,128,1024]{2,1,0:T(8,128)(2,1)S(1)} %pad_maximum_fusion.5), channel_id=1, source_target_pairs={{0,16},{1,17},{2,18},{3,19},{4,20},{5,21},{6,22},{7,23},{8,24},{9,... | collective-permute-start | bytes 1572872 | tf_op jit(solution)/shard_map/ppermute | solution.py:42
  56.0 17.7 %collective-permute-start.27 = (bf16[4,32,1024]{2,1,0:T(8,128)(2,1)S(1)}, bf16[4,32,1024]{2,1,0:T(8,128)(2,1)S(1)}, u32[]{:S(2)}, u32[]{:S(2)}) collective-permute-start(bf16[4,32,1024]{2,1,0:T(8,128)(2,1)S(1)} %collective-permute-done.25.rest_1_.rest_9_), channel_id=1, source_target_pairs={{0,4},{1,3},{2,6},{3,1},{4,0},{5,7},{6,2},{7,5},{8,12},{9,11},{10,... | collective-permute-start | bytes 786440 | tf_op jit(solution)/shard_map/ppermute | solution.py:42
  57.0 18.0 %collective-permute-start.29 = (bf16[4,32,1024]{2,1,0:T(8,128)(2,1)S(1)}, bf16[4,32,1024]{2,1,0:T(8,128)(2,1)S(1)}, u32[]{:S(2)}, u32[]{:S(2)}) collective-permute-start(bf16[4,32,1024]{2,1,0:T(8,128)(2,1)S(1)} %collective-permute-done.25.rest_1_.rest_9_), channel_id=1, source_target_pairs={{0,1},{1,0},{2,3},{3,2},{4,5},{5,4},{6,7},{7,6},{8,9},{9,8},{10,11... | collective-permute-start | bytes 786440 | tf_op jit(solution)/shard_map/ppermute | solution.py:42
  73.7 49.0 %collective-permute-start.16 = (bf16[4,32,3072]{2,1,0:T(8,128)(2,1)S(1)}, bf16[4,32,3072]{2,1,0:T(8,128)(2,1)}, u32[]{:S(2)}, u32[]{:S(2)}) collective-permute-start(bf16[4,32,3072]{2,1,0:T(8,128)(2,1)S(1)} %pad_maximum_fusion.2.rest_0_), channel_id=1, source_target_pairs={{0,2},{1,5},{2,0},{3,7},{4,6},{5,1},{6,4},{7,3},{8,10},{9,13},{10,... | collective-permute-start | bytes 2359304 | tf_op jit(solution)/shard_map/ppermute | solution.py:42
  75.0 46.0 %collective-permute-start.7 = (bf16[4,64,1024]{2,1,0:T(8,128)(2,1)S(1)}, bf16[4,64,1024]{2,1,0:T(8,128)(2,1)S(1)}, u32[]{:S(2)}, u32[]{:S(2)}) collective-permute-start(bf16[4,64,1024]{2,1,0:T(8,128)(2,1)S(1)} %pad_maximum_fusion.3.rest_0_), channel_id=1, source_target_pairs={{0,2},{1,5},{2,0},{3,7},{4,6},{5,1},{6,4},{7,3},{8,10},{9,13},{10,... | collective-permute-start | bytes 1572872 | tf_op jit(solution)/shard_map/ppermute | solution.py:42
  76.0 46.1 %collective-permute-start.8 = (bf16[4,64,1024]{2,1,0:T(8,128)(2,1)S(1)}, bf16[4,64,1024]{2,1,0:T(8,128)(2,1)}, u32[]{:S(2)}, u32[]{:S(2)}) collective-permute-start(bf16[4,64,1024]{2,1,0:T(8,128)(2,1)S(1)} %pad_maximum_fusion.3.rest_0_), channel_id=1, source_target_pairs={{0,4},{1,3},{2,6},{3,1},{4,0},{5,7},{6,2},{7,5},{8,12},{9,11},{10,... | collective-permute-start | bytes 1572872 | tf_op jit(solution)/shard_map/ppermute | solution.py:42
  88.7 34.0 %collective-permute-start.10 = (bf16[4,64,1024]{2,1,0:T(8,128)(2,1)S(1)}, bf16[4,64,1024]{2,1,0:T(8,128)(2,1)}, u32[]{:S(2)}, u32[]{:S(2)}) collective-permute-start(bf16[4,64,1024]{2,1,0:T(8,128)(2,1)S(1)} %pad_maximum_fusion.3.rest_0_), channel_id=1, source_target_pairs={{0,1},{1,0},{2,3},{3,2},{4,5},{5,4},{6,7},{7,6},{8,9},{9,8},{10,11... | collective-permute-start | bytes 1572872 | tf_op jit(solution)/shard_map/ppermute | solution.py:42
  122.1 18.5 %collective-permute-start.9 = (bf16[4,64,1024]{2,1,0:T(8,128)(2,1)}, bf16[4,64,1024]{2,1,0:T(8,128)(2,1)}, u32[]{:S(2)}, u32[]{:S(2)}) collective-permute-start(bf16[4,64,1024]{2,1,0:T(8,128)(2,1)} %copy-done.32), channel_id=1, source_target_pairs={{0,4},{1,3},{2,6},{3,1},{4,0},{5,7},{6,2},{7,5},{8,12},{9,11},{10,... | collective-permute-start | bytes 1572872 | tf_op jit(solution)/shard_map/ppermute | solution.py:42
  122.7 17.9 %collective-permute-start.11 = (bf16[4,64,1024]{2,1,0:T(8,128)(2,1)}, bf16[4,64,1024]{2,1,0:T(8,128)(2,1)S(1)}, u32[]{:S(2)}, u32[]{:S(2)}) collective-permute-start(bf16[4,64,1024]{2,1,0:T(8,128)(2,1)} %copy-done.32), channel_id=1, source_target_pairs={{0,1},{1,0},{2,3},{3,2},{4,5},{5,4},{6,7},{7,6},{8,9},{9,8},{10,11... | collective-permute-start | bytes 1572872 | tf_op jit(solution)/shard_map/ppermute | solution.py:42
  122.7 19.1 %collective-permute-start.12 = (bf16[4,64,1024]{2,1,0:T(8,128)(2,1)}, bf16[4,64,1024]{2,1,0:T(8,128)(2,1)S(1)}, u32[]{:S(2)}, u32[]{:S(2)}) collective-permute-start(bf16[4,64,1024]{2,1,0:T(8,128)(2,1)} %collective-permute-done.8.rest_2_), channel_id=1, source_target_pairs={{0,1},{1,0},{2,3},{3,2},{4,5},{5,4},{6,7},{7,6},{8,9},{9,8},{10,11... | collective-permute-start | bytes 1572872 | tf_op jit(solution)/shard_map/ppermute | solution.py:42
  131.0 24.0 %collective-permute-start.34 = (bf16[4,32,4096]{2,1,0:T(8,128)(2,1)S(1)}, bf16[4,32,4096]{2,1,0:T(8,128)(2,1)}, u32[]{:S(2)}, u32[]{:S(2)}) collective-permute-start(bf16[4,32,4096]{2,1,0:T(8,128)(2,1)S(1)} %pad_maximum_fusion.rest_8_.rest_0_), channel_id=1, source_target_pairs={{0,2},{1,5},{2,0},{3,7},{4,6},{5,1},{6,4},{7,3},{8,10},{9,13},{10,... | collective-permute-start | bytes 3145736 | tf_op jit(solution)/shard_map/ppermute | solution.py:42
  133.6 22.9 %collective-permute-start.18 = (bf16[4,32,3072]{2,1,0:T(8,128)(2,1)}, bf16[4,32,3072]{2,1,0:T(8,128)(2,1)}, u32[]{:S(2)}, u32[]{:S(2)}) collective-permute-start(bf16[4,32,3072]{2,1,0:T(8,128)(2,1)} %collective-permute-done.16.rest_1_), channel_id=1, source_target_pairs={{0,4},{1,3},{2,6},{3,1},{4,0},{5,7},{6,2},{7,5},{8,12},{9,11},{10,... | collective-permute-start | bytes 2359304 | tf_op jit(solution)/shard_map/ppermute | solution.py:42
  154.9 35.2 %collective-permute-start.35 = (bf16[4,32,4096]{2,1,0:T(8,128)(2,1)S(1)}, bf16[4,32,4096]{2,1,0:T(8,128)(2,1)}, u32[]{:S(2)}, u32[]{:S(2)}) collective-permute-start(bf16[4,32,4096]{2,1,0:T(8,128)(2,1)S(1)} %pad_maximum_fusion.rest_8_.rest_0_), channel_id=1, source_target_pairs={{0,4},{1,3},{2,6},{3,1},{4,0},{5,7},{6,2},{7,5},{8,12},{9,11},{10,... | collective-permute-start | bytes 3145736 | tf_op jit(solution)/shard_map/ppermute | solution.py:42
  156.4 33.8 %collective-permute-start.37 = (bf16[4,32,4096]{2,1,0:T(8,128)(2,1)S(1)}, bf16[4,32,4096]{2,1,0:T(8,128)(2,1)}, u32[]{:S(2)}, u32[]{:S(2)}) collective-permute-start(bf16[4,32,4096]{2,1,0:T(8,128)(2,1)S(1)} %pad_maximum_fusion.rest_8_.rest_0_), channel_id=1, source_target_pairs={{0,1},{1,0},{2,3},{3,2},{4,5},{5,4},{6,7},{7,6},{8,9},{9,8},{10,11... | collective-permute-start | bytes 3145736 | tf_op jit(solution)/shard_map/ppermute | solution.py:42
  156.4 34.2 %collective-permute-start.43 = (bf16[4,128,1024]{2,1,0:T(8,128)(2,1)S(1)}, bf16[4,128,1024]{2,1,0:T(8,128)(2,1)}, u32[]{:S(2)}, u32[]{:S(2)}) collective-permute-start(bf16[4,128,1024]{2,1,0:T(8,128)(2,1)S(1)} %pad_maximum_fusion.1.rest_0_), channel_id=1, source_target_pairs={{0,2},{1,5},{2,0},{3,7},{4,6},{5,1},{6,4},{7,3},{8,10},{9,13},{10,... | collective-permute-start | bytes 3145736 | tf_op jit(solution)/shard_map/ppermute | solution.py:42
  157.3 35.0 %collective-permute-start.36 = (bf16[4,32,4096]{2,1,0:T(8,128)(2,1)}, bf16[4,32,4096]{2,1,0:T(8,128)(2,1)}, u32[]{:S(2)}, u32[]{:S(2)}) collective-permute-start(bf16[4,32,4096]{2,1,0:T(8,128)(2,1)} %collective-permute-done.34.rest_9_.rest_1_), channel_id=1, source_target_pairs={{0,4},{1,3},{2,6},{3,1},{4,0},{5,7},{6,2},{7,5},{8,12},{9,11},{10,... | collective-permute-start | bytes 3145736 | tf_op jit(solution)/shard_map/ppermute | solution.py:42
  189.0 42.1 %collective-permute-start.44 = (bf16[4,128,1024]{2,1,0:T(8,128)(2,1)S(1)}, bf16[4,128,1024]{2,1,0:T(8,128)(2,1)S(1)}, u32[]{:S(2)}, u32[]{:S(2)}) collective-permute-start(bf16[4,128,1024]{2,1,0:T(8,128)(2,1)S(1)} %pad_maximum_fusion.1.rest_0_), channel_id=1, source_target_pairs={{0,4},{1,3},{2,6},{3,1},{4,0},{5,7},{6,2},{7,5},{8,12},{9,11},{10,... | collective-permute-start | bytes 3145736 | tf_op jit(solution)/shard_map/ppermute | solution.py:42
  190.1 41.6 %collective-permute-start.38 = (bf16[4,32,4096]{2,1,0:T(8,128)(2,1)}, bf16[4,32,4096]{2,1,0:T(8,128)(2,1)S(1)}, u32[]{:S(2)}, u32[]{:S(2)}) collective-permute-start(bf16[4,32,4096]{2,1,0:T(8,128)(2,1)} %collective-permute-done.34.rest_9_.rest_1_), channel_id=1, source_target_pairs={{0,1},{1,0},{2,3},{3,2},{4,5},{5,4},{6,7},{7,6},{8,9},{9,8},{10,11... | collective-permute-start | bytes 3145736 | tf_op jit(solution)/shard_map/ppermute | solution.py:42
  190.2 41.5 %collective-permute-start.39 = (bf16[4,32,4096]{2,1,0:T(8,128)(2,1)}, bf16[4,32,4096]{2,1,0:T(8,128)(2,1)S(1)}, u32[]{:S(2)}, u32[]{:S(2)}) collective-permute-start(bf16[4,32,4096]{2,1,0:T(8,128)(2,1)} %collective-permute-done.35.rest_10_.rest_2_), channel_id=1, source_target_pairs={{0,1},{1,0},{2,3},{3,2},{4,5},{5,4},{6,7},{7,6},{8,9},{9,8},{10,11... | collective-permute-start | bytes 3145736 | tf_op jit(solution)/shard_map/ppermute | solution.py:42
  190.6 41.6 %collective-permute-start.45 = (bf16[4,128,1024]{2,1,0:T(8,128)(2,1)}, bf16[4,128,1024]{2,1,0:T(8,128)(2,1)S(1)}, u32[]{:S(2)}, u32[]{:S(2)}) collective-permute-start(bf16[4,128,1024]{2,1,0:T(8,128)(2,1)} %collective-permute-done.43.rest_1_), channel_id=1, source_target_pairs={{0,4},{1,3},{2,6},{3,1},{4,0},{5,7},{6,2},{7,5},{8,12},{9,11},{10,... | collective-permute-start | bytes 3145736 | tf_op jit(solution)/shard_map/ppermute | solution.py:42
  192.3 40.0 %collective-permute-start.40 = (bf16[4,32,4096]{2,1,0:T(8,128)(2,1)}, bf16[4,32,4096]{2,1,0:T(8,128)(2,1)S(1)}, u32[]{:S(2)}, u32[]{:S(2)}) collective-permute-start(bf16[4,32,4096]{2,1,0:T(8,128)(2,1)} %collective-permute-done.36.rest_11_.rest_3_), channel_id=1, source_target_pairs={{0,1},{1,0},{2,3},{3,2},{4,5},{5,4},{6,7},{7,6},{8,9},{9,8},{10,11... | collective-permute-start | bytes 3145736 | tf_op jit(solution)/shard_map/ppermute | solution.py:42
  231.1 48.6 %collective-permute-start.46 = (bf16[4,128,1024]{2,1,0:T(8,128)(2,1)S(1)}, bf16[4,128,1024]{2,1,0:T(8,128)(2,1)S(1)}, u32[]{:S(2)}, u32[]{:S(2)}) collective-permute-start(bf16[4,128,1024]{2,1,0:T(8,128)(2,1)S(1)} %pad_maximum_fusion.1.rest_0_), channel_id=1, source_target_pairs={{0,1},{1,0},{2,3},{3,2},{4,5},{5,4},{6,7},{7,6},{8,9},{9,8},{10,11... | collective-permute-start | bytes 3145736 | tf_op jit(solution)/shard_map/ppermute | solution.py:42
  231.7 48.0 %collective-permute-start.47 = (bf16[4,128,1024]{2,1,0:T(8,128)(2,1)}, bf16[4,128,1024]{2,1,0:T(8,128)(2,1)}, u32[]{:S(2)}, u32[]{:S(2)}) collective-permute-start(bf16[4,128,1024]{2,1,0:T(8,128)(2,1)} %collective-permute-done.43.rest_1_), channel_id=1, source_target_pairs={{0,1},{1,0},{2,3},{3,2},{4,5},{5,4},{6,7},{7,6},{8,9},{9,8},{10,11... | collective-permute-start | bytes 3145736 | tf_op jit(solution)/shard_map/ppermute | solution.py:42
  231.8 47.9 %collective-permute-start.48 = (bf16[4,128,1024]{2,1,0:T(8,128)(2,1)S(1)}, bf16[4,128,1024]{2,1,0:T(8,128)(2,1)}, u32[]{:S(2)}, u32[]{:S(2)}) collective-permute-start(bf16[4,128,1024]{2,1,0:T(8,128)(2,1)S(1)} %collective-permute-done.44.rest_2_), channel_id=1, source_target_pairs={{0,1},{1,0},{2,3},{3,2},{4,5},{5,4},{6,7},{7,6},{8,9},{9,8},{10,11... | collective-permute-start | bytes 3145736 | tf_op jit(solution)/shard_map/ppermute | solution.py:42
  232.2 47.5 %collective-permute-start.49 = (bf16[4,128,1024]{2,1,0:T(8,128)(2,1)S(1)}, bf16[4,128,1024]{2,1,0:T(8,128)(2,1)}, u32[]{:S(2)}, u32[]{:S(2)}) collective-permute-start(bf16[4,128,1024]{2,1,0:T(8,128)(2,1)S(1)} %collective-permute-done.45.rest_3_), channel_id=1, source_target_pairs={{0,1},{1,0},{2,3},{3,2},{4,5},{5,4},{6,7},{7,6},{8,9},{9,8},{10,11... | collective-permute-start | bytes 3145736 | tf_op jit(solution)/shard_map/ppermute | solution.py:42
  441.6 41.2 %collective-permute-start.50 = (bf16[16,64,1024]{2,1,0:T(8,128)(2,1)}, bf16[16,64,1024]{2,1,0:T(8,128)(2,1)}, u32[]{:S(2)}, u32[]{:S(2)}) collective-permute-start(bf16[16,64,1024]{2,1,0:T(8,128)(2,1)} %get-tuple-element.74), channel_id=1, source_target_pairs={{0,1},{1,0},{2,3},{3,2},{4,5},{5,4},{6,7},{7,6},{8,9},{9,8},{10,11... | collective-permute-start | bytes 6291464 | tf_op jit(solution)/shard_map/ppermute | solution.py:42
  441.9 66.0 %collective-permute-start.60 = (bf16[16,32,3072]{2,1,0:T(8,128)(2,1)}, bf16[16,32,3072]{2,1,0:T(8,128)(2,1)S(1)}, u32[]{:S(2)}, u32[]{:S(2)}) collective-permute-start(bf16[16,32,3072]{2,1,0:T(8,128)(2,1)} %get-tuple-element.85), channel_id=1, source_target_pairs={{0,1},{1,0},{2,3},{3,2},{4,5},{5,4},{6,7},{7,6},{8,9},{9,8},{10,11... | collective-permute-start | bytes 9437192 | tf_op jit(solution)/shard_map/ppermute | solution.py:42
  452.9 27.5 %collective-permute-start.65 = (bf16[16,32,1024]{2,1,0:T(8,128)(2,1)}, bf16[16,32,1024]{2,1,0:T(8,128)(2,1)}, u32[]{:S(2)}, u32[]{:S(2)}) collective-permute-start(bf16[16,32,1024]{2,1,0:T(8,128)(2,1)} %get-tuple-element.88), channel_id=1, source_target_pairs={{0,1},{1,0},{2,3},{3,2},{4,5},{5,4},{6,7},{7,6},{8,9},{9,8},{10,11... | collective-permute-start | bytes 3145736 | tf_op jit(solution)/shard_map/ppermute | solution.py:42
  469.7 53.0 %collective-permute-start.70 = (bf16[16,32,4096]{2,1,0:T(8,128)(2,1)}, bf16[16,32,4096]{2,1,0:T(8,128)(2,1)S(1)}, u32[]{:S(2)}, u32[]{:S(2)}) collective-permute-start(bf16[16,32,4096]{2,1,0:T(8,128)(2,1)} %get-tuple-element.91), channel_id=1, source_target_pairs={{0,1},{1,0},{2,3},{3,2},{4,5},{5,4},{6,7},{7,6},{8,9},{9,8},{10,11... | collective-permute-start | bytes 12582920 | tf_op jit(solution)/shard_map/ppermute | solution.py:42
  480.3 55.4 %collective-permute-start.75 = (bf16[16,128,1024]{2,1,0:T(8,128)(2,1)}, bf16[16,128,1024]{2,1,0:T(8,128)(2,1)S(1)}, u32[]{:S(2)}, u32[]{:S(2)}) collective-permute-start(bf16[16,128,1024]{2,1,0:T(8,128)(2,1)} %get-tuple-element.93), channel_id=1, source_target_pairs={{0,1},{1,0},{2,3},{3,2},{4,5},{5,4},{6,7},{7,6},{8,9},{9,8},{10,11... | collective-permute-start | bytes 12582920 | tf_op jit(solution)/shard_map/ppermute | solution.py:42
  484.9 20.3 %collective-permute-start.51 = (bf16[8,64,1024]{2,1,0:T(8,128)(2,1)S(1)}, bf16[8,64,1024]{2,1,0:T(8,128)(2,1)S(1)}, u32[]{:S(2)}, u32[]{:S(2)}) collective-permute-start(bf16[8,64,1024]{2,1,0:T(8,128)(2,1)S(1)} %add_convert_fusion.5), channel_id=1, source_target_pairs={{0,4},{1,3},{2,6},{3,1},{4,0},{5,7},{6,2},{7,5},{8,12},{9,11},{10,... | collective-permute-start | bytes 3145736 | tf_op jit(solution)/shard_map/ppermute | solution.py:42
  508.5 22.8 %collective-permute-start.61 = (bf16[8,32,3072]{2,1,0:T(8,128)(2,1)S(1)}, bf16[8,32,3072]{2,1,0:T(8,128)(2,1)S(1)}, u32[]{:S(2)}, u32[]{:S(2)}) collective-permute-start(bf16[8,32,3072]{2,1,0:T(8,128)(2,1)S(1)} %add_convert_fusion.2), channel_id=1, source_target_pairs={{0,4},{1,3},{2,6},{3,1},{4,0},{5,7},{6,2},{7,5},{8,12},{9,11},{10,... | collective-permute-start | bytes 4718600 | tf_op jit(solution)/shard_map/ppermute | solution.py:42
  511.8 21.1 %collective-permute-start.69 = (bf16[1,32,1024]{2,1,0:T(8,128)(2,1)S(1)}, bf16[1,32,1024]{2,1,0:T(8,128)(2,1)S(1)}, u32[]{:S(2)}, u32[]{:S(2)}) collective-permute-start(bf16[1,32,1024]{2,1,0:T(8,128)(2,1)S(1)} %add_convert_fusion.19), channel_id=1, source_target_pairs={{0,8},{1,9},{2,10},{3,11},{4,12},{5,13},{6,14},{7,15},{8,0},{9,1},... | collective-permute-start | bytes 196616 | tf_op jit(solution)/shard_map/ppermute | solution.py:42
  523.6 38.6 %collective-permute-start.71 = (bf16[8,32,4096]{2,1,0:T(8,128)(2,1)S(1)}, bf16[8,32,4096]{2,1,0:T(8,128)(2,1)S(1)}, u32[]{:S(2)}, u32[]{:S(2)}) collective-permute-start(bf16[8,32,4096]{2,1,0:T(8,128)(2,1)S(1)} %add_convert_fusion.1), channel_id=1, source_target_pairs={{0,4},{1,3},{2,6},{3,1},{4,0},{5,7},{6,2},{7,5},{8,12},{9,11},{10,... | collective-permute-start | bytes 6291464 | tf_op jit(solution)/shard_map/ppermute | solution.py:42
  531.6 20.5 %collective-permute-start.62 = (bf16[4,32,3072]{2,1,0:T(8,128)(2,1)S(1)}, bf16[4,32,3072]{2,1,0:T(8,128)(2,1)S(1)}, u32[]{:S(2)}, u32[]{:S(2)}) collective-permute-start(bf16[4,32,3072]{2,1,0:T(8,128)(2,1)S(1)} %add_convert_fusion.6), channel_id=1, source_target_pairs={{0,2},{1,5},{2,0},{3,7},{4,6},{5,1},{6,4},{7,3},{8,10},{9,13},{10,... | collective-permute-start | bytes 2359304 | tf_op jit(solution)/shard_map/ppermute | solution.py:42
  535.5 28.5 %collective-permute-start.54 = (bf16[1,64,1024]{2,1,0:T(8,128)(2,1)S(1)}, bf16[1,64,1024]{2,1,0:T(8,128)(2,1)S(1)}, u32[]{:S(2)}, u32[]{:S(2)}) collective-permute-start(bf16[1,64,1024]{2,1,0:T(8,128)(2,1)S(1)} %add_convert_fusion.18), channel_id=1, source_target_pairs={{0,8},{1,9},{2,10},{3,11},{4,12},{5,13},{6,14},{7,15},{8,0},{9,1},... | collective-permute-start | bytes 393224 | tf_op jit(solution)/shard_map/ppermute | solution.py:42
  536.7 59.1 %collective-permute-start.76 = (bf16[8,128,1024]{2,1,0:T(8,128)(2,1)S(1)}, bf16[8,128,1024]{2,1,0:T(8,128)(2,1)S(1)}, u32[]{:S(2)}, u32[]{:S(2)}) collective-permute-start(bf16[8,128,1024]{2,1,0:T(8,128)(2,1)S(1)} %add_convert_fusion), channel_id=1, source_target_pairs={{0,4},{1,3},{2,6},{3,1},{4,0},{5,7},{6,2},{7,5},{8,12},{9,11},{10,... | collective-permute-start | bytes 6291464 | tf_op jit(solution)/shard_map/ppermute | solution.py:42
  552.4 20.4 %collective-permute-start.63 = (bf16[2,32,3072]{2,1,0:T(8,128)(2,1)S(1)}, bf16[2,32,3072]{2,1,0:T(8,128)(2,1)S(1)}, u32[]{:S(2)}, u32[]{:S(2)}) collective-permute-start(bf16[2,32,3072]{2,1,0:T(8,128)(2,1)S(1)} %add_convert_fusion.11), channel_id=1, source_target_pairs={{0,16},{1,17},{2,18},{3,19},{4,20},{5,21},{6,22},{7,23},{8,24},{9,... | collective-permute-start | bytes 1179656 | tf_op jit(solution)/shard_map/ppermute | solution.py:42
  562.6 35.2 %collective-permute-start.72 = (bf16[4,32,4096]{2,1,0:T(8,128)(2,1)S(1)}, bf16[4,32,4096]{2,1,0:T(8,128)(2,1)S(1)}, u32[]{:S(2)}, u32[]{:S(2)}) collective-permute-start(bf16[4,32,4096]{2,1,0:T(8,128)(2,1)S(1)} %add_convert_fusion.4), channel_id=1, source_target_pairs={{0,2},{1,5},{2,0},{3,7},{4,6},{5,1},{6,4},{7,3},{8,10},{9,13},{10,... | collective-permute-start | bytes 3145736 | tf_op jit(solution)/shard_map/ppermute | solution.py:42
  572.8 25.5 %collective-permute-start.64 = (bf16[1,32,3072]{2,1,0:T(8,128)(2,1)S(1)}, bf16[1,32,3072]{2,1,0:T(8,128)(2,1)S(1)}, u32[]{:S(2)}, u32[]{:S(2)}) collective-permute-start(bf16[1,32,3072]{2,1,0:T(8,128)(2,1)S(1)} %add_convert_fusion.16), channel_id=1, source_target_pairs={{0,8},{1,9},{2,10},{3,11},{4,12},{5,13},{6,14},{7,15},{8,0},{9,1},... | collective-permute-start | bytes 589832 | tf_op jit(solution)/shard_map/ppermute | solution.py:42
  598.1 37.2 %collective-permute-start.73 = (bf16[2,32,4096]{2,1,0:T(8,128)(2,1)S(1)}, bf16[2,32,4096]{2,1,0:T(8,128)(2,1)S(1)}, u32[]{:S(2)}, u32[]{:S(2)}) collective-permute-start(bf16[2,32,4096]{2,1,0:T(8,128)(2,1)S(1)} %add_convert_fusion.8), channel_id=1, source_target_pairs={{0,16},{1,17},{2,18},{3,19},{4,20},{5,21},{6,22},{7,23},{8,24},{9,... | collective-permute-start | bytes 1572872 | tf_op jit(solution)/shard_map/ppermute | solution.py:42
  611.7 34.9 %collective-permute-start.78 = (bf16[2,128,1024]{2,1,0:T(8,128)(2,1)S(1)}, bf16[2,128,1024]{2,1,0:T(8,128)(2,1)S(1)}, u32[]{:S(2)}, u32[]{:S(2)}) collective-permute-start(bf16[2,128,1024]{2,1,0:T(8,128)(2,1)S(1)} %add_convert_fusion.7), channel_id=1, source_target_pairs={{0,16},{1,17},{2,18},{3,19},{4,20},{5,21},{6,22},{7,23},{8,24},{9,... | collective-permute-start | bytes 1572872 | tf_op jit(solution)/shard_map/ppermute | solution.py:42
  (76 other events, 1496.6 us)

commit v2 on v1

v2 whole, which is shorter than its diff:
```python
import functools
import math

import jax
import jax.numpy as jnp
from jax import lax
from jax.experimental import pallas as pl
from jax.experimental.pallas import tpu as pltpu
from jax.sharding import PartitionSpec as P

HEADS = 16
EPSILON = 1e-05
FAR = 1e32
AXES = ("wide", "narrow")
BF = jnp.bfloat16
F32 = jnp.float32
VMEM_LIMIT = 36 * 1024 * 1024

ANY = pl.BlockSpec(memory_space=pl.ANY)
SMEM = pl.BlockSpec(memory_space=pltpu.SMEM)


def params():
    return pltpu.CompilerParams(vmem_limit_bytes=VMEM_LIMIT)


def cost(flops, nbytes, trans=0):
    return pl.CostEstimate(flops=int(flops), bytes_accessed=int(nbytes), transcendentals=int(trans))


class Net:
    def __init__(self, size, rows_min, vec_rows):
        self.size = size
        self.bits = size.bit_length() - 1
        self.high = self.bits - 3
        self.groups = 1 << self.high
        self.fast = size == 1 << self.bits and self.bits >= 3 and rows_min % 16 == 0 and vec_rows == (32, 128)
        self.shards = size if self.fast else 1

    def pp(self, x, mask):
        if not self.fast:
            return x
        pairs = [(d, d ^ mask(d & 1)) for d in range(self.size)]
        return lax.ppermute(x, AXES, pairs)


def first_bit(core):
    return 2 + 2 * core


def second_bit(core):
    return 4 - 2 * core


def other_core(core):
    return 1


def piece_masks(core):
    a, b = first_bit(core), second_bit(core)
    return [0, a, b, 6, 1, 1 ^ b, 1 ^ a, 7]


def bar(*values):
    return lax.optimization_barrier(values)


class Flow:
    def __init__(self, net):
        self.net, self.data = net, {}

    def end(self, values, *prefixes):
        names = [n for n in self.data if n.startswith(prefixes)] if prefixes else []
        values, arrays = bar(values, [self.data[n] for n in names])
        self.data.update(zip(names, arrays))
        return values

    def send(self, name, x, mask):
        self.data[name] = self.net.pp(x, mask)

    def own(self, p, shard):
        if self.net.fast:
            self.data[p + "z0"] = shard
        else:
            self.data[p + "m0"] = lax.all_gather(shard, AXES, axis=0, tiled=True)

    def z(self, p, *steps):
        if self.net.fast:
            for j in steps:
                self.send(f"{p}z{j}", self.data[p + "z0"], lambda c, j=j: j << 3)

    def near(self, p):
        if not self.net.fast:
            return
        block = jnp.stack([self.data.pop(f"{p}z{j}") for j in range(self.net.groups)])
        self.data[p + "m0"] = block
        self.send(p + "m1", block, first_bit)
        self.send(p + "m2", block, second_bit)

    def far(self, p):
        if self.net.fast:
            self.send(p + "m3", self.data[p + "m1"], second_bit)

    def core(self, p, *which):
        if self.net.fast:
            for i in which:
                self.send(f"{p}o{i}", self.data[f"{p}m{i}"], other_core)

    def pieces(self, p):
        if not self.net.fast:
            return [self.data.pop(p + "m0")]
        return [self.data.pop(p + k + str(i)) for k in "mo" for i in range(4)]


BSKIP, GAIN1, SHIFT1, BQUERY, BVALUE, BOUT, GAIN2, SHIFT2, BDOWN = range(9)


def packed_vectors(vectors, wide, rows):
    narrow = jnp.pad(jnp.stack(vectors), ((0, 0), (0, 128 - vectors[0].shape[0])))
    return jnp.pad(
        jnp.concatenate([narrow, wide.reshape(1, 128)], axis=0),
        ((0, rows - len(vectors) - 1), (0, 0)),
    )


def unpack_kernel(net, col, me_ref, *rest):
    pieces, (rows_ref, wide_ref, held, sems) = rest[:8], rest[8:]
    me = me_ref[0]
    masks = piece_masks(me & 1)
    copies = []
    for i, piece in enumerate(pieces):
        for j in range(net.groups):
            source = me ^ (masks[i] ^ (j << 3))
            copies.append(
                pltpu.make_async_copy(
                    piece.at[j, pl.ds(0, 16), pl.ds(col, 128)], held.at[source], sems.at[len(copies)]
                )
            )
    for copy in copies:
        copy.start()
    for copy in copies:
        copy.wait()
    for d in range(0, net.size, 4):
        tile = held[d].astype(F32)
        for k in range(1, 4):
            tile = tile + pltpu.roll(held[d + k].astype(F32), 32 * k, 1)
        rows_ref[:, 32 * d : 32 * d + 128] = tile
    for d in range(net.size):
        wide_ref[:, 128 * d : 128 * d + 128] = held[d].astype(F32)[9:10, :]


def unpack_vectors(net, me, pieces, col):
    return pl.pallas_call(
        functools.partial(unpack_kernel, net, col),
        in_specs=[SMEM] + [ANY] * len(pieces),
        out_shape=[
            jax.ShapeDtypeStruct((16, 32 * net.size), F32),
            jax.ShapeDtypeStruct((1, 128 * net.size), F32),
        ],
        scratch_shapes=[pltpu.VMEM((net.size, 16, 128), BF), pltpu.SemaphoreType.DMA((net.size,))],
        compiler_params=params(),
        cost_estimate=cost(1000, 200000),
        name="unpack_vectors",
    )(me, *pieces)


def sum_vectors(net, rows, start, stop):
    if not net.fast:
        return rows if start else lax.psum(rows, AXES)
    for bit in range(start, stop):
        rows = rows + net.pp(rows, lambda c: 1 << bit)
    return rows


class Scatter:
    def __init__(self, net, parts):
        self.net, self.keep, self.got = net, parts[0], []
        self.send = parts[-1]

    def summed(self, lo, hi, cols=slice(None)):
        total = self.keep[lo:hi, :, cols].astype(F32)
        for arr in self.got:
            total = total + arr[lo:hi, :, cols].astype(F32)
        return total

    def core(self):
        if not self.net.fast:
            total = self.keep[0].astype(F32)
            return lax.psum_scatter(total, AXES, scatter_dimension=0, tiled=True)
        return self.net.pp(self.send, other_core)

    def next(self, got, mask, lo):
        self.got.append(got)
        if not self.net.fast:
            return got
        return self.net.pp(self.summed(lo, 2 * lo).astype(BF), mask)

    def b(self, got):
        return self.next(got, second_bit, 2 * self.net.groups)

    def a(self, got):
        return self.next(got, first_bit, self.net.groups)

    def z(self, got):
        self.got.append(got)
        if not self.net.fast:
            return [got]
        return [
            self.net.pp(self.summed(j, j + 1)[0].astype(BF), lambda c, j=j: j << 3)
            for j in range(1, self.net.groups)
        ]

    def done(self, last, cols=slice(None)):
        if not self.net.fast:
            return last[0][:, cols]
        total = self.summed(0, 1, cols)[0]
        for arr in last:
            total = total + arr[:, cols].astype(F32)
        return total


def load_start(net, me, pieces, dst, sems, which=0, col=0):
    copies = []
    if not net.fast:
        copies.append(pltpu.make_async_copy(pieces[which], dst, sems.at[0]))
    else:
        masks = piece_masks(me & 1)
        rows, cols = dst.shape[0] // net.size, dst.shape[1]
        for i, piece in enumerate(pieces):
            for j in range(net.groups):
                source = me ^ (masks[i] ^ (j << 3))
                at = pl.multiple_of(source * rows, rows)
                copies.append(
                    pltpu.make_async_copy(
                        piece.at[j, :, pl.ds(col, cols)],
                        dst.at[pl.ds(at, rows), :],
                        sems.at[len(copies)],
                    )
                )
    for copy in copies:
        copy.start()
    return copies


def relative(net, rel, core):
    bit_one, bit_two, group = (rel >> 1) & 1, (rel >> 2) & 1, rel >> 3
    top = jnp.where(core == 0, bit_two, bit_one)
    low = jnp.where(core == 0, bit_one, bit_two)
    return (top << (net.high + 1)) | (low << net.high) | group


def store_copies(net, me, src, base, rows, total_rows, outs, col, sems, first_sem):
    cols = pl.ds(col, src.shape[1])
    if not net.fast:
        rows = pl.ds(base, rows)
        return [
            pltpu.make_async_copy(
                src.at[rows, :], outs[0].at[0, rows, cols], sems.at[first_sem]
            )
        ]
    copies = []
    shard = total_rows // net.size
    core = me & 1
    for i in range(0, rows // shard, 2):
        even = base // shard + i
        for k, out in enumerate(outs):
            owner_core = core if k == 0 else 1 - core
            target = even | owner_core
            rel = (me if k == 0 else me ^ 1) ^ target
            at = pl.multiple_of(target * shard, shard)
            copies.append(
                pltpu.make_async_copy(
                    src.at[pl.ds(at, shard), :],
                    out.at[relative(net, rel, owner_core), :, cols],
                    sems.at[first_sem + i + k],
                )
            )
    return copies


def dot(a, b):
    return jnp.dot(a, b, preferred_element_type=F32)


def dot_t(a, b):
    return lax.dot_general(a, b, (((1,), (1,)), ((), ())), preferred_element_type=F32)


def norm_parts(x):
    center = x - jnp.mean(x, axis=1, keepdims=True)
    spread = jnp.mean(center * center, axis=1, keepdims=True)
    rstd = lax.rsqrt(spread + EPSILON)
    return center * rstd, rstd


def sums(x):
    return jnp.sum(x, axis=0, keepdims=True)


def add_to(ref, value, step):
    @pl.when(step == 0)
    def _():
        ref[...] = value

    @pl.when(step > 0)
    def _():
        ref[...] += value


def row_block(tok):
    return min(512, tok)


def weight_scratch(net, *shapes):
    out = []
    for shape in shapes:
        out += [pltpu.VMEM(shape, BF), pltpu.SemaphoreType.DMA((net.shards,))]
    return out


def n_pieces(net, whole=1):
    return 8 if net.fast else whole


def skip_kernel(net, me_ref, frames, skip, *rest):
    np_ = n_pieces(net)
    pieces, (raw_ref, w, sems) = rest[:np_], rest[np_:]

    @pl.when(pl.program_id(0) == 0)
    def _():
        for copy in load_start(net, me_ref[0], pieces, w, sems):
            copy.wait()

    width = frames.shape[1]
    raw_ref[...] = dot(frames[...], w[:width, :]) + dot(skip[...], w[width:, :])


def skip_forward(net, me, frames, skip, pieces):
    tok, width = frames.shape
    blk = row_block(tok)
    rows = pl.BlockSpec((blk, width), lambda i: (i, 0))
    return pl.pallas_call(
        functools.partial(skip_kernel, net),
        grid=(tok // blk,),
        in_specs=[SMEM, rows, rows] + [ANY] * len(pieces),
        out_specs=rows,
        out_shape=jax.ShapeDtypeStruct((tok, width), F32),
        scratch_shapes=weight_scratch(net, (2 * width, width)),
        compiler_params=params(),
        cost_estimate=cost(4 * tok * width * width, tok * width * 8 + 4 * width * width),
        name="skip_forward",
    )(me, frames, skip, *pieces)


def vec_row(vecs, k):
    return vecs[k : k + 1, :]


def qkv_kernel(net, me_ref, raw, vecs, *rest):
    np_ = n_pieces(net)
    pieces, (normed_ref, out_ref, w, sems) = rest[:np_], rest[np_:]

    @pl.when(pl.program_id(0) == 0)
    def _():
        copies = load_start(net, me_ref[0], pieces, w, sems)
        for copy in copies:
            copy.wait()

    xhat, _ = norm_parts(raw[...] + vec_row(vecs, BSKIP))
    normed = (xhat * vec_row(vecs, GAIN1) + vec_row(vecs, SHIFT1)).astype(BF)
    normed_ref[...] = normed
    width = raw.shape[1]
    out_ref[:, :width] = (dot(normed, w[:, :width]) + vec_row(vecs, BQUERY)).astype(BF)
    out_ref[:, width : 2 * width] = dot(normed, w[:, width : 2 * width]).astype(BF)
    out_ref[:, 2 * width :] = (dot(normed, w[:, 2 * width :]) + vec_row(vecs, BVALUE)).astype(BF)


def qkv_forward(net, me, raw, vecs, pieces):
    tok, width = raw.shape
    cols = 3 * width
    blk = row_block(tok)
    return pl.pallas_call(
        functools.partial(qkv_kernel, net),
        grid=(tok // blk,),
        in_specs=[
            SMEM,
            pl.BlockSpec((blk, width), lambda i: (i, 0)),
            pl.BlockSpec((16, width), lambda i: (0, 0)),
        ]
        + [ANY] * len(pieces),
        out_specs=[
            pl.BlockSpec((blk, width), lambda i: (i, 0)),
            pl.BlockSpec((blk, cols), lambda i: (i, 0)),
        ],
        out_shape=[jax.ShapeDtypeStruct((tok, width), BF), jax.ShapeDtypeStruct((tok, cols), BF)],
        scratch_shapes=weight_scratch(net, (width, cols)),
        compiler_params=params(),
        cost_estimate=cost(2 * tok * width * cols, tok * width * 12 + 6 * width * width),
        name="qkv_forward",
    )(me, raw, vecs, *pieces)


def gelu_both(v):
    lead, cubic = 0.7978845608, 0.7978845608 * 0.044715
    square = v * v
    half = 0.5 + 0.5 * jnp.tanh(v * (lead + cubic * square))
    slope = half + (half - half * half) * (v * (2 * lead + (6 * cubic) * square))
    return v * half, slope


def up_kernel(net, me_ref, raw, mixed, vecs, b_up, *rest):
    np_ = n_pieces(net, 2)
    pieces, rest = rest[:np_], rest[np_:]
    second_ref, normed_ref, act_ref, pull_ref, w_out, sems_out, w_up, sems_up = rest

    @pl.when(pl.program_id(0) == 0)
    def _():
        copies = load_start(net, me_ref[0], pieces, w_out, sems_out, 0, 0)
        copies += load_start(net, me_ref[0], pieces, w_up, sems_up, 1, w_out.shape[1])
        for copy in copies:
            copy.wait()

    bias = vec_row(vecs, BSKIP) + vec_row(vecs, BOUT)
    second = raw[...] + dot(mixed[...], w_out[...]) + bias
    second_ref[...] = second
    xhat, _ = norm_parts(second)
    normed = (xhat * vec_row(vecs, GAIN2) + vec_row(vecs, SHIFT2)).astype(BF)
    normed_ref[...] = normed
    chunk = 1024
    for at in range(0, w_up.shape[1], chunk):
        part = slice(at, at + chunk)
        hidden = dot(normed, w_up[:, part]) + b_up[:, part]
        act, pull = gelu_both(hidden)
        act_ref[:, part] = act.astype(BF)
        pull_ref[:, part] = pull.astype(BF)


def up_forward(net, me, raw, mixed, pieces, vecs, b_up):
    tok, width = raw.shape
    ff = b_up.shape[1]
    blk = min(256, tok)
    rows = pl.BlockSpec((blk, width), lambda i: (i, 0))
    wide = pl.BlockSpec((blk, ff), lambda i: (i, 0))
    vec = pl.BlockSpec((16, width), lambda i: (0, 0))
    vec_ff = pl.BlockSpec((1, ff), lambda i: (0, 0))
    return pl.pallas_call(
        functools.partial(up_kernel, net),
        grid=(tok // blk,),
        in_specs=[SMEM, rows, rows, vec, vec_ff] + [ANY] * len(pieces),
        out_specs=[rows, rows, wide, wide],
        out_shape=[
            jax.ShapeDtypeStruct((tok, width), F32),
            jax.ShapeDtypeStruct((tok, width), BF),
            jax.ShapeDtypeStruct((tok, ff), BF),
            jax.ShapeDtypeStruct((tok, ff), BF),
        ],
        scratch_shapes=weight_scratch(net, (width, width), (width, ff)),
        compiler_params=params(),
        cost_estimate=cost(
            2 * tok * width * (width + ff), tok * (width * 12 + ff * 4) + 2 * width * (width + ff)
        ),
        name="up_forward",
    )(me, raw, mixed, vecs, b_up, *pieces)


def down_kernel(net, me_ref, second, act, vecs, *rest):
    pieces, (out_ref, w, sems) = rest[: n_pieces(net)], rest[-3:]

    @pl.when(pl.program_id(0) == 0)
    def _():
        for copy in load_start(net, me_ref[0], pieces, w, sems):
            copy.wait()

    out_ref[...] = (second[...] + dot(act[...], w[...]) + vec_row(vecs, BDOWN)).astype(BF)


def down_forward(net, me, second, act, pieces, vecs, part, parts, before=()):
    tok, width = second.shape
    ff = act.shape[1]
    blk = min(256, tok)
    steps = tok // blk // parts
    start = part * steps
    rows = pl.BlockSpec((blk, width), lambda i: (start + i, 0))
    wide = pl.BlockSpec((blk, ff), lambda i: (start + i, 0))
    vec = pl.BlockSpec((16, width), lambda i: (0, 0))
    return pl.pallas_call(
        functools.partial(down_kernel, net),
        grid=(steps,),
        in_specs=[SMEM, rows, wide, vec] + [ANY] * (len(pieces) + len(before)),
        out_specs=rows,
        out_shape=jax.ShapeDtypeStruct((tok, width), BF),
        input_output_aliases={4 + len(pieces): 0} if before else {},
        scratch_shapes=weight_scratch(net, (ff, width)),
        compiler_params=params(),
        cost_estimate=cost(
            2 * tok * width * ff // parts, tok * (width * 6 + ff * 2) // parts + 2 * width * ff
        ),
        name="down_forward",
    )(me, second, act, vecs, *pieces, *before)


def hidden_kernel(net, me_ref, pull, cot, *rest):
    np_ = n_pieces(net)
    pieces, (gh_ref, bsum_ref, csum_ref, w, sems) = rest[:np_], rest[np_:]
    step = pl.program_id(0)

    @pl.when(step == 0)
    def _():
        for copy in load_start(net, me_ref[0], pieces, w, sems):
            copy.wait()

    chunk = 1024
    for at in range(0, w.shape[0], chunk):
        part = slice(at, at + chunk)
        gh = (dot_t(cot[...], w[part, :]) * pull[:, part].astype(F32)).astype(BF)
        gh_ref[:, part] = gh
        add_to(bsum_ref.at[:, part], sums(gh.astype(F32)), step)
    add_to(csum_ref, sums(cot[...].astype(F32)), step)


def hidden_back(net, me, pull, cot, pieces):
    tok, width = cot.shape
    ff = pull.shape[1]
    blk = row_block(tok)
    rows = pl.BlockSpec((blk, width), lambda i: (i, 0))
    wide = pl.BlockSpec((blk, ff), lambda i: (i, 0))
    vec = pl.BlockSpec((1, width), lambda i: (0, 0))
    vec_ff = pl.BlockSpec((1, ff), lambda i: (0, 0))
    return pl.pallas_call(
        functools.partial(hidden_kernel, net),
        grid=(tok // blk,),
        in_specs=[SMEM, wide, rows] + [ANY] * len(pieces),
        out_specs=[wide, vec_ff, vec],
        out_shape=[
            jax.ShapeDtypeStruct((tok, ff), BF),
            jax.ShapeDtypeStruct((1, ff), F32),
            jax.ShapeDtypeStruct((1, width), F32),
        ],
        scratch_shapes=weight_scratch(net, (ff, width)),
        compiler_params=params(),
        cost_estimate=cost(2 * tok * width * ff, tok * (width * 2 + ff * 4) + 2 * width * ff),
        name="hidden_back",
    )(me, pull, cot, *pieces)


def grad_kernel(net, lefts, rights, blk, col, outs_n, into_n, me_ref, *rest):
    left_refs, right_refs = rest[:lefts], rest[lefts : lefts + rights]
    rest = rest[lefts + rights + into_n :]
    outs, (acc, sems) = rest[:outs_n], rest[outs_n:]
    step = pl.program_id(0)
    total, cols = acc.shape
    steps = total // blk
    per_left = steps // lefts
    per_step = sems.shape[0] // steps
    for s in range(steps):

        @pl.when(step == s)
        def _():
            left = left_refs[s // per_left][...].T
            at = 0
            for right in right_refs:
                chunk = min(1024, right.shape[1])
                for i in range(0, right.shape[1], chunk):
                    acc[s * blk : (s + 1) * blk, at : at + chunk] = dot(
                        left, right[:, i : i + chunk]
                    ).astype(BF)
                    at += chunk
            for copy in store_copies(
                net, me_ref[0], acc, s * blk, blk, total, outs, col, sems, s * per_step
            ):
                copy.start()

    @pl.when(step == steps - 1)
    def _():
        for s in range(steps):
            for copy in store_copies(
                net, me_ref[0], acc, s * blk, blk, total, outs, col, sems, s * per_step
            ):
                copy.wait()


def weight_grad(net, me, lefts, rights, name, into=(), col=0, all_cols=0):
    tok = lefts[0].shape[0]
    cols = sum(right.shape[1] for right in rights)
    each = lefts[0].shape[1]
    total = each * len(lefts)
    blk = min(512, each)
    per_left = each // blk
    steps = total // blk
    all_cols = all_cols or cols
    if net.fast:
        per_step = blk // (total // net.size)
        shapes = [jax.ShapeDtypeStruct((net.size // 2, total // net.size, all_cols), BF)] * 2
    else:
        per_step = 1
        shapes = [jax.ShapeDtypeStruct((1, total, all_cols), BF)]

    def index(k):
        return lambda i: (0, jnp.clip(i - k * per_left, 0, per_left - 1))

    first_into = 1 + len(lefts) + len(rights)
    return pl.pallas_call(
        functools.partial(
            grad_kernel, net, len(lefts), len(rights), blk, col, len(shapes), len(into)
        ),
        grid=(steps,),
        in_specs=[SMEM]
        + [pl.BlockSpec((tok, blk), index(k)) for k in range(len(lefts))]
        + [
            pl.BlockSpec(right.shape, lambda i: (0, 0), pipeline_mode=pl.Buffered(1))
            for right in rights
        ]
        + [ANY] * len(into),
        out_specs=[ANY] * len(shapes),
        out_shape=shapes,
        input_output_aliases={first_into + k: k for k in range(len(into))},
        scratch_shapes=[
            pltpu.VMEM((total, cols), BF),
            pltpu.SemaphoreType.DMA((steps * per_step,)),
        ],
        compiler_params=params(),
        cost_estimate=cost(
            2 * tok * total * cols, 2 * tok * (total + cols) + 2 * total * cols
        ),
        name=name,
    )(me, *lefts, *rights, *into)


def norm_back(dn, x, gain):
    xhat, rstd = norm_parts(x)
    scaled = dn * gain
    mean_one = jnp.mean(scaled, axis=1, keepdims=True)
    mean_two = jnp.mean(scaled * xhat, axis=1, keepdims=True)
    return (scaled - mean_one - xhat * mean_two) * rstd, dn * xhat


def second_kernel(net, me_ref, gh, second, cot, vecs, *rest):
    np_ = n_pieces(net, 2)
    pieces, rest = rest[:np_], rest[np_:]
    gsec_ref, gattn_ref, gmix_ref, ggain_ref, gshift_ref, gbout_ref = rest[:6]
    w_up, sems_up, w_out, sems_out = rest[6:]
    step = pl.program_id(0)

    @pl.when(step == 0)
    def _():
        copies = load_start(net, me_ref[0], pieces, w_up, sems_up, 1, w_out.shape[1])
        copies += load_start(net, me_ref[0], pieces, w_out, sems_out, 0, 0)
        for copy in copies:
            copy.wait()

    dn = dot_t(gh[...], w_up[...])
    pulled, dx = norm_back(dn, second[...], vec_row(vecs, GAIN2))
    gsec = cot[...].astype(F32) + pulled
    gsec_ref[...] = gsec
    gattn = gsec.astype(BF)
    gattn_ref[...] = gattn
    gmix_ref[...] = dot_t(gattn, w_out[...]).astype(BF)
    add_to(ggain_ref, sums(dx), step)
    add_to(gshift_ref, sums(dn), step)
    add_to(gbout_ref, sums(gattn.astype(F32)), step)


def second_back(net, me, gh, second, cot, pieces, vecs):
    tok, width = second.shape
    ff = gh.shape[1]
    blk = min(256, tok)
    rows = pl.BlockSpec((blk, width), lambda i: (i, 0))
    wide = pl.BlockSpec((blk, ff), lambda i: (i, 0))
    vec = pl.BlockSpec((1, width), lambda i: (0, 0))
    vec_shape = jax.ShapeDtypeStruct((1, width), F32)
    return pl.pallas_call(
        functools.partial(second_kernel, net),
        grid=(tok // blk,),
        in_specs=[SMEM, wide, rows, rows, pl.BlockSpec((16, width), lambda i: (0, 0))]
        + [ANY] * len(pieces),
        out_specs=[rows, rows, rows, vec, vec, vec],
        out_shape=[
            jax.ShapeDtypeStruct((tok, width), F32),
            jax.ShapeDtypeStruct((tok, width), BF),
            jax.ShapeDtypeStruct((tok, width), BF),
            vec_shape,
            vec_shape,
            vec_shape,
        ],
        scratch_shapes=weight_scratch(net, (width, ff), (width, width)),
        compiler_params=params(),
        cost_estimate=cost(
            2 * tok * width * (width + ff), tok * (width * 14 + ff * 2) + 2 * width * (width + ff)
        ),
        name="second_back",
    )(me, gh, second, cot, vecs, *pieces)


def first_kernel(net, me_ref, gq, gk, gv, raw, gsec, vecs, *rest):
    np_ = n_pieces(net)
    pieces, rest = rest[:np_], rest[np_:]
    gfirst_ref, ggain_ref, gshift_ref, gbskip_ref, gbq_ref, gbv_ref, w, sems = rest
    step = pl.program_id(0)

    @pl.when(step == 0)
    def _():
        for copy in load_start(net, me_ref[0], pieces, w, sems):
            copy.wait()

    width = gq.shape[1]
    dn = dot_t(gq[...], w[:, :width])
    dn = dn + dot_t(gk[...], w[:, width : 2 * width])
    dn = dn + dot_t(gv[...], w[:, 2 * width :])
    pulled, dx = norm_back(dn, raw[...] + vec_row(vecs, BSKIP), vec_row(vecs, GAIN1))
    gfirst = (gsec[...] + pulled).astype(BF)
    gfirst_ref[...] = gfirst
    add_to(ggain_ref, sums(dx), step)
    add_to(gshift_ref, sums(dn), step)
    add_to(gbskip_ref, sums(gfirst.astype(F32)), step)
    add_to(gbq_ref, sums(gq[...].astype(F32)), step)
    add_to(gbv_ref, sums(gv[...].astype(F32)), step)


def first_back(net, me, gq, gk, gv, raw, gsec, pieces, vecs):
    tok, width = raw.shape
    blk = min(256, tok)
    rows = pl.BlockSpec((blk, width), lambda i: (i, 0))
    vec = pl.BlockSpec((1, width), lambda i: (0, 0))
    vec_shape = jax.ShapeDtypeStruct((1, width), F32)
    return pl.pallas_call(
        functools.partial(first_kernel, net),
        grid=(tok // blk,),
        in_specs=[SMEM, rows, rows, rows, rows, rows, pl.BlockSpec((16, width), lambda i: (0, 0))]
        + [ANY] * len(pieces),
        out_specs=[rows] + [vec] * 5,
        out_shape=[jax.ShapeDtypeStruct((tok, width), BF)] + [vec_shape] * 5,
        scratch_shapes=weight_scratch(net, (width, 3 * width)),
        compiler_params=params(),
        cost_estimate=cost(6 * tok * width * width, tok * width * 16 + 6 * width * width),
        name="first_back",
    )(me, gq, gk, gv, raw, gsec, vecs, *pieces)


def joined_kernel(net, me_ref, gfirst, *rest):
    np_ = n_pieces(net)
    pieces, (gframes_ref, gskip_ref, w, sems) = rest[:np_], rest[np_:]

    @pl.when(pl.program_id(0) == 0)
    def _():
        for copy in load_start(net, me_ref[0], pieces, w, sems):
            copy.wait()

    width = gframes_ref.shape[1]
    gframes_ref[...] = dot_t(gfirst[...], w[:width, :]).astype(BF)
    gskip_ref[...] = dot_t(gfirst[...], w[width:, :]).astype(BF)


def joined_back(net, me, gfirst, pieces):
    tok, width = gfirst.shape
    blk = row_block(tok)
    rows = pl.BlockSpec((blk, width), lambda i: (i, 0))
    out = jax.ShapeDtypeStruct((tok, width), BF)
    return pl.pallas_call(
        functools.partial(joined_kernel, net),
        grid=(tok // blk,),
        in_specs=[SMEM, rows] + [ANY] * len(pieces),
        out_specs=[rows, rows],
        out_shape=[out, out],
        scratch_shapes=weight_scratch(net, (2 * width, width)),
        compiler_params=params(),
        cost_estimate=cost(4 * tok * width * width, tok * width * 6 + 4 * width * width),
        name="joined_back",
    )(me, gfirst, *pieces)


def far_apart(row_tag, col_tag, row_at):
    shape = (row_tag.shape[0], col_tag.shape[1])
    i = row_at + lax.broadcasted_iota(jnp.int32, shape, 0)
    j = lax.broadcasted_iota(jnp.int32, shape, 1)
    ok = (row_tag == col_tag) | (i == j)
    return jnp.where(ok, jnp.abs(i - j).astype(F32), FAR)


def head_slope(head):
    return jnp.exp2((jnp.full((1, 1), head, jnp.int32).astype(F32) + 1.0) * (-8.0 / HEADS))


def far_kernel(blk, tag_q, tag_k, out_ref):
    out_ref[...] = far_apart(tag_q[...], tag_k[...], pl.program_id(0) * blk)


def far_matrix(row_tag, col_tag):
    tok = row_tag.shape[0]
    blk = min(256, tok)
    return pl.pallas_call(
        functools.partial(far_kernel, blk),
        grid=(tok // blk,),
        in_specs=[pl.BlockSpec((blk, 1), lambda i: (i, 0)), pl.BlockSpec((1, tok), lambda i: (0, 0))],
        out_specs=pl.BlockSpec((blk, tok), lambda i: (i, 0)),
        out_shape=jax.ShapeDtypeStruct((tok, tok), F32),
        compiler_params=params(),
        cost_estimate=cost(8 * tok * tok, 4 * tok * tok),
        name="far_matrix",
    )(row_tag.reshape(tok, 1), col_tag.reshape(1, tok))


def attend_kernel(size, blk, first_pair, q, k, v, far, *rest):
    out_ref, lse_ref, columns = rest[-3:]
    pair = first_pair + pl.program_id(0)
    tok = q.shape[0]
    lane = lax.broadcasted_iota(jnp.int32, (1, 2 * size), 1)
    scale = size**-0.5
    for i in range(tok // blk):
        at = slice(i * blk, (i + 1) * blk)
        q_blk = q[at, :] * scale
        outs, lse = [], []
        for h in range(2):
            mine = (lane >= h * size) & (lane < (h + 1) * size)
            scores = dot_t(jnp.where(mine, q_blk, 0), k[...]) - head_slope(2 * pair + h) * far[at, :]
            top = jnp.max(scores, axis=1, keepdims=True)
            expo = jnp.exp(scores - top)
            denom = jnp.sum(expo, axis=1, keepdims=True)
            outs.append(dot(expo.astype(BF), v[...]) / denom)
            lse.append(top + jnp.log(denom))
        out_ref[at, :] = jnp.where(lane < size, outs[0], outs[1]).astype(BF)
        columns[at, :] = jnp.where(lane < size, lse[0], lse[1])
    rows = columns[...].T
    lse_ref[0, 0:1, :] = rows[0:1, :]
    lse_ref[0, 1:2, :] = rows[size : size + 1, :]


def attend(qkv, far, heads, part, parts, before=()):
    tok = qkv.shape[0]
    width = qkv.shape[1] // 3
    size = width // heads
    pairs = heads // 2
    here = pairs // parts
    start = part * here
    blk = min(256, tok)

    def cols(k):
        return pl.BlockSpec((tok, 2 * size), lambda p: (0, k * pairs + start + p))

    return pl.pallas_call(
        functools.partial(attend_kernel, size, blk, start),
        grid=(here,),
        in_specs=[
            cols(0),
            cols(1),
            cols(2),
            pl.BlockSpec((tok, tok), lambda p: (0, 0), pipeline_mode=pl.Buffered(1)),
        ]
        + [ANY] * len(before),
        out_specs=[cols(0), pl.BlockSpec((1, 8, tok), lambda p: (start + p, 0, 0))],
        out_shape=[
            jax.ShapeDtypeStruct((tok, width), BF),
            jax.ShapeDtypeStruct((pairs, 8, tok), F32),
        ],
        input_output_aliases={4 + k: k for k in range(len(before))},
        scratch_shapes=[pltpu.VMEM((tok, 2 * size), F32)],
        compiler_params=params(),
        cost_estimate=cost(
            16 * here * 2 * tok * tok * size, tok * width * 8 // parts, here * 2 * tok * tok
        ),
        name="attend",
    )(qkv, qkv, qkv, far, *before)


def attend_back_kernel(size, blk, first_pair, q, k, v, g, o, lse, far, *rest):
    gq_ref, gk_ref, gv_ref = rest[-3:]
    pair = first_pair + pl.program_id(0)
    tok = q.shape[0]
    lane = lax.broadcasted_iota(jnp.int32, (1, 2 * size), 1)
    scale = size**-0.5
    q_all = q[...] * scale
    g_all = g[...]
    products = (g_all.astype(F32) * o[...].astype(F32)).T
    k_t = (k[...] * scale).astype(F32).T.astype(BF)
    grads_q = []
    for h in range(2):
        mine = (lane >= h * size) & (lane < (h + 1) * size)
        q_h = jnp.where(mine, q_all, 0)
        g_h = jnp.where(mine, g_all, 0)
        delta = jnp.sum(products[h * size : (h + 1) * size, :], axis=0, keepdims=True)
        norm = lse[0, h : h + 1, :]
        slope = head_slope(2 * pair + h)
        grad_q = jnp.zeros((size, tok), F32)
        for i in range(tok // blk):
            at = slice(i * blk, (i + 1) * blk)
            scores = dot_t(k[at, :], q_h) - slope * far[at, :]
            probs = jnp.exp(scores - norm)
            pulled = dot_t(v[at, :], g_h)
            ds = (probs * (pulled - delta)).astype(BF)
            gv = dot(probs.astype(BF), g_all)
            gk = dot(ds, q_all)
            grad_q = grad_q + dot(k_t[h * size : (h + 1) * size, at], ds)
            if h == 0:
                gv_ref[at, :] = gv.astype(BF)
                gk_ref[at, :] = gk.astype(BF)
            else:
                gv_ref[at, :] = jnp.where(mine, gv.astype(BF), gv_ref[at, :])
                gk_ref[at, :] = jnp.where(mine, gk.astype(BF), gk_ref[at, :])
        grads_q.append(grad_q)
    gq_ref[...] = jnp.concatenate(grads_q, axis=0).T.astype(BF)


def attend_back(qkv, grad_mixed, mixed, lse, far, heads, part, parts, before=()):
    tok = qkv.shape[0]
    width = qkv.shape[1] // 3
    size = width // heads
    pairs = heads // 2
    here = pairs // parts
    start = part * here
    blk = min(256, tok)

    def cols(k):
        return pl.BlockSpec((tok, 2 * size), lambda p: (0, k * pairs + start + p))

    out = jax.ShapeDtypeStruct((tok, width), BF)
    return pl.pallas_call(
        functools.partial(attend_back_kernel, size, blk, start),
        grid=(here,),
        in_specs=[
            cols(0),
            cols(1),
            cols(2),
            cols(0),
            cols(0),
            pl.BlockSpec((1, 8, tok), lambda p: (start + p, 0, 0)),
            pl.BlockSpec((tok, tok), lambda p: (0, 0), pipeline_mode=pl.Buffered(1)),
        ]
        + [ANY] * len(before),
        out_specs=[cols(0)] * 3,
        out_shape=[out] * 3,
        input_output_aliases={7 + k: k for k in range(len(before))},
        compiler_params=params(),
        cost_estimate=cost(
            40 * here * 2 * tok * tok * size, tok * width * 16 // parts, here * 2 * tok * tok
        ),
        name="attend_back",
    )(qkv, qkv, qkv, grad_mixed, mixed, lse, far, *before)


def tags(length_row, mask_row, tok):
    order = jnp.arange(length_row.shape[0])
    ends = jnp.sum(jnp.where(order[:, None] <= order[None, :], length_row[:, None], 0), axis=0)
    slots = jnp.arange(tok, dtype=jnp.int32)
    segment = jnp.sum((slots[:, None] >= ends[None, :]).astype(jnp.int32), axis=1)
    used = slots < jnp.sum(length_row)
    return jnp.where(used, segment, -1), jnp.where(used & (mask_row == 1), segment, -2)


def body(size, frames, skip, lengths, key_mask, cotangent, *weights):
    (
        w_skip, b_skip, pre_attn_gain, pre_attn_bias, w_qkv, b_query, b_value, w_out, b_out,
        pre_ffn_gain, pre_ffn_bias, w_up, b_up, w_down, b_down,
    ) = weights
    tok, width = frames.shape
    net = Net(
        size,
        min(w.shape[0] for w in (w_skip, w_qkv, w_out, w_up, w_down)),
        (b_skip.shape[0], b_up.shape[0]),
    )
    index = lax.axis_index(AXES).astype(jnp.int32)
    me = index.reshape(1)
    narrow = (
        b_skip, pre_attn_gain, pre_attn_bias, b_query, b_value, b_out, pre_ffn_gain, pre_ffn_bias, b_down,
    )

    def stacked(arrays):
        return jnp.stack(arrays) if net.fast else arrays[0]

    flow = Flow(net)
    flow.own("s", w_skip)
    flow.z("s", 1, 2, 3)
    w_two, w_three = w_qkv, [w_out, w_up]
    if net.fast:
        w_two = jnp.concatenate([w_qkv, packed_vectors(narrow, b_up, w_qkv.shape[0])], axis=1)
        w_three = [jnp.concatenate(w_three, axis=1)]
    w_two, w_three, w_down = flow.end((w_two, w_three, w_down), "s")
    flow.own("q", w_two)
    flow.own("u", w_three[-1])
    flow.own("o", w_three[0])
    flow.own("d", w_down)
    flow.near("s")
    flow.z("q", 1, 2)
    tag_q, tag_k = tags(lengths[0], key_mask, tok)
    tag_q, tag_k = flow.end((tag_q, tag_k), "s", "q")
    flow.far("s")
    flow.core("s", 0, 1)
    flow.z("q", 3)
    far = far_matrix(tag_q, tag_k)
    far, tag_q = flow.end((far, tag_q), "s", "q", "u")
    flow.core("s", 2, 3)
    flow.near("q")
    flow.z("u", 2)
    far_t = far_matrix(tag_k, tag_q)
    frames, far_t = flow.end((frames, far_t), "s")
    pieces_s = flow.pieces("s")
    raw = skip_forward(net, me, frames, skip, pieces_s)
    raw = flow.end(raw, "q", "u")
    flow.far("q")
    flow.core("q", 0)
    flow.z("u", 1, 3)
    raw = flow.end(raw, "q")
    flow.core("q", 1, 2, 3)
    raw = flow.end(raw, "q", "u")
    flow.near("u")
    pieces_q = flow.pieces("q")
    if net.fast:
        vecs, bup = unpack_vectors(net, me, pieces_q, 3 * width)
    else:
        every = [lax.all_gather(v, AXES, axis=0, tiled=True).astype(F32) for v in (*narrow, b_up)]
        vecs, bup = jnp.pad(jnp.stack(every[:-1]), ((0, 16 - len(narrow)), (0, 0))), every[-1][None]
    normed, qkv = qkv_forward(net, me, raw, vecs, pieces_q)
    qkv = flow.end(qkv, "d")
    flow.z("d", 1, 2)
    attended = attend(qkv, far, HEADS, 0, 2)
    attended = flow.end(attended, "u", "d")
    flow.far("u")
    flow.core("u", 0, 1, 2)
    flow.z("d", 3)
    attended = attend(qkv, far, HEADS, 1, 2, attended)
    attended = flow.end(attended, "u", "d")
    flow.core("u", 3)
    attended = flow.end(attended, "u", "d")
    flow.near("d")
    mixed, lse = attended
    pieces_u = ([] if net.fast else flow.pieces("o")) + flow.pieces("u")
    second, normed2, act, pull = up_forward(net, me, raw, mixed, pieces_u, vecs, bup)
    act = flow.end(act, "d")
    flow.far("d")
    flow.core("d", 0, 1, 2)
    down = Scatter(net, weight_grad(net, me, [act], [cotangent], "grad_down"))
    down.keep, down.send = flow.end((down.keep, down.send), "d")
    flow.core("d", 3)
    pieces_d = flow.pieces("d")

    down.keep, down.send, pieces_d = bar(down.keep, down.send, pieces_d)
    down_got = down.core()
    gh, gbup, gbdown = hidden_back(net, me, pull, cotangent, pieces_d)
    gh, down_got = bar(gh, down_got)
    down_got = down.b(down_got)
    up_cols = 4 * width + width if net.fast else 0
    up_parts = weight_grad(net, me, [normed2], [gh], "grad_up", all_cols=up_cols)
    gh, up_parts = bar(gh, up_parts)
    gsec, gattn, gmixed, ggain2, gshift2, gbout = second_back(
        net, me, gh, second, cotangent, pieces_u, vecs
    )
    gattn, gmixed, down_got = bar(gattn, gmixed, down_got)
    down_got = down.a(down_got)
    if net.fast:
        up = Scatter(
            net,
            weight_grad(net, me, [mixed], [gattn], "grad_out", up_parts, 4 * width, up_cols),
        )
        out = None
    else:
        up = Scatter(net, up_parts)
        out = Scatter(net, weight_grad(net, me, [mixed], [gattn], "grad_out"))
    gmixed, up.keep, up.send = bar(gmixed, up.keep, up.send)
    up_got = up.core()
    back = (qkv, gmixed, mixed, lse, far_t, HEADS)
    grads = attend_back(*back, 0, 4)
    grads, down_got, up_got = bar(grads, down_got, up_got)
    down_got = down.z(down_got)
    up_got = up.b(up_got)
    grads = attend_back(*back, 1, 4, grads)
    grads = attend_back(*back, 2, 4, grads)
    grads, down_got, up_got = bar(grads, down_got, up_got)
    up_got = up.a(up_got)
    grads = attend_back(*back, 3, 4, grads)
    (gq, gk, gv), up_got = bar(grads, up_got)
    up_got = up.z(up_got)
    gqkv = Scatter(net, weight_grad(net, me, [normed], [gq, gk, gv], "grad_qkv"))
    gq, gqkv.keep, gqkv.send, up_got = bar(gq, gqkv.keep, gqkv.send, up_got)
    qkv_got = gqkv.core()
    gfirst, ggain1, gshift1, gbskip, gbq, gbv = first_back(
        net, me, gq, gk, gv, raw, gsec, pieces_q, vecs
    )
    gfirst, qkv_got, ggain1 = bar(gfirst, qkv_got, ggain1)
    qkv_got = gqkv.b(qkv_got)
    rows = [gbskip, ggain1, gshift1, gbq, gbv, gbout, ggain2, gshift2, gbdown, gbup.reshape(-1, width)]
    rows = sum_vectors(net, jnp.concatenate(rows, axis=0), 0, 1)
    gskip_w = Scatter(net, weight_grad(net, me, [frames, skip], [gfirst], "grad_skip"))
    gfirst, gskip_w.keep, gskip_w.send, rows, qkv_got = bar(
        gfirst, gskip_w.keep, gskip_w.send, rows, qkv_got
    )
    qkv_got = gqkv.a(qkv_got)
    skip_got = gskip_w.core()
    rows = sum_vectors(net, rows, 1, 2)
    gframes, gskip = joined_back(net, me, gfirst, pieces_s)
    gframes, qkv_got, skip_got, second, rows = bar(gframes, qkv_got, skip_got, second, rows)
    skip_got = gskip_w.b(skip_got)
    qkv_got = gqkv.z(qkv_got)
    rows = sum_vectors(net, rows, 2, 3)
    layer_out = down_forward(net, me, second, act, pieces_d, vecs, 0, 2)
    layer_out, qkv_got, skip_got, rows = bar(layer_out, qkv_got, skip_got, rows)
    skip_got = gskip_w.a(skip_got)
    rows = sum_vectors(net, rows, 3, 4)
    layer_out = down_forward(net, me, second, act, pieces_d, vecs, 1, 2, [layer_out])
    layer_out, skip_got, rows = bar(layer_out, skip_got, rows)
    skip_got = gskip_w.z(skip_got)
    rows = sum_vectors(net, rows, 4, net.bits)

    def mine(row):
        each = width // size
        return lax.dynamic_slice(rows[row], (index * each,), (each,))

    wide = rows[9:].reshape(-1)
    each = wide.shape[0] // size
    o_bup = lax.dynamic_slice(wide, (index * each,), (each,))
    up_out = up.done(up_got, slice(0, 4 * width) if net.fast else slice(None))
    if net.fast:
        out_out = up.done(up_got, slice(4 * width, 5 * width))
    else:
        out_out = out.core()
    return (
        layer_out,
        gframes,
        gskip,
        gskip_w.done(skip_got),
        mine(0),
        mine(1),
        mine(2),
        gqkv.done(qkv_got),
        mine(3),
        mine(4),
        out_out,
        mine(5),
        mine(6),
        mine(7),
        up_out,
        o_bup,
        down.done(down_got),
        mine(8),
    )


def solution(mesh):
    mat, vec = P(AXES, None), P(AXES)
    size = math.prod(mesh.shape.values())
    return jax.shard_map(
        functools.partial(body, size),
        mesh=mesh,
        in_specs=(
            mat, mat, mat, vec, mat,
            mat, vec, vec, vec, mat, vec, vec, mat, vec, vec, vec, mat, vec, mat, vec,
        ),
        out_specs=(
            mat, mat, mat,
            mat, vec, vec, vec, mat, vec, vec, mat, vec, vec, vec, mat, vec, mat, vec,
        ),
        check_vma=False,
    )
```

time: 664 us -> 521 us (0.78)
  waiting for transfers between devices: 231 us -> 67.2 us
  local copies, waits for them, and re-layouts: 27.8 us -> 44.1 us
    ppermute x80 -> x69, waiting for transfers between devices: 231 us -> 67.2 us  [pp(): return lax.ppermute(x, AXES, pairs)]
    unnamed x90 -> x210, local copies, waits for them, and re-layouts: 10.9 us -> 37.4 us
    convert_element_type x21 -> x12, other arithmetic: 15.1 us -> 26.3 us  [the longest x8 19.8 us: next(): return self.net.pp(self.summed(lo, 2 * lo).astype(BF), mask)]
    add x5 -> x10, other arithmetic: 0.04 us -> 9.03 us  [the longest x5 8.98 us: done(): total = total + arr[:, cols].astype(F32)]
    concatenate x4 -> x1, local copies, waits for them, and re-layouts: 7.09 us -> 0.09 us  [body(): rows = sum_vectors(net, jnp.concatenate(rows, axis=0), 0, 1)]
    pallas_call x8 -> x17, Pallas kernels: 181 us -> 187 us  [the longest x5 56.1 us: weight_grad(): pl.pallas_call(functools.partial(grad_kernel, net, len(lefts), len(rights...]
    ppermute x80 -> x69, starting transfers between devices: 74 us -> 76.6 us  [pp(): return lax.ppermute(x, AXES, pairs)]
  transfers between devices with their start and end apart: 80 -> 69, of which waited for: 28 -> 16; matrix products, arithmetic and copies ran while one was open for 6% -> 6% of each run, Pallas kernels for 23% -> 54%
where the time goes in v2:
time: 521 us; the launch traced here: 514 us
  Pallas kernels  280 us (54%)
  starting transfers between devices  76.6 us (15%)
  waiting for transfers between devices  67.2 us (13%)
  local copies, waits for them, and re-layouts  44.1 us (8%)
  other arithmetic  43.2 us (8%)
    ppermute x69, starting transfers between devices, pp(): return lax.ppermute(x, AXES, pairs)  76.6 us
    ppermute x69, waiting for transfers between devices, pp(): return lax.ppermute(x, AXES, pairs)  67.2 us
    pallas_call x5, Pallas kernels, weight_grad(): pl.pallas_call(functools.partial(grad_kernel, net, len(lefts), len(rights...  56.1 us
    pallas_call x4, Pallas kernels, attend_back(): pl.pallas_call(functools.partial(attend_back_kernel, size, blk, start), g...  55.8 us
    pallas_call x2, Pallas kernels, attend(): pl.pallas_call(functools.partial(attend_kernel, size, blk, start), grid=(...  38 us
    unnamed x210, local copies, waits for them, and re-layouts  37.4 us
    pallas_call x1, Pallas kernels, up_forward(): pl.pallas_call(functools.partial(up_kernel, net), grid=(tok // blk,), in_...  27 us
    convert_element_type x8, other arithmetic, next(): return self.net.pp(self.summed(lo, 2 * lo).astype(BF), mask)  19.8 us
  transfers between devices with their start and end apart: 69, of which 16 were waited for; matrix products, arithmetic and copies ran while one was open for 6% of the time, Pallas kernels for 54%

profile of v2, /device:TPU:0, one launch (start us, length us, event | category | flops | bytes accessed | tf_op | source)
XLA Modules:
  0.0 513.5 jit_solution(8687649897757399189)
XLA Ops:
  0.7 3.1 collective-permute-start
  3.8 2.6 collective-permute-start.1
  11.1 5.8 %collective-permute-done.1 = bf16[64,1024]{1,0:T(8,128)(2,1)S(1)} collective-permute-done((bf16[64,1024]{1,0:T(8,128)(2,1)}, bf16[64,1024]{1,0:T(8,128)(2,1)S(1)}, u32[]{:S(2)}, u32[]{:S(2)}) %collective-permute-start.1) | collective-permute-done | bytes 131104 | tf_op jit(solution)/shard_map/ppermute | solution.py:44
  25.6 4.7 collective-permute-done.5
  30.3 3.9 collective-permute-done.6
  35.3 2.4 collective-permute-start.10
  41.3 3.0 collective-permute-done.10
  49.9 4.2 collective-permute-start.15
  59.6 9.2 %skip_forward.1.raw = f32[1024,1024]{1,0:T(8,128)S(1)} custom-call(s32[1]{0:T(128)} %bitcast.me_ref, bf16[1024,1024]{1,0:T(8,128)(2,1)S(1)} %copy-done.41, bf16[1024,1024]{1,0:T(8,128)(2,1)S(1)} %copy-done.43, bf16[4,64,1024]{2,1,0:T(8,128)(2,1)S(1)} %pad_maximum_fusion.3.rest_0_, bf16[4,64,1024]{2,1,0:T(8,128)(2,1)S(1)} %copy-done.62, ...), custom_call_target="tpu_custom_call" | custom-call | flops 4294967296 | bytes 12582912 | tf_op jit(solution)/shard_map/skip_forward/pallas_call | solution.py:342
  69.6 11.7 %collective-permute-done.16.rest_3_ = bf16[4,32,3200]{2,1,0:T(8,128)(2,1)S(1)} collective-permute-done((bf16[4,32,3200]{2,1,0:T(8,128)(2,1)S(1)}, bf16[4,32,3200]{2,1,0:T(8,128)(2,1)S(1)}, u32[]{:S(2)}, u32[]{:S(2)}) %collective-permute-start.16) | collective-permute-done | bytes 819232 | tf_op jit(solution)/shard_map/ppermute | solution.py:44
  81.9 2.6 collective-permute-start.18
  86.2 6.7 %collective-permute-done.18 = bf16[32,5120]{1,0:T(8,128)(2,1)S(1)} collective-permute-done((bf16[32,5120]{1,0:T(8,128)(2,1)S(1)}, bf16[32,5120]{1,0:T(8,128)(2,1)S(1)}, u32[]{:S(2)}, u32[]{:S(2)}) %collective-permute-start.18) | collective-permute-done | bytes 327712 | tf_op jit(solution)/shard_map/ppermute | solution.py:44
  92.8 8.4 %collective-permute-done.19 = bf16[32,5120]{1,0:T(8,128)(2,1)S(1)} collective-permute-done((bf16[32,5120]{1,0:T(8,128)(2,1)S(1)}, bf16[32,5120]{1,0:T(8,128)(2,1)S(1)}, u32[]{:S(2)}, u32[]{:S(2)}) %collective-permute-start.19) | collective-permute-done | bytes 327712 | tf_op jit(solution)/shard_map/ppermute | solution.py:44
  104.7 12.2 %qkv_forward.1 = (bf16[1024,1024]{1,0:T(8,128)(2,1)S(1)}, bf16[1024,3072]{1,0:T(8,128)(2,1)}) custom-call(s32[1]{0:T(128)} %bitcast.me_ref, f32[1024,1024]{1,0:T(8,128)S(1)} %skip_forward.1.raw, f32[16,1024]{1,0:T(8,128)S(1)} %get-tuple-element.303.vecs, bf16[4,32,3200]{2,1,0:T(8,128)(2,1)S(1)} %pad_maximum_fusion.2.rest_0_, ...), custom_call_target="tpu_custom_call" | custom-call | flops 6442450944 | bytes 18874368 | tf_op jit(solution)/shard_map/qkv_forward/pallas_call | solution.py:382
  122.0 2.8 copy-done.79
  124.8 19.1 %attend.2 = (bf16[1024,1024]{1,0:T(8,128)(2,1)S(1)}, f32[8,8,1024]{2,1,0:T(8,128)S(1)}) custom-call(bf16[1024,3072]{1,0:T(8,128)(2,1)S(1)} %copy-done.79, bf16[1024,3072]{1,0:T(8,128)(2,1)S(1)} %copy-done.79, bf16[1024,3072]{1,0:T(8,128)(2,1)S(1)} %copy-done.79, f32[1024,1024]{1,0:T(8,128)S(1)} %copy-done.16), custom_call_target="tpu_custom_call" | custom-call | flops 8589934592 | bytes 4194304 | tf_op jit(solution)/shard_map/attend/pallas_call | solution.py:839
  145.5 2.5 collective-permute-start.31
  148.1 18.9 %attend.3 = (bf16[1024,1024]{1,0:T(8,128)(2,1)S(1)}, f32[8,8,1024]{2,1,0:T(8,128)S(1)}) custom-call(bf16[1024,3072]{1,0:T(8,128)(2,1)S(1)} %copy-done.79, bf16[1024,3072]{1,0:T(8,128)(2,1)S(1)} %copy-done.79, bf16[1024,3072]{1,0:T(8,128)(2,1)S(1)} %copy-done.79, f32[1024,1024]{1,0:T(8,128)S(1)} %copy-done.16, ...), custom_call_target="tpu_custom_call", output_to_operand_aliasing={{0}: (4, {}), {1}: (5, {})} | custom-call | flops 8589934592 | bytes 4194304 | tf_op jit(solution)/shard_map/attend/pallas_call | solution.py:839
  168.4 2.8 collective-permute-done.32.rest_7_
  174.3 27.0 %up_forward.1 = (f32[1024,1024]{1,0:T(8,128)}, bf16[1024,1024]{1,0:T(8,128)(2,1)S(1)}, bf16[1024,4096]{1,0:T(8,128)(2,1)}, bf16[1024,4096]{1,0:T(8,128)(2,1)}) custom-call(s32[1]{0:T(128)} %bitcast.me_ref, f32[1024,1024]{1,0:T(8,128)} %copy-done.70, bf16[1024,1024]{1,0:T(8,128)(2,1)S(1)} %get-tuple-element.338.mixed.rest_0_.o, ...), custom_call_target="tpu_custom_call" | custom-call | flops 10737418240 | bytes 39845888 | tf_op jit(solution)/shard_map/up_forward/pallas_call | solution.py:446
  204.2 13.0 %grad_down.1 = (bf16[16,128,1024]{2,1,0:T(8,128)(2,1)S(1)}, bf16[16,128,1024]{2,1,0:T(8,128)(2,1)S(1)}) custom-call(s32[1]{0:T(128)} %bitcast.me_ref, bf16[1024,4096]{1,0:T(8,128)(2,1)} %get-tuple-element.354.rest_0_.act, bf16[1024,1024]{1,0:T(8,128)(2,1)S(1)} %copy-done.39), custom_call_target="tpu_custom_call" | custom-call | flops 8589934592 | bytes 18874368 | tf_op jit(solution)/shard_map/grad_down/pallas_call | solution.py:602
  217.8 2.4 collective-permute-done.39.rest_7_
  220.5 17.1 %hidden_back.1 = (bf16[1024,4096]{1,0:T(8,128)(2,1)}, f32[1,4096]{1,0:T(1,128)S(1)}, f32[1,1024]{1,0:T(1,128)S(1)}) custom-call(s32[1]{0:T(128)} %bitcast.me_ref, bf16[1024,4096]{1,0:T(8,128)(2,1)} %get-tuple-element.348.pull, bf16[1024,1024]{1,0:T(8,128)(2,1)S(1)} %copy-done.39, bf16[4,128,1024]{2,1,0:T(8,128)(2,1)S(1)} %pad_maximum_fusion.1.rest_0_, ...), custom_call_target="tpu_custom_call" | custom-call | flops 8589934592 | bytes 27262976 | tf_op jit(solution)/shard_map/hidden_back/pallas_call | solution.py:529
  237.7 3.9 add_convert_fusion.1
  244.2 14.8 %grad_up.1 = (bf16[16,32,5120]{2,1,0:T(8,128)(2,1)S(1)}, bf16[16,32,5120]{2,1,0:T(8,128)(2,1)}) custom-call(s32[1]{0:T(128)} %bitcast.me_ref, bf16[1024,1024]{1,0:T(8,128)(2,1)S(1)} %copy-done.85, bf16[1024,4096]{1,0:T(8,128)(2,1)} %get-tuple-element.383.rest_1_.gh), custom_call_target="tpu_custom_call" | custom-call | flops 8589934592 | bytes 18874368 | tf_op jit(solution)/shard_map/grad_up/pallas_call | solution.py:602
  260.7 19.2 %second_back.1 = (f32[1024,1024]{1,0:T(8,128)}, bf16[1024,1024]{1,0:T(8,128)(2,1)S(1)}, bf16[1024,1024]{1,0:T(8,128)(2,1)S(1)}, f32[1,1024]{1,0:T(1,128)S(1)}, f...) custom-call(s32[1]{0:T(128)} %bitcast.me_ref, bf16[1024,4096]{1,0:T(8,128)(2,1)} %get-tuple-element.383.rest_1_.gh, ...), custom_call_target="tpu_custom_call" | custom-call | flops 10737418240 | bytes 33554432 | tf_op jit(solution)/shard_map/second_back/pallas_call | solution.py:671
  284.1 4.3 grad_out.1
  288.9 4.6 add_convert_fusion.5
  294.6 13.8 %attend_back.4 = (bf16[1024,1024]{1,0:T(8,128)(2,1)S(1)}, bf16[1024,1024]{1,0:T(8,128)(2,1)S(1)}, bf16[1024,1024]{1,0:T(8,128)(2,1)S(1)}) custom-call(bf16[1024,3072]{1,0:T(8,128)(2,1)} %get-tuple-element.306.q.k.v, bf16[1024,3072]{1,0:T(8,128)(2,1)} %get-tuple-element.306.q.k.v, bf16[1024,3072]{1,0:T(8,128)(2,1)} %get-tuple-element.306.q.k.v, ...), custom_call_target="tpu_custom_call" | custom-call | flops 10737418240 | bytes 4194304 | tf_op jit(solution)/shard_map/attend_back/pallas_call | solution.py:915
  308.4 4.6 add_convert_fusion
  320.7 14.2 %attend_back.5 = (bf16[1024,1024]{1,0:T(8,128)(2,1)S(1)}, bf16[1024,1024]{1,0:T(8,128)(2,1)S(1)}, bf16[1024,1024]{1,0:T(8,128)(2,1)S(1)}) custom-call(bf16[1024,3072]{1,0:T(8,128)(2,1)} %get-tuple-element.306.q.k.v, bf16[1024,3072]{1,0:T(8,128)(2,1)} %get-tuple-element.306.q.k.v, ...), custom_call_target="tpu_custom_call", output_to_operand_aliasing={{0}: (7, {}), {1}: (8, {}), {2}: (9, {})} | custom-call | flops 10737418240 | bytes 4194304 | tf_op jit(solution)/shard_map/attend_back/pallas_call | solution.py:915
  334.9 14.0 %attend_back.6 = (bf16[1024,1024]{1,0:T(8,128)(2,1)S(1)}, bf16[1024,1024]{1,0:T(8,128)(2,1)S(1)}, bf16[1024,1024]{1,0:T(8,128)(2,1)S(1)}) custom-call(bf16[1024,3072]{1,0:T(8,128)(2,1)} %get-tuple-element.306.q.k.v, bf16[1024,3072]{1,0:T(8,128)(2,1)} %get-tuple-element.306.q.k.v, ...), custom_call_target="tpu_custom_call", output_to_operand_aliasing={{0}: (7, {}), {1}: (8, {}), {2}: (9, {})} | custom-call | flops 10737418240 | bytes 4194304 | tf_op jit(solution)/shard_map/attend_back/pallas_call | solution.py:915
  349.8 2.3 add_convert_fusion.3
  353.2 13.8 %attend_back.7 = (bf16[1024,1024]{1,0:T(8,128)(2,1)S(1)}, bf16[1024,1024]{1,0:T(8,128)(2,1)S(1)}, bf16[1024,1024]{1,0:T(8,128)(2,1)S(1)}) custom-call(bf16[1024,3072]{1,0:T(8,128)(2,1)} %get-tuple-element.306.q.k.v, bf16[1024,3072]{1,0:T(8,128)(2,1)} %get-tuple-element.306.q.k.v, ...), custom_call_target="tpu_custom_call", output_to_operand_aliasing={{0}: (7, {}), {1}: (8, {}), {2}: (9, {})} | custom-call | flops 10737418240 | bytes 4194304 | tf_op jit(solution)/shard_map/attend_back/pallas_call | solution.py:915
  369.7 2.5 fusion.9
  372.4 2.3 collective-permute-start.50
  381.6 12.4 %grad_qkv.1 = (bf16[16,32,3072]{2,1,0:T(8,128)(2,1)S(1)}, bf16[16,32,3072]{2,1,0:T(8,128)(2,1)}) custom-call(s32[1]{0:T(128)} %bitcast.me_ref, bf16[1024,1024]{1,0:T(8,128)(2,1)S(1)} %copy-done.83, bf16[1024,1024]{1,0:T(8,128)(2,1)S(1)} %copy-done.74, bf16[1024,1024]{1,0:T(8,128)(2,1)S(1)} %copy-done.76, bf16[1024,1024]{1,0:T(8,128)(2,1)S(1)} %copy-done.78), custom_call_target="tpu_custom_call" | custom-call | flops 6442450944 | bytes 14680064 | tf_op jit(solution)/shard_map/grad_qkv/pallas_call | solution.py:602
  394.0 4.0 collective-permute-done.50
  398.2 14.9 %first_back.1 = (bf16[1024,1024]{1,0:T(8,128)(2,1)S(1)}, f32[1,1024]{1,0:T(1,128)S(1)}, f32[1,1024]{1,0:T(1,128)S(1)}, f32[1,1024]{1,0:T(1,128)S(1)}, f32[1,1024]{1,0:T(1,128)S(1)}, /*index=5*/f32[1,1024]{1,0:T(1,128)S(1)}) custom-call(s32[1]{0:T(128)} %bitcast.me_ref, bf16[1024,1024]{1,0:T(8,128)(2,1)S(1)} %copy-done.74, bf16[1024,1024]{1,0:T(8,128)(2,1)S(1)} %copy-done.76, ...), custom_call_target="tpu_custom_call" | custom-call | flops 6442450944 | bytes 23068672 | tf_op jit(solution)/shard_map/first_back/pallas_call | solution.py:725
  418.8 2.4 fusion.1
  426.5 11.6 %grad_skip.1 = (bf16[16,64,1024]{2,1,0:T(8,128)(2,1)S(1)}, bf16[16,64,1024]{2,1,0:T(8,128)(2,1)S(1)}) custom-call(s32[1]{0:T(128)} %bitcast.me_ref, bf16[1024,1024]{1,0:T(8,128)(2,1)S(1)} %copy-done.42, bf16[1024,1024]{1,0:T(8,128)(2,1)S(1)} %copy-done.44, bf16[1024,1024]{1,0:T(8,128)(2,1)S(1)} %copy-done.72), custom_call_target="tpu_custom_call" | custom-call | flops 4294967296 | bytes 10485760 | tf_op jit(solution)/shard_map/grad_skip/pallas_call | solution.py:602
  446.2 10.4 %joined_back.1 = (bf16[1024,1024]{1,0:T(8,128)(2,1)}, bf16[1024,1024]{1,0:T(8,128)(2,1)}) custom-call(s32[1]{0:T(128)} %bitcast.me_ref, bf16[1024,1024]{1,0:T(8,128)(2,1)S(1)} %copy-done.72, bf16[4,64,1024]{2,1,0:T(8,128)(2,1)S(1)} %copy-done.38, bf16[4,64,1024]{2,1,0:T(8,128)(2,1)S(1)} %copy-done.63, bf16[4,64,1024]{2,1,0:T(8,128)(2,1)} %collective-permute-done.4.rest_2_, ...), custom_call_target="tpu_custom_call" | custom-call | flops 4294967296 | bytes 10485760 | tf_op jit(solution)/shard_map/joined_back/pallas_call | solution.py:758
  459.7 5.1 collective-permute-start.58
  468.3 8.1 %down_forward.2.rest_8_ = bf16[1024,1024]{1,0:T(8,128)(2,1)} custom-call(s32[1]{0:T(128)} %bitcast.me_ref, f32[1024,1024]{1,0:T(8,128)S(1)} %copy-done.1, bf16[1024,4096]{1,0:T(8,128)(2,1)} %get-tuple-element.354.rest_0_.act, f32[16,1024]{1,0:T(8,128)S(1)} %get-tuple-element.303.vecs, bf16[4,128,1024]{2,1,0:T(8,128)(2,1)S(1)} %pad_maximum_fusion.1.rest_0_, ...), custom_call_target="tpu_custom_call" | custom-call | flops 4294967296 | bytes 15728640 | tf_op jit(solution)/shard_map/down_forward/pallas_call | solution.py:486
  476.5 5.5 %collective-permute-done.59 = bf16[32,3072]{1,0:T(8,128)(2,1)S(1)} collective-permute-done((bf16[32,3072]{1,0:T(8,128)(2,1)S(1)}, bf16[32,3072]{1,0:T(8,128)(2,1)S(1)}, u32[]{:S(2)}, u32[]{:S(2)}) %collective-permute-start.59) | collective-permute-done | bytes 196640 | tf_op jit(solution)/shard_map/ppermute | solution.py:44
  483.3 3.2 collective-permute-start.64
  488.3 8.4 %down_forward.3 = bf16[1024,1024]{1,0:T(8,128)(2,1)} custom-call(s32[1]{0:T(128)} %bitcast.me_ref, f32[1024,1024]{1,0:T(8,128)S(1)} %copy-done.1, bf16[1024,4096]{1,0:T(8,128)(2,1)} %get-tuple-element.354.rest_0_.act, f32[16,1024]{1,0:T(8,128)S(1)} %get-tuple-element.303.vecs, ...), custom_call_target="tpu_custom_call", output_to_operand_aliasing={{}: (12, {})} | custom-call | flops 4294967296 | bytes 15728640 | tf_op jit(solution)/shard_map/down_forward/pallas_call | solution.py:486
  502.0 5.9 %collective-permute-done.68 = f32[13,1024]{1,0:T(8,128)S(1)} collective-permute-done((f32[13,1024]{1,0:T(8,128)S(1)}, f32[13,1024]{1,0:T(8,128)S(1)}, u32[]{:S(2)}, u32[]{:S(2)}) %collective-permute-start.68) | collective-permute-done | bytes 53280 | tf_op jit(solution)/shard_map/ppermute | solution.py:44
  (370 shorter events, 118.7 us)
Async XLA Ops:
  17.9 16.2 %collective-permute-start.3 = (bf16[4,64,1024]{2,1,0:T(8,128)(2,1)S(1)}, bf16[4,64,1024]{2,1,0:T(8,128)(2,1)S(1)}, u32[]{:S(2)}, u32[]{:S(2)}) collective-permute-start(bf16[4,64,1024]{2,1,0:T(8,128)(2,1)S(1)} %pad_maximum_fusion.3.rest_0_), channel_id=1, source_target_pairs={{0,2},{1,5},{2,0},{3,7},{4,6},{5,1},{6,4},{7,3},{8,10},{9,13},{10,... | collective-permute-start | bytes 1572872 | tf_op jit(solution)/shard_map/ppermute | solution.py:44
  19.5 14.7 %collective-permute-start.4 = (bf16[4,64,1024]{2,1,0:T(8,128)(2,1)S(1)}, bf16[4,64,1024]{2,1,0:T(8,128)(2,1)}, u32[]{:S(2)}, u32[]{:S(2)}) collective-permute-start(bf16[4,64,1024]{2,1,0:T(8,128)(2,1)S(1)} %pad_maximum_fusion.3.rest_0_), channel_id=1, source_target_pairs={{0,4},{1,3},{2,6},{3,1},{4,0},{5,7},{6,2},{7,5},{8,12},{9,11},{10,... | collective-permute-start | bytes 1572872 | tf_op jit(solution)/shard_map/ppermute | solution.py:44
  47.6 21.3 %collective-permute-start.13 = (bf16[4,32,3200]{2,1,0:T(8,128)(2,1)S(1)}, bf16[4,32,3200]{2,1,0:T(8,128)(2,1)S(1)}, u32[]{:S(2)}, u32[]{:S(2)}) collective-permute-start(bf16[4,32,3200]{2,1,0:T(8,128)(2,1)S(1)} %pad_maximum_fusion.2.rest_0_), channel_id=1, source_target_pairs={{0,2},{1,5},{2,0},{3,7},{4,6},{5,1},{6,4},{7,3},{8,10},{9,13},{10,... | collective-permute-start | bytes 2457608 | tf_op jit(solution)/shard_map/ppermute | solution.py:44
  48.2 20.7 %collective-permute-start.14 = (bf16[4,32,3200]{2,1,0:T(8,128)(2,1)S(1)}, bf16[4,32,3200]{2,1,0:T(8,128)(2,1)S(1)}, u32[]{:S(2)}, u32[]{:S(2)}) collective-permute-start(bf16[4,32,3200]{2,1,0:T(8,128)(2,1)S(1)} %pad_maximum_fusion.2.rest_0_), channel_id=1, source_target_pairs={{0,4},{1,3},{2,6},{3,1},{4,0},{5,7},{6,2},{7,5},{8,12},{9,11},{10,... | collective-permute-start | bytes 2457608 | tf_op jit(solution)/shard_map/ppermute | solution.py:44
  49.9 19.0 %collective-permute-start.15 = (bf16[32,5120]{1,0:T(8,128)(2,1)}, bf16[32,5120]{1,0:T(8,128)(2,1)S(1)}, u32[]{:S(2)}, u32[]{:S(2)}) collective-permute-start(bf16[32,5120]{1,0:T(8,128)(2,1)} %pad_maximum_fusion.4), channel_id=1, source_target_pairs={{0,16},{1,17},{2,18},{3,19},{4,20},{5,21},{6,22},{7,23},{8,24},{9,... | collective-permute-start | bytes 983048 | tf_op jit(solution)/shard_map/ppermute | solution.py:44
  81.3 19.9 %collective-permute-start.20 = (bf16[4,32,3200]{2,1,0:T(8,128)(2,1)S(1)}, bf16[4,32,3200]{2,1,0:T(8,128)(2,1)S(1)}, u32[]{:S(2)}, u32[]{:S(2)}) collective-permute-start(bf16[4,32,3200]{2,1,0:T(8,128)(2,1)S(1)} %collective-permute-done.13.rest_1_), channel_id=1, source_target_pairs={{0,1},{1,0},{2,3},{3,2},{4,5},{5,4},{6,7},{7,6},{8,9},{9,8},{10,11... | collective-permute-start | bytes 2457608 | tf_op jit(solution)/shard_map/ppermute | solution.py:44
  81.4 19.9 %collective-permute-start.21 = (bf16[4,32,3200]{2,1,0:T(8,128)(2,1)S(1)}, bf16[4,32,3200]{2,1,0:T(8,128)(2,1)S(1)}, u32[]{:S(2)}, u32[]{:S(2)}) collective-permute-start(bf16[4,32,3200]{2,1,0:T(8,128)(2,1)S(1)} %collective-permute-done.14.rest_2_), channel_id=1, source_target_pairs={{0,1},{1,0},{2,3},{3,2},{4,5},{5,4},{6,7},{7,6},{8,9},{9,8},{10,11... | collective-permute-start | bytes 2457608 | tf_op jit(solution)/shard_map/ppermute | solution.py:44
  81.9 19.4 %collective-permute-start.22 = (bf16[4,32,3200]{2,1,0:T(8,128)(2,1)S(1)}, bf16[4,32,3200]{2,1,0:T(8,128)(2,1)S(1)}, u32[]{:S(2)}, u32[]{:S(2)}) collective-permute-start(bf16[4,32,3200]{2,1,0:T(8,128)(2,1)S(1)} %collective-permute-done.16.rest_3_), channel_id=1, source_target_pairs={{0,1},{1,0},{2,3},{3,2},{4,5},{5,4},{6,7},{7,6},{8,9},{9,8},{10,11... | collective-permute-start | bytes 2457608 | tf_op jit(solution)/shard_map/ppermute | solution.py:44
  84.5 16.7 %collective-permute-start.19 = (bf16[32,5120]{1,0:T(8,128)(2,1)S(1)}, bf16[32,5120]{1,0:T(8,128)(2,1)S(1)}, u32[]{:S(2)}, u32[]{:S(2)}) collective-permute-start(bf16[32,5120]{1,0:T(8,128)(2,1)S(1)} %copy-done.89), channel_id=1, source_target_pairs={{0,24},{1,25},{2,26},{3,27},{4,28},{5,29},{6,30},{7,31},{8,16},{9,... | collective-permute-start | bytes 983048 | tf_op jit(solution)/shard_map/ppermute | solution.py:44
  101.4 42.5 %collective-permute-start.23 = (bf16[4,32,5120]{2,1,0:T(8,128)(2,1)S(1)}, bf16[4,32,5120]{2,1,0:T(8,128)(2,1)S(1)}, u32[]{:S(2)}, u32[]{:S(2)}) collective-permute-start(bf16[4,32,5120]{2,1,0:T(8,128)(2,1)S(1)} %pad_maximum_fusion.rest_0_), channel_id=1, source_target_pairs={{0,2},{1,5},{2,0},{3,7},{4,6},{5,1},{6,4},{7,3},{8,10},{9,13},{10,... | collective-permute-start | bytes 3932168 | tf_op jit(solution)/shard_map/ppermute | solution.py:44
  103.0 40.9 %collective-permute-start.24 = (bf16[4,32,5120]{2,1,0:T(8,128)(2,1)S(1)}, bf16[4,32,5120]{2,1,0:T(8,128)(2,1)S(1)}, u32[]{:S(2)}, u32[]{:S(2)}) collective-permute-start(bf16[4,32,5120]{2,1,0:T(8,128)(2,1)S(1)} %pad_maximum_fusion.rest_0_), channel_id=1, source_target_pairs={{0,4},{1,3},{2,6},{3,1},{4,0},{5,7},{6,2},{7,5},{8,12},{9,11},{10,... | collective-permute-start | bytes 3932168 | tf_op jit(solution)/shard_map/ppermute | solution.py:44
  120.1 23.7 %collective-permute-start.25 = (bf16[128,1024]{1,0:T(8,128)(2,1)S(1)}, bf16[128,1024]{1,0:T(8,128)(2,1)S(1)}, u32[]{:S(2)}, u32[]{:S(2)}) collective-permute-start(bf16[128,1024]{1,0:T(8,128)(2,1)S(1)} %copy-done.99), channel_id=1, source_target_pairs={{0,8},{1,9},{2,10},{3,11},{4,12},{5,13},{6,14},{7,15},{8,0},{9,1},... | collective-permute-start | bytes 786440 | tf_op jit(solution)/shard_map/ppermute | solution.py:44
  120.2 23.7 %collective-permute-start.26 = (bf16[128,1024]{1,0:T(8,128)(2,1)S(1)}, bf16[128,1024]{1,0:T(8,128)(2,1)S(1)}, u32[]{:S(2)}, u32[]{:S(2)}) collective-permute-start(bf16[128,1024]{1,0:T(8,128)(2,1)S(1)} %copy-done.99), channel_id=1, source_target_pairs={{0,16},{1,17},{2,18},{3,19},{4,20},{5,21},{6,22},{7,23},{8,24},{9,... | collective-permute-start | bytes 786440 | tf_op jit(solution)/shard_map/ppermute | solution.py:44
  143.9 23.1 %collective-permute-start.27 = (bf16[4,32,5120]{2,1,0:T(8,128)(2,1)S(1)}, bf16[4,32,5120]{2,1,0:T(8,128)(2,1)S(1)}, u32[]{:S(2)}, u32[]{:S(2)}) collective-permute-start(bf16[4,32,5120]{2,1,0:T(8,128)(2,1)S(1)} %collective-permute-done.23.rest_1_), channel_id=1, source_target_pairs={{0,4},{1,3},{2,6},{3,1},{4,0},{5,7},{6,2},{7,5},{8,12},{9,11},{10,... | collective-permute-start | bytes 3932168 | tf_op jit(solution)/shard_map/ppermute | solution.py:44
  145.0 22.1 %collective-permute-start.29 = (bf16[4,32,5120]{2,1,0:T(8,128)(2,1)S(1)}, bf16[4,32,5120]{2,1,0:T(8,128)(2,1)S(1)}, u32[]{:S(2)}, u32[]{:S(2)}) collective-permute-start(bf16[4,32,5120]{2,1,0:T(8,128)(2,1)S(1)} %collective-permute-done.23.rest_1_), channel_id=1, source_target_pairs={{0,1},{1,0},{2,3},{3,2},{4,5},{5,4},{6,7},{7,6},{8,9},{9,8},{10,11... | collective-permute-start | bytes 3932168 | tf_op jit(solution)/shard_map/ppermute | solution.py:44
  145.0 22.0 %collective-permute-start.28 = (bf16[4,32,5120]{2,1,0:T(8,128)(2,1)S(1)}, bf16[4,32,5120]{2,1,0:T(8,128)(2,1)S(1)}, u32[]{:S(2)}, u32[]{:S(2)}) collective-permute-start(bf16[4,32,5120]{2,1,0:T(8,128)(2,1)S(1)} %pad_maximum_fusion.rest_0_), channel_id=1, source_target_pairs={{0,1},{1,0},{2,3},{3,2},{4,5},{5,4},{6,7},{7,6},{8,9},{9,8},{10,11... | collective-permute-start | bytes 3932168 | tf_op jit(solution)/shard_map/ppermute | solution.py:44
  145.5 21.6 %collective-permute-start.30 = (bf16[4,32,5120]{2,1,0:T(8,128)(2,1)S(1)}, bf16[4,32,5120]{2,1,0:T(8,128)(2,1)S(1)}, u32[]{:S(2)}, u32[]{:S(2)}) collective-permute-start(bf16[4,32,5120]{2,1,0:T(8,128)(2,1)S(1)} %collective-permute-done.24.rest_2_), channel_id=1, source_target_pairs={{0,1},{1,0},{2,3},{3,2},{4,5},{5,4},{6,7},{7,6},{8,9},{9,8},{10,11... | collective-permute-start | bytes 3932168 | tf_op jit(solution)/shard_map/ppermute | solution.py:44
  145.5 21.5 %collective-permute-start.31 = (bf16[128,1024]{1,0:T(8,128)(2,1)S(1)}, bf16[128,1024]{1,0:T(8,128)(2,1)S(1)}, u32[]{:S(2)}, u32[]{:S(2)}) collective-permute-start(bf16[128,1024]{1,0:T(8,128)(2,1)S(1)} %copy-done.99), channel_id=1, source_target_pairs={{0,24},{1,25},{2,26},{3,27},{4,28},{5,29},{6,30},{7,31},{8,16},{9,... | collective-permute-start | bytes 786440 | tf_op jit(solution)/shard_map/ppermute | solution.py:44
  171.4 31.3 %collective-permute-start.33 = (bf16[4,128,1024]{2,1,0:T(8,128)(2,1)S(1)}, bf16[4,128,1024]{2,1,0:T(8,128)(2,1)S(1)}, u32[]{:S(2)}, u32[]{:S(2)}) collective-permute-start(bf16[4,128,1024]{2,1,0:T(8,128)(2,1)S(1)} %pad_maximum_fusion.1.rest_0_), channel_id=1, source_target_pairs={{0,2},{1,5},{2,0},{3,7},{4,6},{5,1},{6,4},{7,3},{8,10},{9,13},{10,... | collective-permute-start | bytes 3145736 | tf_op jit(solution)/shard_map/ppermute | solution.py:44
  171.9 30.7 %collective-permute-start.34 = (bf16[4,128,1024]{2,1,0:T(8,128)(2,1)S(1)}, bf16[4,128,1024]{2,1,0:T(8,128)(2,1)S(1)}, u32[]{:S(2)}, u32[]{:S(2)}) collective-permute-start(bf16[4,128,1024]{2,1,0:T(8,128)(2,1)S(1)} %pad_maximum_fusion.1.rest_0_), channel_id=1, source_target_pairs={{0,4},{1,3},{2,6},{3,1},{4,0},{5,7},{6,2},{7,5},{8,12},{9,11},{10,... | collective-permute-start | bytes 3145736 | tf_op jit(solution)/shard_map/ppermute | solution.py:44
  202.6 14.8 %collective-permute-start.35 = (bf16[4,128,1024]{2,1,0:T(8,128)(2,1)S(1)}, bf16[4,128,1024]{2,1,0:T(8,128)(2,1)S(1)}, u32[]{:S(2)}, u32[]{:S(2)}) collective-permute-start(bf16[4,128,1024]{2,1,0:T(8,128)(2,1)S(1)} %collective-permute-done.33.rest_1_), channel_id=1, source_target_pairs={{0,4},{1,3},{2,6},{3,1},{4,0},{5,7},{6,2},{7,5},{8,12},{9,11},{10,... | collective-permute-start | bytes 3145736 | tf_op jit(solution)/shard_map/ppermute | solution.py:44
  203.6 13.8 %collective-permute-start.37 = (bf16[4,128,1024]{2,1,0:T(8,128)(2,1)S(1)}, bf16[4,128,1024]{2,1,0:T(8,128)(2,1)S(1)}, u32[]{:S(2)}, u32[]{:S(2)}) collective-permute-start(bf16[4,128,1024]{2,1,0:T(8,128)(2,1)S(1)} %collective-permute-done.33.rest_1_), channel_id=1, source_target_pairs={{0,1},{1,0},{2,3},{3,2},{4,5},{5,4},{6,7},{7,6},{8,9},{9,8},{10,11... | collective-permute-start | bytes 3145736 | tf_op jit(solution)/shard_map/ppermute | solution.py:44
  203.6 13.8 %collective-permute-start.36 = (bf16[4,128,1024]{2,1,0:T(8,128)(2,1)S(1)}, bf16[4,128,1024]{2,1,0:T(8,128)(2,1)S(1)}, u32[]{:S(2)}, u32[]{:S(2)}) collective-permute-start(bf16[4,128,1024]{2,1,0:T(8,128)(2,1)S(1)} %pad_maximum_fusion.1.rest_0_), channel_id=1, source_target_pairs={{0,1},{1,0},{2,3},{3,2},{4,5},{5,4},{6,7},{7,6},{8,9},{9,8},{10,11... | collective-permute-start | bytes 3145736 | tf_op jit(solution)/shard_map/ppermute | solution.py:44
  204.1 13.3 %collective-permute-start.38 = (bf16[4,128,1024]{2,1,0:T(8,128)(2,1)S(1)}, bf16[4,128,1024]{2,1,0:T(8,128)(2,1)S(1)}, u32[]{:S(2)}, u32[]{:S(2)}) collective-permute-start(bf16[4,128,1024]{2,1,0:T(8,128)(2,1)S(1)} %collective-permute-done.34.rest_2_), channel_id=1, source_target_pairs={{0,1},{1,0},{2,3},{3,2},{4,5},{5,4},{6,7},{7,6},{8,9},{9,8},{10,11... | collective-permute-start | bytes 3145736 | tf_op jit(solution)/shard_map/ppermute | solution.py:44
  220.2 17.5 %collective-permute-start.40 = (bf16[16,128,1024]{2,1,0:T(8,128)(2,1)S(1)}, bf16[16,128,1024]{2,1,0:T(8,128)(2,1)}, u32[]{:S(2)}, u32[]{:S(2)}) collective-permute-start(bf16[16,128,1024]{2,1,0:T(8,128)(2,1)S(1)} %get-tuple-element.378), channel_id=1, source_target_pairs={{0,1},{1,0},{2,3},{3,2},{4,5},{5,4},{6,7},{7,6},{8,9},{9,8},{10,11... | collective-permute-start | bytes 12582920 | tf_op jit(solution)/shard_map/ppermute | solution.py:44
  241.6 40.9 %collective-permute-start.41 = (bf16[8,128,1024]{2,1,0:T(8,128)(2,1)}, bf16[8,128,1024]{2,1,0:T(8,128)(2,1)}, u32[]{:S(2)}, u32[]{:S(2)}) collective-permute-start(bf16[8,128,1024]{2,1,0:T(8,128)(2,1)} %add_convert_fusion.1), channel_id=1, source_target_pairs={{0,4},{1,3},{2,6},{3,1},{4,0},{5,7},{6,2},{7,5},{8,12},{9,11},{10,... | collective-permute-start | bytes 6291464 | tf_op jit(solution)/shard_map/ppermute | solution.py:44
  288.4 20.0 %collective-permute-start.43 = (bf16[16,32,5120]{2,1,0:T(8,128)(2,1)}, bf16[16,32,5120]{2,1,0:T(8,128)(2,1)}, u32[]{:S(2)}, u32[]{:S(2)}) collective-permute-start(bf16[16,32,5120]{2,1,0:T(8,128)(2,1)} %get-tuple-element.402), channel_id=1, source_target_pairs={{0,1},{1,0},{2,3},{3,2},{4,5},{5,4},{6,7},{7,6},{8,9},{9,8},{10,11... | collective-permute-start | bytes 15728648 | tf_op jit(solution)/shard_map/ppermute | solution.py:44
  293.6 14.9 %collective-permute-start.42 = (bf16[4,128,1024]{2,1,0:T(8,128)(2,1)S(1)}, bf16[4,128,1024]{2,1,0:T(8,128)(2,1)S(1)}, u32[]{:S(2)}, u32[]{:S(2)}) collective-permute-start(bf16[4,128,1024]{2,1,0:T(8,128)(2,1)S(1)} %add_convert_fusion.5), channel_id=1, source_target_pairs={{0,2},{1,5},{2,0},{3,7},{4,6},{5,1},{6,4},{7,3},{8,10},{9,13},{10,... | collective-permute-start | bytes 3145736 | tf_op jit(solution)/shard_map/ppermute | solution.py:44
  313.0 36.0 %collective-permute-start.47 = (bf16[8,32,5120]{2,1,0:T(8,128)(2,1)}, bf16[8,32,5120]{2,1,0:T(8,128)(2,1)}, u32[]{:S(2)}, u32[]{:S(2)}) collective-permute-start(bf16[8,32,5120]{2,1,0:T(8,128)(2,1)} %add_convert_fusion), channel_id=1, source_target_pairs={{0,4},{1,3},{2,6},{3,1},{4,0},{5,7},{6,2},{7,5},{8,12},{9,11},{10,... | collective-permute-start | bytes 7864328 | tf_op jit(solution)/shard_map/ppermute | solution.py:44
  316.3 32.7 %collective-permute-start.44 = (bf16[128,1024]{1,0:T(8,128)(2,1)S(1)}, bf16[128,1024]{1,0:T(8,128)(2,1)S(1)}, u32[]{:S(2)}, u32[]{:S(2)}) collective-permute-start(bf16[128,1024]{1,0:T(8,128)(2,1)S(1)} %get-tuple-element.481), channel_id=1, source_target_pairs={{0,8},{1,9},{2,10},{3,11},{4,12},{5,13},{6,14},{7,15},{8,0},{9,1},... | collective-permute-start | bytes 786440 | tf_op jit(solution)/shard_map/ppermute | solution.py:44
  316.4 32.6 %collective-permute-start.45 = (bf16[128,1024]{1,0:T(8,128)(2,1)S(1)}, bf16[128,1024]{1,0:T(8,128)(2,1)S(1)}, u32[]{:S(2)}, u32[]{:S(2)}) collective-permute-start(bf16[128,1024]{1,0:T(8,128)(2,1)S(1)} %get-tuple-element.480), channel_id=1, source_target_pairs={{0,16},{1,17},{2,18},{3,19},{4,20},{5,21},{6,22},{7,23},{8,24},{9,... | collective-permute-start | bytes 786440 | tf_op jit(solution)/shard_map/ppermute | solution.py:44
  318.6 30.4 %collective-permute-start.46 = (bf16[128,1024]{1,0:T(8,128)(2,1)S(1)}, bf16[128,1024]{1,0:T(8,128)(2,1)S(1)}, u32[]{:S(2)}, u32[]{:S(2)}) collective-permute-start(bf16[128,1024]{1,0:T(8,128)(2,1)S(1)} %get-tuple-element.479), channel_id=1, source_target_pairs={{0,24},{1,25},{2,26},{3,27},{4,28},{5,29},{6,30},{7,31},{8,16},{9,... | collective-permute-start | bytes 786440 | tf_op jit(solution)/shard_map/ppermute | solution.py:44
  352.1 17.7 %collective-permute-start.48 = (bf16[4,32,5120]{2,1,0:T(8,128)(2,1)S(1)}, bf16[4,32,5120]{2,1,0:T(8,128)(2,1)S(1)}, u32[]{:S(2)}, u32[]{:S(2)}) collective-permute-start(bf16[4,32,5120]{2,1,0:T(8,128)(2,1)S(1)} %add_convert_fusion.3), channel_id=1, source_target_pairs={{0,2},{1,5},{2,0},{3,7},{4,6},{5,1},{6,4},{7,3},{8,10},{9,13},{10,... | collective-permute-start | bytes 3932168 | tf_op jit(solution)/shard_map/ppermute | solution.py:44
  372.3 21.7 %collective-permute-start.49 = (bf16[32,5120]{1,0:T(8,128)(2,1)S(1)}, bf16[32,5120]{1,0:T(8,128)(2,1)S(1)}, u32[]{:S(2)}, u32[]{:S(2)}) collective-permute-start(bf16[32,5120]{1,0:T(8,128)(2,1)S(1)} %get-tuple-element.478), channel_id=1, source_target_pairs={{0,8},{1,9},{2,10},{3,11},{4,12},{5,13},{6,14},{7,15},{8,0},{9,1},... | collective-permute-start | bytes 983048 | tf_op jit(solution)/shard_map/ppermute | solution.py:44
  372.4 25.7 %collective-permute-start.50 = (bf16[32,5120]{1,0:T(8,128)(2,1)S(1)}, bf16[32,5120]{1,0:T(8,128)(2,1)S(1)}, u32[]{:S(2)}, u32[]{:S(2)}) collective-permute-start(bf16[32,5120]{1,0:T(8,128)(2,1)S(1)} %get-tuple-element.477), channel_id=1, source_target_pairs={{0,16},{1,17},{2,18},{3,19},{4,20},{5,21},{6,22},{7,23},{8,24},{9,... | collective-permute-start | bytes 983048 | tf_op jit(solution)/shard_map/ppermute | solution.py:44
  374.6 23.4 %collective-permute-start.51 = (bf16[32,5120]{1,0:T(8,128)(2,1)S(1)}, bf16[32,5120]{1,0:T(8,128)(2,1)S(1)}, u32[]{:S(2)}, u32[]{:S(2)}) collective-permute-start(bf16[32,5120]{1,0:T(8,128)(2,1)S(1)} %get-tuple-element.476), channel_id=1, source_target_pairs={{0,24},{1,25},{2,26},{3,27},{4,28},{5,29},{6,30},{7,31},{8,16},{9,... | collective-permute-start | bytes 983048 | tf_op jit(solution)/shard_map/ppermute | solution.py:44
  398.1 15.1 %collective-permute-start.52 = (bf16[16,32,3072]{2,1,0:T(8,128)(2,1)}, bf16[16,32,3072]{2,1,0:T(8,128)(2,1)S(1)}, u32[]{:S(2)}, u32[]{:S(2)}) collective-permute-start(bf16[16,32,3072]{2,1,0:T(8,128)(2,1)} %get-tuple-element.432), channel_id=1, source_target_pairs={{0,1},{1,0},{2,3},{3,2},{4,5},{5,4},{6,7},{7,6},{8,9},{9,8},{10,11... | collective-permute-start | bytes 9437192 | tf_op jit(solution)/shard_map/ppermute | solution.py:44
  416.0 22.2 %collective-permute-start.54 = (bf16[8,32,3072]{2,1,0:T(8,128)(2,1)}, bf16[8,32,3072]{2,1,0:T(8,128)(2,1)}, u32[]{:S(2)}, u32[]{:S(2)}) collective-permute-start(bf16[8,32,3072]{2,1,0:T(8,128)(2,1)} %add_convert_fusion.2), channel_id=1, source_target_pairs={{0,4},{1,3},{2,6},{3,1},{4,0},{5,7},{6,2},{7,5},{8,12},{9,11},{10,... | collective-permute-start | bytes 4718600 | tf_op jit(solution)/shard_map/ppermute | solution.py:44
  421.3 16.8 %collective-permute-start.53 = (f32[13,1024]{1,0:T(8,128)S(1)}, f32[13,1024]{1,0:T(8,128)S(1)}, u32[]{:S(2)}, u32[]{:S(2)}) collective-permute-start(f32[13,1024]{1,0:T(8,128)S(1)} %concatenate.15), channel_id=1, source_target_pairs={{0,1},{1,0},{2,3},{3,2},{4,5},{5,4},{6,7},{7,6},{8,9},{9,8},{10,11... | collective-permute-start | bytes 159752 | tf_op jit(solution)/shard_map/ppermute | solution.py:44
  438.2 18.5 %collective-permute-start.56 = (bf16[16,64,1024]{2,1,0:T(8,128)(2,1)S(1)}, bf16[16,64,1024]{2,1,0:T(8,128)(2,1)S(1)}, u32[]{:S(2)}, u32[]{:S(2)}) collective-permute-start(bf16[16,64,1024]{2,1,0:T(8,128)(2,1)S(1)} %get-tuple-element.452), channel_id=1, source_target_pairs={{0,1},{1,0},{2,3},{3,2},{4,5},{5,4},{6,7},{7,6},{8,9},{9,8},{10,11... | collective-permute-start | bytes 6291464 | tf_op jit(solution)/shard_map/ppermute | solution.py:44
  440.2 16.4 %collective-permute-start.55 = (bf16[4,32,3072]{2,1,0:T(8,128)(2,1)S(1)}, bf16[4,32,3072]{2,1,0:T(8,128)(2,1)S(1)}, u32[]{:S(2)}, u32[]{:S(2)}) collective-permute-start(bf16[4,32,3072]{2,1,0:T(8,128)(2,1)S(1)} %add_convert_fusion.6), channel_id=1, source_target_pairs={{0,2},{1,5},{2,0},{3,7},{4,6},{5,1},{6,4},{7,3},{8,10},{9,13},{10,... | collective-permute-start | bytes 2359304 | tf_op jit(solution)/shard_map/ppermute | solution.py:44
  457.1 24.9 %collective-permute-start.61 = (bf16[8,64,1024]{2,1,0:T(8,128)(2,1)S(1)}, bf16[8,64,1024]{2,1,0:T(8,128)(2,1)S(1)}, u32[]{:S(2)}, u32[]{:S(2)}) collective-permute-start(bf16[8,64,1024]{2,1,0:T(8,128)(2,1)S(1)} %add_convert_fusion.4), channel_id=1, source_target_pairs={{0,4},{1,3},{2,6},{3,1},{4,0},{5,7},{6,2},{7,5},{8,12},{9,11},{10,... | collective-permute-start | bytes 3145736 | tf_op jit(solution)/shard_map/ppermute | solution.py:44
  459.7 16.8 %collective-permute-start.58 = (bf16[32,3072]{1,0:T(8,128)(2,1)S(1)}, bf16[32,3072]{1,0:T(8,128)(2,1)S(1)}, u32[]{:S(2)}, u32[]{:S(2)}) collective-permute-start(bf16[32,3072]{1,0:T(8,128)(2,1)S(1)} %get-tuple-element.484), channel_id=1, source_target_pairs={{0,8},{1,9},{2,10},{3,11},{4,12},{5,13},{6,14},{7,15},{8,0},{9,1},... | collective-permute-start | bytes 589832 | tf_op jit(solution)/shard_map/ppermute | solution.py:44
  464.8 17.2 %collective-permute-start.59 = (bf16[32,3072]{1,0:T(8,128)(2,1)S(1)}, bf16[32,3072]{1,0:T(8,128)(2,1)S(1)}, u32[]{:S(2)}, u32[]{:S(2)}) collective-permute-start(bf16[32,3072]{1,0:T(8,128)(2,1)S(1)} %get-tuple-element.483), channel_id=1, source_target_pairs={{0,16},{1,17},{2,18},{3,19},{4,20},{5,21},{6,22},{7,23},{8,24},{9,... | collective-permute-start | bytes 589832 | tf_op jit(solution)/shard_map/ppermute | solution.py:44
  465.2 16.8 %collective-permute-start.60 = (bf16[32,3072]{1,0:T(8,128)(2,1)S(1)}, bf16[32,3072]{1,0:T(8,128)(2,1)S(1)}, u32[]{:S(2)}, u32[]{:S(2)}) collective-permute-start(bf16[32,3072]{1,0:T(8,128)(2,1)S(1)} %get-tuple-element.482), channel_id=1, source_target_pairs={{0,24},{1,25},{2,26},{3,27},{4,28},{5,29},{6,30},{7,31},{8,16},{9,... | collective-permute-start | bytes 589832 | tf_op jit(solution)/shard_map/ppermute | solution.py:44
  482.3 14.4 %collective-permute-start.63 = (bf16[4,64,1024]{2,1,0:T(8,128)(2,1)S(1)}, bf16[4,64,1024]{2,1,0:T(8,128)(2,1)S(1)}, u32[]{:S(2)}, u32[]{:S(2)}) collective-permute-start(bf16[4,64,1024]{2,1,0:T(8,128)(2,1)S(1)} %add_convert_fusion.7), channel_id=1, source_target_pairs={{0,2},{1,5},{2,0},{3,7},{4,6},{5,1},{6,4},{7,3},{8,10},{9,13},{10,... | collective-permute-start | bytes 1572872 | tf_op jit(solution)/shard_map/ppermute | solution.py:44
  483.3 13.4 %collective-permute-start.64 = (f32[13,1024]{1,0:T(8,128)S(1)}, f32[13,1024]{1,0:T(8,128)S(1)}, u32[]{:S(2)}, u32[]{:S(2)}) collective-permute-start(f32[13,1024]{1,0:T(8,128)S(1)} %add.310), channel_id=1, source_target_pairs={{0,8},{1,9},{2,10},{3,11},{4,12},{5,13},{6,14},{7,15},{8,0},{9,1},... | collective-permute-start | bytes 159752 | tf_op jit(solution)/shard_map/ppermute | solution.py:44
  497.6 13.9 %collective-permute-start.67 = (bf16[64,1024]{1,0:T(8,128)(2,1)S(1)}, bf16[64,1024]{1,0:T(8,128)(2,1)S(1)}, u32[]{:S(2)}, u32[]{:S(2)}) collective-permute-start(bf16[64,1024]{1,0:T(8,128)(2,1)S(1)} %get-tuple-element.486), channel_id=1, source_target_pairs={{0,24},{1,25},{2,26},{3,27},{4,28},{5,29},{6,30},{7,31},{8,16},{9,... | collective-permute-start | bytes 393224 | tf_op jit(solution)/shard_map/ppermute | solution.py:44
  (125 other events, 1531.5 us)
